TPU v7x, 32 devices: a whole 2x2x4 slice. The times are simulated.
32 devices in a mesh: tile: 8 (over y, x, core), grp: 4 (over z).
Axes of the slice: x: 2, y: 2, z: 4, core: 2. Of those that a mesh axis runs over, the one named last changes fastest.
Arguments:
- forcing_vector: float32 [70, 64, 512], P(None, 'tile', 'grp'), may hold values from -8 to 8
- shift_weights: float32 [70, 64, 512], P(None, 'tile', 'grp'), may hold values from 0.0001 to 0.0004
- layer_link_factor: float32 [69], replicated, may hold values from 0.5 to 8
- previous_kelvin_field: float32 [70, 8, 4096], P(None, None, ('tile', 'grp')), may hold values from 0.8 to 1.2
- longwave_opacity: float32 [70], replicated, may hold values from 0.02 to 0.5
- shortwave_opacity: float32 [70], replicated, may hold values from 0.01 to 0.05
Outputs:
- solution_field: float32 [70, 64, 512], P(None, 'tile', 'grp')
- radiation_state: float32 [70, 8, 4096], P(None, None, ('tile', 'grp'))
All inputs are finite; a program needn't handle non-finite values.
Results may differ from a plain program's by a relative error of at most 0.0003.
Values sent between devices are 32-bit elements; how exact they have to be, the bound alone decides.
No kernel may reach another device: no remote copies, remote signals or barrier semaphores. Data moves between devices by JAX's collectives and lax.ppermute only.
A program may use at most 64 MiB of HBM per device.

v0:
```python
import math

import jax
import jax.numpy as jnp
from jax import lax
from jax.sharding import PartitionSpec as P

LAYER_TOTAL = 70
SHARD_POINTS = 8
CY = 128
ITERS = 2


def with_halo(value, sides, width):
    for axis, dim in sides:
        devices, length = (lax.axis_size(axis), value.shape[dim])
        up = [(i, (i + 1) % devices) for i in range(devices)]
        down = [(j, i) for i, j in up]
        last = lax.slice_in_dim(value, length - width, length, axis=dim)
        first = lax.slice_in_dim(value, 0, width, axis=dim)
        before = lax.ppermute(last, axis, up)
        after = lax.ppermute(first, axis, down)
        value = jnp.concatenate([before, value, after], axis=dim)
    return value


def column_inverse(layer_link_factor):
    size = layer_link_factor.shape[0] + 1
    zero_one = jnp.zeros((1,), jnp.float32)
    upper = jnp.concatenate([layer_link_factor, zero_one])
    lower = jnp.concatenate([zero_one, layer_link_factor])
    matrix = (
        jnp.diag(4.0 + upper + lower)
        - jnp.diag(layer_link_factor, 1)
        - jnp.diag(layer_link_factor, -1)
    )
    factor = jnp.linalg.cholesky(matrix)
    return jax.scipy.linalg.cho_solve((factor, True), jnp.eye(size, dtype=jnp.float32))


def radiation_tables(longwave_opacity, shortwave_opacity):
    levels = longwave_opacity.shape[0]
    transmitted = jnp.exp(-longwave_opacity)
    zero_one = jnp.zeros((1,), jnp.float32)
    interfaces = jnp.concatenate([zero_one, jnp.cumsum(longwave_opacity)])
    interface_index = jnp.arange(levels + 1)[:, None]
    layer_index = jnp.arange(levels)[None, :]
    below_mask = layer_index < interface_index
    gap_down = jnp.where(below_mask, interfaces[:, None] - interfaces[None, 1:], 0.0)
    downward = jnp.where(below_mask, jnp.exp(-gap_down), 0.0) * (1.0 - transmitted)[None, :]
    above_mask = layer_index >= interface_index
    gap_up = jnp.where(above_mask, interfaces[None, :-1] - interfaces[:, None], 0.0)
    upward = jnp.where(above_mask, jnp.exp(-gap_up), 0.0) * (1.0 - transmitted)[None, :]
    surface = jnp.exp(-(interfaces[-1] - interfaces))
    upward = upward.at[:, levels - 1].add(surface)
    matrix = downward[:-1] - downward[1:] + upward[1:] - upward[:-1]
    solar_edges = jnp.concatenate([zero_one, jnp.cumsum(shortwave_opacity)])
    absorbed = 10.0 * (jnp.exp(-solar_edges[:-1]) - jnp.exp(-solar_edges[1:]))
    return (matrix, absorbed)


def sun_cosine(global_row, total_rows):
    latitude = ((global_row.astype(jnp.float32) + 0.5) / total_rows - 0.5) * (math.pi / 2)
    return jnp.cos(latitude - 0.4)


def vertical(source, layer_link_factor):
    fluxes = layer_link_factor[:, None, None] * (source[:-1] - source[1:])
    zeros_level = jnp.zeros_like(source[:1])
    return jnp.concatenate([fluxes, zeros_level], axis=0) - jnp.concatenate(
        [zeros_level, fluxes], axis=0
    )


def operate(source, shift_weights, layer_link_factor, group_index, group_count):
    padded = with_halo(source, (("tile", 1), ("grp", 2)), 1)
    lower_rim = jnp.where(group_index > 0, padded[:, 1:-1, 0:1], source[:, :, 0:1])
    upper_rim = jnp.where(group_index < group_count - 1, padded[:, 1:-1, -1:], source[:, :, -1:])
    across = jnp.concatenate([lower_rim, source[:, :, :-1]], axis=2) + jnp.concatenate(
        [source[:, :, 1:], upper_rim], axis=2
    )
    beside = padded[:, 2:, 1:-1] + padded[:, :-2, 1:-1] + across
    return shift_weights * source + 4.0 * source - beside + vertical(source, layer_link_factor)


def coarse_matrix(block_mass, tile_count, group_count):
    block_count = tile_count * group_count
    ordering = jnp.arange(block_count)
    tile_of = ordering // group_count
    group_of = ordering % group_count
    same_group = group_of[:, None] == group_of[None, :]
    tile_gap = (tile_of[:, None] - tile_of[None, :]) % tile_count
    x_near = same_group & ((tile_gap == 1) | (tile_gap == tile_count - 1))
    same_tile = tile_of[:, None] == tile_of[None, :]
    y_near = (same_tile & (jnp.abs(group_of[:, None] - group_of[None, :]) == 1)).astype(jnp.float32)
    y_count = jnp.sum(y_near, axis=1)
    diagonal = block_mass + 2.0 * LAYER_TOTAL * CY + LAYER_TOTAL * SHARD_POINTS * y_count
    return (
        jnp.diag(diagonal)
        - LAYER_TOTAL * CY * x_near.astype(jnp.float32)
        - LAYER_TOTAL * SHARD_POINTS * y_near
    )


def element(vector, position):
    return lax.dynamic_index_in_dim(vector, position, 0, keepdims=False)


def orthogonalize(direction, operator_image, weights, directions, images):
    direction = direction - weights[0] * directions[0]
    operator_image = operator_image - weights[0] * images[0]
    return (direction, operator_image)


def per_device(
    forcing_vector,
    shift_weights,
    layer_link_factor,
    previous_kelvin_field,
    longwave_opacity,
    shortwave_opacity,
):
    highest = lax.Precision.HIGHEST
    tile_count = lax.axis_size("tile")
    group_count = lax.axis_size("grp")
    tile_index = lax.axis_index("tile")
    group_index = lax.axis_index("grp")
    matrix, absorbed = radiation_tables(longwave_opacity, shortwave_opacity)
    share_rows = CY // tile_count
    position = jnp.arange(CY)
    global_row = group_index * CY + tile_index * share_rows + position % share_rows
    cosine = sun_cosine(global_row, CY * group_count)
    second_power_entry = previous_kelvin_field * previous_kelvin_field
    emission = second_power_entry * second_power_entry
    column_heating = jnp.dot(matrix, emission.reshape(LAYER_TOTAL, -1), precision=highest).reshape(
        emission.shape
    )
    column_heating = column_heating + absorbed[:, None, None] * cosine[None, None, :]
    column_heating = column_heating - jnp.mean(column_heating, axis=0, keepdims=True)
    heating = lax.all_to_all(column_heating, "tile", split_axis=2, concat_axis=2, tiled=True)
    forcing = forcing_vector + heating
    inverse = column_inverse(layer_link_factor)
    own_index = tile_index * group_count + group_index
    block_mass = jnp.sum(shift_weights).reshape(1)
    factor = None
    solution = jnp.zeros_like(forcing)
    residual = forcing
    directions = []
    images = []
    image_norms = []
    gram_matrix = None
    residual_products = None
    for number in range(ITERS):
        smooth = jnp.dot(inverse, residual.reshape(LAYER_TOTAL, -1), precision=highest).reshape(
            residual.shape
        )
        smooth_image = operate(smooth, shift_weights, layer_link_factor, group_index, group_count)
        remainder = residual - smooth_image
        mass_all, sums_all = (
            lax.all_gather(block_mass, ("tile", "grp"), axis=0, tiled=True),
            lax.all_gather(jnp.sum(remainder).reshape(1), ("tile", "grp"), axis=0, tiled=True),
        )
        if factor is None:
            factor = jnp.linalg.cholesky(coarse_matrix(mass_all, tile_count, group_count))
        coarse = jax.scipy.linalg.cho_solve((factor, True), sums_all)
        own_value = element(coarse, own_index)
        direction = smooth + own_value
        operator_image = operate(
            direction, shift_weights, layer_link_factor, group_index, group_count
        )
        partial_value = jnp.stack(
            [jnp.sum(operator_image * earlier) for earlier in images]
            + [jnp.sum(residual * operator_image), jnp.sum(operator_image * operator_image)]
        )
        totals = lax.psum(partial_value, ("tile", "grp"))
        crossing = totals[:number]
        projection = totals[number]
        image_norm = totals[number + 1]
        if number > 0:
            weights = crossing / jnp.diagonal(gram_matrix)
            new_row = crossing - jnp.dot(gram_matrix, weights, precision=highest)
            image_norm = (
                image_norm
                - 2.0 * jnp.sum(weights * crossing)
                + jnp.dot(
                    weights, jnp.dot(gram_matrix, weights, precision=highest), precision=highest
                )
            )
            projection = projection - jnp.sum(weights * residual_products)
            direction, operator_image = orthogonalize(
                direction, operator_image, weights, directions, images
            )
        step_size = projection / image_norm
        if number == 0:
            gram_matrix = image_norm.reshape(1, 1)
            residual_products = (projection - step_size * image_norm).reshape(1)
        else:
            upper_block = jnp.concatenate([gram_matrix, new_row[:, None]], axis=1)
            lower_block = jnp.concatenate([new_row, image_norm.reshape(1)])[None, :]
            gram_matrix = jnp.concatenate([upper_block, lower_block], axis=0)
            residual_products = jnp.concatenate(
                [
                    residual_products - step_size * new_row,
                    (projection - step_size * image_norm).reshape(1),
                ]
            )
        solution = solution + step_size * direction
        residual = residual - step_size * operator_image
        directions.append(direction)
        images.append(operator_image)
        image_norms.append(image_norm)
    radiation_state = lax.all_to_all(solution, "tile", split_axis=2, concat_axis=2, tiled=True)
    return (solution, radiation_state)


def solution(mesh):
    return jax.shard_map(
        per_device,
        mesh=mesh,
        in_specs=(
            P(None, "tile", "grp"),
            P(None, "tile", "grp"),
            P(),
            P(None, None, ("tile", "grp")),
            P(),
            P(),
        ),
        out_specs=(P(None, "tile", "grp"), P(None, None, ("tile", "grp"))),
        check_vma=False,
    )
```

profile of v0, /device:TPU:0, one launch (start us, length us, event | category | flops | bytes accessed | tf_op | source)
XLA Modules:
  0.0 284.5 jit_solution(4636732581692526821)
XLA Ops:
  0.7 0.6 copy-done.15
  2.2 0.8 copy.60
  3.6 0.7 slice_add_fusion.2
  4.9 1.0 copy.61
  5.9 5.2 %all-to-all-start = ((f32[70,8,128]{0,1,2:T(8,128)}), f32[70,8,128]{0,1,2:T(8,128)S(1)}, u32[]{:S(2)}, u32[]{:S(2)}) async-start(f32[70,8,128]{0,1,2:T(8,128)} %copy.61), calls=%async_computation | async-start | bytes 1048576 | tf_op jit(solution)/shard_map/all_to_all | solution.py:140
  11.1 0.6 copy-done.9
  12.0 6.4 %cholesky.33 = f32[70,70]{1,0:T(8,128)S(1)} custom-call(f32[70,70]{1,0:T(8,128)S(1)} %add_multiply_fusion), custom_call_target="Cholesky" | custom-call | tf_op jit(solution)/shard_map/jit(cholesky)/cholesky | solution.py:37
  18.4 0.6 compare_reduce_fusion.1
  19.1 0.7 fusion.23
  19.7 5.4 %custom-call.18 = f32[1,70,70]{1,2,0:T(8,128)S(1)} custom-call(f32[1,70,70]{2,1,0:T(8,128)S(1)} %fusion.23), custom_call_target="InvertDiagBlocksLowerTriangular" | custom-call | tf_op jit(solution)/shard_map/jit(_cho_solve)/triangular_solve | solution.py:38
  25.4 0.7 convert_reduce_fusion
  26.5 0.7 copy-done.6
  28.0 2.7 collective-permute-start
  30.9 1.5 collective-permute-done
  32.4 2.6 collective-permute-done.1
  35.8 1.6 collective-permute-start.2
  37.4 2.2 collective-permute-start.3
  39.8 1.2 collective-permute-done.3
  41.6 0.8 copy-done
  42.4 1.0 fusion.20
  43.4 0.8 dynamic-update-slice.10
  44.2 0.8 dynamic-update-slice.9
  45.0 39.4 %all-reduce.13 = (f32[32]{0:T(128)S(1)}, f32[32]{0:T(128)S(1)}) all-reduce(f32[32]{0:T(128)S(1)} %dynamic-update-slice.9, f32[32]{0:T(128)S(1)} %dynamic-update-slice.10), channel_id=1, replica_groups=mesh['tile'=8,'grp'=4] {'tile','grp'}, use_global_device_ids=true, to_apply=%add.10 | all-reduce | flops 64 | bytes 512
  84.4 0.7 copy-done.16
  85.1 0.7 copy-done.12
  85.9 2.9 %cholesky.70 = f32[32,32]{1,0:T(8,128)S(1)} custom-call(f32[32,32]{1,0:T(8,128)S(1)} %add_multiply_fusion.1), custom_call_target="Cholesky" | custom-call | tf_op jit(solution)/shard_map/jit(cholesky)/cholesky | solution.py:164
  88.8 0.6 compare_reduce_fusion
  89.4 0.7 fusion.31
  90.1 2.4 custom-call.20
  94.1 2.6 collective-permute-start.4
  96.9 1.5 collective-permute-done.5
  99.1 2.3 collective-permute-start.7
  101.6 5.3 %collective-permute-done.6 = f32[70,10,1]{0,2,1:T(1,128)S(1)} collective-permute-done((f32[70,10,1]{0,2,1:T(1,128)S(1)}, f32[70,10,1]{0,2,1:T(1,128)S(1)}, u32[]{:S(2)}, u32[]{:S(2)}) %collective-permute-start.6) | collective-permute-done | bytes 2832 | tf_op jit(solution)/shard_map/ppermute | solution.py:21
  107.4 0.9 multiply_reduce_fusion.4
  108.4 1.4 pad_maximum_fusion.14
  109.7 37.2 %psum.14 = f32[2]{0:T(128)S(1)} all-reduce(f32[2]{0:T(128)S(1)} %pad_maximum_fusion.14), channel_id=1, replica_groups=mesh['tile'=8,'grp'=4] {'tile','grp'}, use_global_device_ids=true, to_apply=%region_12.14 | all-reduce | flops 2 | bytes 16 | tf_op jit(solution)/shard_map/psum | solution.py:175
  147.0 0.7 fusion.67
  149.8 1.0 collective-permute-start.8
  150.9 0.8 copy.90
  151.6 0.8 collective-permute-done.8
  152.4 3.0 %collective-permute-done.9 = f32[70,1,128]{2,1,0:T(1,128)S(1)} collective-permute-done((f32[70,1,128]{2,1,0:T(1,128)S(1)}, f32[70,1,128]{2,1,0:T(1,128)S(1)}, u32[]{:S(2)}, u32[]{:S(2)}) %collective-permute-start.9) | collective-permute-done | bytes 35872 | tf_op jit(solution)/shard_map/ppermute | solution.py:21
  156.8 2.9 %collective-permute-start.10 = (f32[70,10,1]{0,2,1:T(1,128)S(1)}, f32[70,10,1]{0,2,1:T(1,128)S(1)}, u32[]{:S(2)}, u32[]{:S(2)}) collective-permute-start(f32[70,10,1]{0,2,1:T(1,128)S(1)} %copy.71), channel_id=1, source_target_pairs={{0,1},{1,2},{2,3},{3,0},{4,5},{5,6},{6,7},{7,4},{8,9},{9,10},{10,1... | collective-permute-start | bytes 8408 | tf_op jit(solution)/shard_map/ppermute | solution.py:21
  159.7 1.0 collective-permute-start.11
  160.7 0.8 slice_multiply_fusion
  161.5 1.8 collective-permute-done.11
  163.9 0.8 copy-done.3
  164.7 0.9 fusion.10
  165.7 0.8 dynamic-update-slice.11
  167.1 38.6 %all-reduce.12 = f32[32]{0:T(128)S(1)} all-reduce(f32[32]{0:T(128)S(1)} %dynamic-update-slice.11), channel_id=1, replica_groups=mesh['tile'=8,'grp'=4] {'tile','grp'}, use_global_device_ids=true, to_apply=%add.12 | all-reduce | flops 32 | bytes 256
  206.6 0.7 broadcast_add_fusion
  207.3 1.0 collective-permute-start.12
  208.4 1.5 collective-permute-done.12
  209.9 2.8 collective-permute-done.13
  213.5 1.9 collective-permute-start.14
  215.3 2.0 collective-permute-start.15
  217.3 0.8 fusion.21
  218.2 0.8 collective-permute-done.15
  219.5 0.8 copy-done.4
  220.3 1.0 multiply_reduce_fusion.2
  221.4 2.0 pad_maximum_fusion.15
  224.0 39.1 %psum.15 = f32[3]{0:T(128)S(1)} all-reduce(f32[3]{0:T(128)S(1)} %pad_maximum_fusion.15), channel_id=1, replica_groups=mesh['tile'=8,'grp'=4] {'tile','grp'}, use_global_device_ids=true, to_apply=%region_17.19 | all-reduce | flops 3 | bytes 24 | tf_op jit(solution)/shard_map/psum | solution.py:175
  267.8 1.3 multiply_add_fusion
  269.8 13.8 %all_to_all.10 = f32[70,8,128]{0,1,2:T(8,128)S(1)} all-to-all(f32[70,8,128]{0,1,2:T(8,128)S(1)} %copy.79), channel_id=1, replica_groups=mesh['tile'=8,'grp'=4] {'tile'}, dimensions={2} | all-to-all | bytes 573440 | tf_op jit(solution)/shard_map/all_to_all | solution.py:212
  283.6 0.9 copy.80
  (140 shorter events, 15.1 us)
Async XLA Ops:
  0.6 0.7 copy-start.15
  0.6 2.7 copy-start.5
  5.9 20.3 %all-to-all-start = ((f32[70,8,128]{0,1,2:T(8,128)}), f32[70,8,128]{0,1,2:T(8,128)S(1)}, u32[]{:S(2)}, u32[]{:S(2)}) async-start(f32[70,8,128]{0,1,2:T(8,128)} %copy.61), calls=%async_computation | async-start | bytes 1048576 | tf_op jit(solution)/shard_map/all_to_all | solution.py:140
  11.1 0.7 copy-start.9
  11.8 13.6 %copy-start.11 = (s32[32]{0:T(128)}, s32[32]{0:T(128)S(1)}, u32[]{:S(2)}) copy-start(s32[32]{0:T(128)S(1)} %get-tuple-element.79) | copy-start | bytes 388
  11.8 13.6 %copy-start.13 = (s32[32]{0:T(128)}, s32[32]{0:T(128)S(1)}, u32[]{:S(2)}) copy-start(s32[32]{0:T(128)S(1)} %get-tuple-element.80) | copy-start | bytes 388
  26.3 1.0 copy-start.6
  28.0 4.4 %collective-permute-start = (f32[70,1,128]{2,1,0:T(1,128)S(1)}, f32[70,1,128]{2,1,0:T(1,128)S(1)}, u32[]{:S(2)}, u32[]{:S(2)}) collective-permute-start(f32[70,1,128]{2,1,0:T(1,128)S(1)} %get-tuple-element.47), channel_id=1, source_target_pairs={{4,0},{8,4},{12,8},{16,12},{20,16},{24,20},{28,24},{0,28},{5,1},{9... | collective-permute-start | bytes 107528 | tf_op jit(solution)/shard_map/ppermute | solution.py:22
  30.7 4.3 %collective-permute-start.1 = (f32[70,1,128]{2,1,0:T(1,128)S(1)}, f32[70,1,128]{2,1,0:T(1,128)S(1)}, u32[]{:S(2)}, u32[]{:S(2)}) collective-permute-start(f32[70,1,128]{2,1,0:T(1,128)S(1)} %get-tuple-element.48), channel_id=1, source_target_pairs={{0,4},{4,8},{8,12},{12,16},{16,20},{20,24},{24,28},{28,0},{1,5},{5... | collective-permute-start | bytes 107528 | tf_op jit(solution)/shard_map/ppermute | solution.py:21
  35.8 5.4 %collective-permute-start.2 = (f32[70,10,1]{0,2,1:T(1,128)S(1)}, f32[70,10,1]{0,2,1:T(1,128)S(1)}, u32[]{:S(2)}, u32[]{:S(2)}) collective-permute-start(f32[70,10,1]{0,2,1:T(1,128)S(1)} %copy.63), channel_id=1, source_target_pairs={{0,1},{1,2},{2,3},{3,0},{4,5},{5,6},{6,7},{7,4},{8,9},{9,10},{10,1... | collective-permute-start | bytes 8408 | tf_op jit(solution)/shard_map/ppermute | solution.py:21
  37.4 3.6 %collective-permute-start.3 = (f32[70,10,1]{0,2,1:T(1,128)S(1)}, f32[70,10,1]{0,2,1:T(1,128)S(1)}, u32[]{:S(2)}, u32[]{:S(2)}) collective-permute-start(f32[70,10,1]{0,2,1:T(1,128)S(1)} %copy.65), channel_id=1, source_target_pairs={{1,0},{2,1},{3,2},{0,3},{5,4},{6,5},{7,6},{4,7},{9,8},{10,9},{11,1... | collective-permute-start | bytes 8408 | tf_op jit(solution)/shard_map/ppermute | solution.py:22
  41.4 1.0 copy-start
  84.4 0.7 copy-start.16
  85.1 0.7 copy-start.12
  85.1 0.7 copy-start.14
  94.0 4.3 %collective-permute-start.5 = (f32[70,1,128]{2,1,0:T(1,128)S(1)}, f32[70,1,128]{2,1,0:T(1,128)S(1)}, u32[]{:S(2)}, u32[]{:S(2)}) collective-permute-start(f32[70,1,128]{2,1,0:T(1,128)S(1)} %get-tuple-element.61), channel_id=1, source_target_pairs={{0,4},{4,8},{8,12},{12,16},{16,20},{20,24},{24,28},{28,0},{1,5},{5... | collective-permute-start | bytes 107528 | tf_op jit(solution)/shard_map/ppermute | solution.py:21
  94.1 4.3 %collective-permute-start.4 = (f32[70,1,128]{2,1,0:T(1,128)S(1)}, f32[70,1,128]{2,1,0:T(1,128)S(1)}, u32[]{:S(2)}, u32[]{:S(2)}) collective-permute-start(f32[70,1,128]{2,1,0:T(1,128)S(1)} %get-tuple-element.62), channel_id=1, source_target_pairs={{4,0},{8,4},{12,8},{16,12},{20,16},{24,20},{28,24},{0,28},{5,1},{9... | collective-permute-start | bytes 107528 | tf_op jit(solution)/shard_map/ppermute | solution.py:22
  98.9 2.5 copy-start.10
  99.1 7.9 %collective-permute-start.7 = (f32[70,10,1]{0,2,1:T(1,128)S(1)}, f32[70,10,1]{0,2,1:T(1,128)S(1)}, u32[]{:S(2)}, u32[]{:S(2)}) collective-permute-start(f32[70,10,1]{0,2,1:T(1,128)S(1)} %copy.69), channel_id=1, source_target_pairs={{1,0},{2,1},{3,2},{0,3},{5,4},{6,5},{7,6},{4,7},{9,8},{10,9},{11,1... | collective-permute-start | bytes 8408 | tf_op jit(solution)/shard_map/ppermute | solution.py:22
  101.4 5.4 %collective-permute-start.6 = (f32[70,10,1]{0,2,1:T(1,128)S(1)}, f32[70,10,1]{0,2,1:T(1,128)S(1)}, u32[]{:S(2)}, u32[]{:S(2)}) collective-permute-start(f32[70,10,1]{0,2,1:T(1,128)S(1)} %copy.67), channel_id=1, source_target_pairs={{0,1},{1,2},{2,3},{3,0},{4,5},{5,6},{6,7},{7,4},{8,9},{9,10},{10,1... | collective-permute-start | bytes 8408 | tf_op jit(solution)/shard_map/ppermute | solution.py:21
  149.8 2.6 collective-permute-start.8
  150.8 4.6 %collective-permute-start.9 = (f32[70,1,128]{2,1,0:T(1,128)S(1)}, f32[70,1,128]{2,1,0:T(1,128)S(1)}, u32[]{:S(2)}, u32[]{:S(2)}) collective-permute-start(f32[70,1,128]{2,1,0:T(1,128)S(1)} %get-tuple-element.44), channel_id=1, source_target_pairs={{0,4},{4,8},{8,12},{12,16},{16,20},{20,24},{24,28},{28,0},{1,5},{5... | collective-permute-start | bytes 107528 | tf_op jit(solution)/shard_map/ppermute | solution.py:21
  155.4 0.6 copy-start.7
  156.6 4.1 %copy-start.2 = (f32[9,8,8,128]{3,2,1,0:T(8,128)S(1)}, f32[9,8,8,128]{3,2,1,0:T(8,128)}, u32[]{:S(2)}) copy-start(f32[9,8,8,128]{3,2,1,0:T(8,128)} %copy.90) | copy-start | bytes 884740
  156.8 6.7 %collective-permute-start.10 = (f32[70,10,1]{0,2,1:T(1,128)S(1)}, f32[70,10,1]{0,2,1:T(1,128)S(1)}, u32[]{:S(2)}, u32[]{:S(2)}) collective-permute-start(f32[70,10,1]{0,2,1:T(1,128)S(1)} %copy.71), channel_id=1, source_target_pairs={{0,1},{1,2},{2,3},{3,0},{4,5},{5,6},{6,7},{7,4},{8,9},{9,10},{10,1... | collective-permute-start | bytes 8408 | tf_op jit(solution)/shard_map/ppermute | solution.py:21
  159.7 3.6 %collective-permute-start.11 = (f32[70,10,1]{0,2,1:T(1,128)S(1)}, f32[70,10,1]{0,2,1:T(1,128)S(1)}, u32[]{:S(2)}, u32[]{:S(2)}) collective-permute-start(f32[70,10,1]{0,2,1:T(1,128)S(1)} %copy.73), channel_id=1, source_target_pairs={{1,0},{2,1},{3,2},{0,3},{5,4},{6,5},{7,6},{4,7},{9,8},{10,9},{11,1... | collective-permute-start | bytes 8408 | tf_op jit(solution)/shard_map/ppermute | solution.py:22
  163.8 1.0 copy-start.3
  163.8 1.0 copy-start.8
  207.3 2.6 collective-permute-start.12
  208.3 4.4 %collective-permute-start.13 = (f32[70,1,128]{2,1,0:T(1,128)S(1)}, f32[70,1,128]{2,1,0:T(1,128)S(1)}, u32[]{:S(2)}, u32[]{:S(2)}) collective-permute-start(f32[70,1,128]{2,1,0:T(1,128)S(1)} %get-tuple-element.54), channel_id=1, source_target_pairs={{0,4},{4,8},{8,12},{12,16},{16,20},{20,24},{24,28},{28,0},{1,5},{5... | collective-permute-start | bytes 107528 | tf_op jit(solution)/shard_map/ppermute | solution.py:21
  213.5 5.7 %collective-permute-start.14 = (f32[70,10,1]{0,2,1:T(1,128)S(1)}, f32[70,10,1]{0,2,1:T(1,128)S(1)}, u32[]{:S(2)}, u32[]{:S(2)}) collective-permute-start(f32[70,10,1]{0,2,1:T(1,128)S(1)} %copy.75), channel_id=1, source_target_pairs={{0,1},{1,2},{2,3},{3,0},{4,5},{5,6},{6,7},{7,4},{8,9},{9,10},{10,1... | collective-permute-start | bytes 8408 | tf_op jit(solution)/shard_map/ppermute | solution.py:21
  215.3 3.6 %collective-permute-start.15 = (f32[70,10,1]{0,2,1:T(1,128)S(1)}, f32[70,10,1]{0,2,1:T(1,128)S(1)}, u32[]{:S(2)}, u32[]{:S(2)}) collective-permute-start(f32[70,10,1]{0,2,1:T(1,128)S(1)} %copy.77), channel_id=1, source_target_pairs={{1,0},{2,1},{3,2},{0,3},{5,4},{6,5},{7,6},{4,7},{9,8},{10,9},{11,1... | collective-permute-start | bytes 8408 | tf_op jit(solution)/shard_map/ppermute | solution.py:22
  219.4 1.0 copy-start.4
  269.1 0.7 copy-start.1
where the time goes:
time: 286 us; the launch traced here: 285 us
  blocking collectives  168 us (59%)
  other arithmetic  35.2 us (12%)
  starting transfers between devices  26.3 us (9%)
  waiting for transfers between devices  22.8 us (8%)
  local copies, waits for them, and re-layouts  21.6 us (8%)
  between operations  8.08 us (3%)
    unnamed x2, blocking collectives  78 us
    psum x2, blocking collectives, per_device(): totals = lax.psum(partial_value, ('tile', 'grp'))  76.4 us
    ppermute x8, waiting for transfers between devices, with_halo(): before = lax.ppermute(last, axis, up)  15.2 us
    ppermute x8, starting transfers between devices, with_halo(): after = lax.ppermute(first, axis, down)  14.7 us
    all_to_all x1, blocking collectives, per_device(): lax.all_to_all(solution, 'tile', split_axis=2, concat_axis=2, tiled=True)  13.8 us
    unnamed x49, local copies, waits for them, and re-layouts  11.1 us
    ppermute x8, waiting for transfers between devices, with_halo(): after = lax.ppermute(first, axis, down)  7.61 us
    another operation x3, other arithmetic, column_inverse(): factor = jnp.linalg.cholesky(matrix)  7.07 us
  transfers between devices with their start and end apart: 17, of which 11 were waited for; matrix products, arithmetic and copies ran while one was open for 6% of the time, Pallas kernels for 0%

commit v1 on v0

v1 whole, which is shorter than its diff:
```python
import math

import jax
import jax.numpy as jnp
from jax import lax
from jax.experimental import pallas as pl
from jax.experimental.pallas import tpu as pltpu
from jax.sharding import PartitionSpec as P

F32 = jnp.float32
HIGHEST = lax.Precision.HIGHEST
VMEM = pl.BlockSpec(memory_space=pltpu.VMEM)


def iota(shape, dim):
    return lax.broadcasted_iota(jnp.int32, shape, dim)


def turn(value, shift, axis=1):
    shift = shift % value.shape[axis]
    return pltpu.roll(value, shift, axis) if shift else value


def total(value):
    return jnp.sum(value, axis=(0, 1), keepdims=True)


def call(kernel, outs, *args):
    return pl.pallas_call(
        kernel,
        out_shape=[jax.ShapeDtypeStruct(shape, F32) for shape in outs],
        in_specs=[VMEM] * len(args),
        out_specs=[VMEM] * len(outs),
        compiler_params=pltpu.CompilerParams(vmem_limit_bytes=32 * 1024 * 1024),
    )(*args)


def load_columns(ref, points, levels, padded):
    tiles = []
    for i in range(points):
        tile = ref[pl.ds(i, levels, stride=points), :]
        if padded > levels:
            tile = jnp.concatenate([tile, jnp.zeros((padded - levels, tile.shape[1]), F32)], axis=0)
        tiles.append(tile)
    return tiles


def store_columns(ref, tiles, levels):
    for i, tile in enumerate(tiles):
        ref[pl.ds(i, levels, stride=len(tiles)), :] = tile[:levels]


def swap_groups(tiles):
    count, lanes = len(tiles), tiles[0].shape[1]
    width = lanes // count
    group = iota(tiles[0].shape, 1) // width
    tiles = list(tiles)
    step = count // 2
    while step:
        low = (group & step) == 0
        for j in range(count):
            if j & step == 0:
                a, b = tiles[j], tiles[j + step]
                tiles[j] = jnp.where(low, a, turn(b, step * width))
                tiles[j + step] = jnp.where(low, turn(a, -step * width), b)
        step //= 2
    return tiles


def pack_kernel(levels, x_ref, out_ref):
    points, padded, _ = out_ref.shape
    for s, tile in enumerate(swap_groups(load_columns(x_ref, points, levels, padded))):
        out_ref[s] = tile


def unpack_kernel(levels, x_ref, out_ref):
    points = x_ref.shape[0]
    store_columns(out_ref, swap_groups([x_ref[s] for s in range(points)]), levels)


def tables_kernel(levels, rows_ref, inverse_ref, matrix_ref, absorbed_ref):
    shape = inverse_ref.shape
    sub, lane = iota(shape, 0), iota(shape, 1)

    def column(row, mask):
        return jnp.broadcast_to(jnp.sum(jnp.where(mask, row, 0.0), axis=1, keepdims=True), shape)

    link, thermal, solar = rows_ref[0:1, :], rows_ref[1:2, :], rows_ref[2:3, :]
    lower = column(link, lane == sub - 1)
    upper = column(link, lane == sub)
    diagonal = 4.0 + lower + upper
    lower, upper = -lower, -upper
    result = jnp.where(lane == sub, 1.0, 0.0).astype(F32)
    step = 1
    while step < levels:
        inverse = 1.0 / diagonal
        a = -lower * turn(inverse, step, 0)
        c = -upper * turn(inverse, -step, 0)
        diagonal = diagonal + a * turn(upper, step, 0) + c * turn(lower, -step, 0)
        result = result + a * turn(result, step, 0) + c * turn(result, -step, 0)
        lower, upper = a * turn(lower, step, 0), c * turn(upper, -step, 0)
        step *= 2
    valid = (sub < levels) & (lane < levels)
    inverse_ref[...] = jnp.where(valid, result / diagonal, 0.0)

    own = column(thermal, lane == sub)
    top_column = column(thermal, lane < sub)
    bottom_column = column(thermal, lane <= sub)
    top_row = jnp.sum(jnp.where(sub < lane, own, 0.0), axis=0, keepdims=True)
    bottom_row = jnp.sum(jnp.where(sub <= lane, own, 0.0), axis=0, keepdims=True)
    whole = jnp.sum(thermal, axis=1, keepdims=True)
    emitted = 1.0 - jnp.exp(-thermal)

    def decay(mask, gap):
        return jnp.where(mask, jnp.exp(-jnp.where(mask, gap, 0.0)), 0.0)

    below, above = lane < sub, lane > sub
    matrix = decay(below, top_column - bottom_row) - decay(below, bottom_column - bottom_row)
    matrix = matrix + decay(above, top_row - bottom_column) - decay(above, top_row - top_column)
    matrix = (matrix - jnp.where(lane == sub, 2.0, 0.0)) * emitted
    surface = (lane == levels - 1) & (sub < levels)
    matrix = matrix + decay(surface, whole - bottom_column) - decay(surface, whole - top_column)
    matrix_ref[...] = jnp.where(valid, matrix, 0.0)
    entering = column(solar, lane < sub)
    leaving = column(solar, lane <= sub)
    absorbed = 10.0 * (jnp.exp(-entering) - jnp.exp(-leaving))
    absorbed_ref[...] = jnp.where(sub < levels, absorbed, 0.0)


def scalars_row(values, lanes):
    count = len(values)
    padded = -(-count // 8) * 8
    rows = [jnp.sum(value, axis=0, keepdims=True) for value in values]
    rows += [jnp.zeros_like(rows[0])] * (padded - count)
    sums = jnp.sum(jnp.concatenate(rows, axis=0), axis=1, keepdims=True)
    shape = (padded, lanes)
    spread = jnp.where(iota(shape, 0) == iota(shape, 1), sums, 0.0)
    return jnp.sum(spread, axis=0, keepdims=True)


def fold(tile):
    parts = [tile[8 * j : 8 * j + 8] for j in range(tile.shape[0] // 8)]
    while len(parts) > 1:
        parts = [a + b for a, b in zip(parts[::2], parts[1::2])] + parts[len(parts) // 2 * 2 :]
    return parts[0]


def add_all(parts):
    parts = list(parts)
    while len(parts) > 1:
        parts = [a + b for a, b in zip(parts[::2], parts[1::2])] + parts[len(parts) // 2 * 2 :]
    return parts[0]


def smooth_kernel(
    levels,
    swap,
    kelvin_ref,
    forcing_ref,
    weight_ref,
    inverse_ref,
    matrix_ref,
    absorbed_ref,
    cosine_ref,
    residual_ref,
    smooth_ref,
    rim_ref,
    west_ref,
    east_ref,
    message_ref,
):
    points, padded, across = residual_ref.shape
    kelvin = [kelvin_ref[i] for i in range(points)]
    if swap:
        kelvin = swap_groups(kelvin)
    squares = [tile * tile for tile in kelvin]
    emission = jnp.concatenate([tile * tile for tile in squares], axis=1)
    heating = jnp.dot(matrix_ref[:, :padded], emission, precision=HIGHEST, preferred_element_type=F32)
    sun = absorbed_ref[...] * cosine_ref[...]
    forcing = load_columns(forcing_ref, points, levels, padded)
    weight = load_columns(weight_ref, points, levels, padded)
    real = iota(sun.shape, 0) < levels
    residual = []
    for i in range(points):
        heat = heating[:, i * across : (i + 1) * across] + sun
        mean = jnp.sum(fold(heat), axis=0, keepdims=True) * (1.0 / levels)
        residual.append(forcing[i] + jnp.where(real, heat - mean, 0.0))
    smooth = jnp.dot(
        inverse_ref[:, :padded],
        jnp.concatenate(residual, axis=1),
        precision=HIGHEST,
        preferred_element_type=F32,
    )
    smooth = [smooth[:, i * across : (i + 1) * across] for i in range(points)]
    for i in range(points):
        residual_ref[i] = residual[i]
        smooth_ref[i] = smooth[i]
    west_ref[0], west_ref[1], west_ref[2] = smooth[0], smooth[1], weight[0]
    east_ref[0], east_ref[1], east_ref[2] = smooth[-2], smooth[-1], weight[-1]
    stride = across // points
    lane = iota((padded, across), 1)
    rim = jnp.zeros((padded, across), F32)
    for i in range(points):
        place = (lane - stride * i + 2) & (across - 1)
        rim = jnp.where(place < 4, turn(smooth[i], stride * i), rim)
        rim = jnp.where((place == 5) | (place == 6), turn(weight[i], stride * i + 4), rim)
    rim_ref[...] = rim
    folded = [fold(tile) for tile in smooth]
    loss = add_all([fold(a * b) for a, b in zip(smooth, weight)])
    mass = add_all([fold(tile) for tile in weight])
    every = add_all(folded)
    lane = iota(every.shape, 1)
    scalars = scalars_row(
        [
            add_all([fold(tile) for tile in residual]) - loss,
            folded[0],
            folded[-1],
            jnp.where(lane == 0, every, 0.0),
            jnp.where(lane == across - 1, every, 0.0),
            mass,
        ],
        across,
    )
    levels_row = jnp.concatenate([rim, jnp.zeros((across - padded, across), F32)], axis=0).T
    last = stride * (points - 1)
    message = jnp.concatenate(
        [
            levels_row[0:1],
            levels_row[across - 1 : across],
            levels_row[last : last + 1],
            levels_row[last - 1 : last],
            scalars,
            jnp.zeros((3, across), F32),
        ],
        axis=0,
    )
    for n in range(message_ref.shape[0]):
        message_ref[n] = message


def small_inverse(block):
    size = len(block)
    block = [list(row) for row in block]
    for k in range(size):
        pivot = 1.0 / block[k][k]
        row = [block[k][j] * pivot for j in range(size)]
        for i in range(size):
            if i != k:
                factor = block[i][k]
                for j in range(size):
                    if j != k:
                        block[i][j] = block[i][j] - factor * row[j]
                block[i][k] = -factor * pivot
        for j in range(size):
            block[k][j] = row[j]
        block[k][k] = pivot
    return block


def product(a, b):
    size = range(len(a))
    return [[add_all([a[i][k] * b[k][j] for k in size]) for j in size] for i in size]


def apply(a, v):
    size = range(len(a))
    return [add_all([a[i][k] * v[k] for k in size]) for i in size]


def flip(a):
    return [list(row) for row in zip(*a)]


def turn_block(a, shift):
    return [[turn(value, shift) for value in row] for row in a]


def with_diagonal(block, row_sums, beside):
    size = range(len(block))
    return [
        [
            row_sums[i] - add_all([block[i][k] for k in size if k != i] + beside[i]) if i == j else block[i][j]
            for j in size
        ]
        for i in size
    ]


def coarse_factor(mass, tiles, groups, x_face, y_face):
    zero = jnp.zeros_like(mass)
    size = range(groups)
    diagonal = [[zero - y_face if abs(i - j) == 1 else zero for i in size] for j in size]
    coupling = [[zero - x_face if i == j else zero for i in size] for j in size]
    row_sums = [turn(mass, -j) for j in size]
    diagonal = with_diagonal(diagonal, row_sums, [[zero - 2.0 * x_face]] * groups)
    steps = []
    step = 1
    while step < tiles:
        inverse = small_inverse(diagonal)
        shift = step * groups
        steps.append((inverse, coupling))
        left = product(coupling, turn_block(inverse, shift))
        low = product(left, flip(coupling))
        high = turn_block(product(flip(coupling), product(inverse, coupling)), -shift)
        row_sums = reduce_sums(inverse, coupling, row_sums, shift)
        diagonal = [[diagonal[i][j] - (low[i][j] + high[i][j]) for j in size] for i in size]
        coupling = [[-v for v in row] for row in product(left, turn_block(coupling, shift))]
        step *= 2
        beside = [
            [add_all(coupling[i]), turn(add_all(flip(coupling)[i]), -step * groups)] for i in size
        ]
        diagonal = with_diagonal(diagonal, row_sums, beside)
    last = [[diagonal[i][j] + (coupling[i][j] + coupling[j][i]) for j in size] for i in size]
    last = with_diagonal(last, row_sums, [[]] * groups)
    return steps, small_inverse(last)


def reduce_sums(inverse, coupling, values, shift):
    scaled = apply(inverse, values)
    low = apply(coupling, [turn(v, shift) for v in scaled])
    high = [turn(v, -shift) for v in apply(flip(coupling), scaled)]
    return [v - (a + b) for v, a, b in zip(values, low, high)]


def coarse_solve(steps, last, sums, groups):
    values = [turn(sums, -j) for j in range(groups)]
    shift = groups
    for inverse, coupling in steps:
        values = reduce_sums(inverse, coupling, values, shift)
        shift *= 2
    values = apply(last, values)
    residue = iota(sums.shape, 1) % groups
    result = values[0]
    for j in range(1, groups):
        result = jnp.where(residue == j, turn(values[j], j), result)
    return result


def around(row, groups):
    residue = iota(row.shape, 1) % groups
    south = jnp.where(residue == 0, row, turn(row, 1))
    north = jnp.where(residue == groups - 1, row, turn(row, -1))
    return turn(row, groups), turn(row, -groups), south, north


def by_block(received):
    blocks, lanes = received.shape
    if blocks < lanes:
        received = jnp.concatenate([received] * (lanes // blocks), axis=0)
    return received.T


def save_steps(ref, steps, last):
    rows = [v for inverse, coupling in steps for block in (inverse, coupling) for row in block for v in row]
    rows += [v for row in last for v in row]
    for n, row in enumerate(rows):
        ref[n : n + 1, :] = row


def saved_rows(tiles, groups):
    steps = max(tiles - 1, 0).bit_length()
    return (2 * steps + 1) * groups * groups


def load_steps(ref, tiles, groups):
    place = 0
    blocks = []
    for _ in range(2 * max(tiles - 1, 0).bit_length() + 1):
        block = []
        for _ in range(groups):
            block.append([ref[place + j : place + j + 1, :] for j in range(groups)])
            place += groups
        blocks.append(block)
    return list(zip(blocks[:-1:2], blocks[1::2])), blocks[-1]


def second_kernel(
    levels,
    tiles,
    groups,
    received_ref,
    from_west_ref,
    from_east_ref,
    from_south_ref,
    from_north_ref,
    rim_ref,
    smooth_ref,
    residual_ref,
    weight_ref,
    inverse_ref,
    second_ref,
    steps_ref,
    coarse_ref,
    message_ref,
):
    points, padded, across = smooth_ref.shape
    blocks = tiles * groups
    stride = across // points
    tile_index, group_index = lax.axis_index("tile"), lax.axis_index("grp")
    at_south, at_north = group_index == 0, group_index == groups - 1

    scalars = by_block(received_ref[pl.ds(4, blocks, stride=8), :])
    base, west, east, south, north, mass = [scalars[j : j + 1, :] for j in range(6)]
    residue = iota(base.shape, 1) % groups
    facing_south = jnp.where(residue == 0, south, turn(north, 1))
    facing_north = jnp.where(residue == groups - 1, north, turn(south, -1))
    sums = base + (
        (turn(east, groups) - west)
        + (turn(west, -groups) - east)
        + (facing_south - south)
        + (facing_north - north)
    )
    steps, last = coarse_factor(
        mass, tiles, groups, float(levels * across), float(levels * points)
    )
    coarse = coarse_solve(steps, last, sums, groups)
    save_steps(steps_ref, steps, last)
    coarse_ref[...] = coarse

    west_tile = lax.rem(tile_index + tiles - 1, tiles)
    east_tile = lax.rem(tile_index + 1, tiles)
    south_group = jnp.maximum(group_index - 1, 0)
    north_group = jnp.minimum(group_index + 1, groups - 1)
    places = [
        tile * groups + group
        for tile, group in (
            (tile_index, group_index),
            (west_tile, group_index),
            (east_tile, group_index),
            (tile_index, south_group),
            (tile_index, north_group),
            (west_tile, south_group),
            (east_tile, south_group),
            (west_tile, north_group),
            (east_tile, north_group),
        )
    ]
    lane = iota(coarse.shape, 1)
    picked = [jnp.sum(jnp.where(lane == place, coarse, 0.0), axis=1, keepdims=True) for place in places]
    shape = (padded, across)
    real = iota(shape, 0) < levels
    own, e_west, e_east, e_south, e_north, e_sw, e_se, e_nw, e_ne = [
        jnp.where(real, value, 0.0) for value in picked
    ]

    corner_rows = [
        received_ref[pl.ds(8 * places[5] + 3, 1), :],
        received_ref[pl.ds(8 * places[6] + 1, 1), :],
        received_ref[pl.ds(8 * places[7] + 2, 1), :],
        received_ref[pl.ds(8 * places[8], 1), :],
    ]
    corners = jnp.concatenate(corner_rows + [jnp.zeros((across - 4, across), F32)], axis=0).T
    c_sw, c_se, c_nw, c_ne = [corners[:padded, j : j + 1] for j in range(4)]

    lane = iota(shape, 1)
    first, final = lane == 0, lane == across - 1

    def across_sum(tile, low, high):
        low = jnp.where(first, jnp.where(at_south, tile, low), turn(tile, 1))
        high = jnp.where(final, jnp.where(at_north, tile, high), turn(tile, -1))
        return low + high

    weight = load_columns(weight_ref, points, levels, padded)
    weight = [from_west_ref[2]] + weight + [from_east_ref[2]]
    field = (
        [from_west_ref[0], from_west_ref[1]]
        + [smooth_ref[i] for i in range(points)]
        + [from_east_ref[0], from_east_ref[1]]
    )

    def spread_image(tile_weight, here, ends, low, high):
        value = tile_weight * here
        if ends:
            value = value + add_all([here - there for there in ends])
        return value + jnp.where(first, here - low, jnp.where(final, here - high, 0.0))

    rim, from_south, from_north = rim_ref[...], from_south_ref[...], from_north_ref[...]
    lows = [c_sw] + [turn(from_south, 1 - stride * i) for i in range(points)] + [c_se]
    highs = [c_nw] + [turn(from_north, -1 - stride * i) for i in range(points)] + [c_ne]
    near = [(e_west, (own,), e_sw, e_nw)] + [(own, (), e_south, e_north)] * points
    near += [(e_east, (own,), e_se, e_ne)]
    near[1] = (own, (e_west,), e_south, e_north)
    near[points] = (own, (e_east,), e_south, e_north)
    image = [
        (field[i] + field[i + 2])
        + across_sum(field[i + 1], lows[i], highs[i])
        - (weight[i] * field[i + 1] + spread_image(weight[i], *near[i]))
        for i in range(points + 2)
    ]
    edge = stride * (points - 1)

    def ring_image(tile, step, here, west, east, west_lane, east_lane, c_west, c_east):
        rim_weight = turn(tile, -4)
        spread = rim_weight * here + (here - own)
        spread = spread + jnp.where(lane == west_lane, here - west, jnp.where(lane == east_lane, here - east, 0.0))
        return (
            jnp.where(lane == west_lane, c_west, turn(tile, stride))
            + jnp.where(lane == east_lane, c_east, turn(tile, -stride))
            + (turn(tile, step) + turn(rim, -step))
            - (rim_weight * tile + spread)
        )

    ring_south = ring_image(from_south, 1, e_south, e_sw, e_se, across - 1, edge - 1, c_sw, c_se)
    ring_north = ring_image(from_north, -1, e_north, e_nw, e_ne, 0, edge, c_nw, c_ne)
    inside = lane & (stride - 1)
    is_south, is_north = inside == stride - 1, inside == 0
    ring = jnp.where(is_south, ring_south, jnp.where(is_north, ring_north, 0.0))
    ring_field = jnp.where(is_south, from_south, from_north)
    second = jnp.dot(
        inverse_ref[:, :padded],
        jnp.concatenate(image + [ring], axis=1),
        precision=HIGHEST,
        preferred_element_type=F32,
    )
    second = [second[:, i * across : (i + 1) * across] for i in range(points + 3)]
    ring = ring_field - second.pop()
    second = [field[i + 1] - tile for i, tile in enumerate(second)]

    names = ("image", "change", "residual")
    pairs = {}
    sides = {name: [] for name in names}
    left = []

    def collect(key, value):
        pairs.setdefault(key, []).append(fold(value))

    for i in range(points):
        tile = second[i + 1]
        second_ref[i] = tile
        again = (
            (second[i] + second[i + 2])
            + across_sum(tile, turn(ring, 1 - stride * i), turn(ring, -1 - stride * i))
            - weight[i + 1] * tile
        )
        residual = residual_ref[i]
        result = residual - image[i + 1]
        change = result - again
        left.append(fold(again + (result - 4.0 * tile)))
        heavy = weight[i + 1]
        collect("qq", result * result)
        collect("rq", residual * result)
        collect("qd", result * change)
        collect("dd", change * change)
        collect("rd", residual * change)
        collect("ww", heavy * heavy)
        sides.setdefault("weight", []).append(fold(heavy))
        for name, value in zip(names, (result, change, residual)):
            sides[name].append(fold(value))
            collect("w" + name, heavy * value)
    pairs = {key: add_all(value) for key, value in pairs.items()}
    lane = iota(pairs["qq"].shape, 1)
    out = [pairs[key] for key in ("qq", "rq", "qd", "dd", "rd")]
    for name in names + ("weight",):
        every = add_all(sides[name])
        out += [
            pairs["ww"] if name == "weight" else pairs["w" + name],
            sides[name][0],
            sides[name][-1],
            jnp.where(lane == 0, every, 0.0),
            jnp.where(lane == across - 1, every, 0.0),
        ]
    out.append(add_all(left))
    row = scalars_row(out, across)
    message_ref[...] = jnp.broadcast_to(row, message_ref.shape)


def final_kernel(
    levels,
    tiles,
    groups,
    swap,
    received_ref,
    steps_ref,
    coarse_ref,
    smooth_ref,
    second_ref,
    field_ref,
    packed_ref,
):
    points, padded, across = smooth_ref.shape
    blocks = tiles * groups
    rows = by_block(received_ref[...])
    rows = [rows[j : j + 1, :] for j in range(26)]
    steps, last = load_steps(steps_ref, tiles, groups)
    coarse = coarse_solve(steps, last, rows[25], groups)
    jumps = [coarse - near for near in around(coarse, groups)]

    def against(part):
        return add_all([rows[part] * coarse] + [rows[part + 1 + j] * jumps[j] for j in range(4)])

    j_w, j_e, j_s, j_n = jumps
    x_face, y_face = float(levels * across), float(levels * points)
    weighted = add_all([rows[21 + j] * jumps[j] for j in range(4)])
    square = (
        coarse * (rows[20] * coarse + 2.0 * weighted)
        + x_face * (j_w * j_w + j_e * j_e)
        + y_face * (j_s * j_s + j_n * j_n)
        + (2.0 * levels) * ((j_w + j_e) * (j_s + j_n))
    )
    lane = iota(coarse.shape, 1)
    place = lax.axis_index("tile") * groups + lax.axis_index("grp")
    parts = [
        rows[0],
        rows[1],
        rows[2] + against(5),
        rows[3] + 2.0 * against(10) + square,
        rows[4] + against(15),
    ]
    parts = [jnp.where(lane < blocks, part, 0.0) for part in parts]
    parts += [jnp.where(lane == place, value, 0.0) for value in (coarse_ref[...], coarse)]
    parts.append(jnp.zeros_like(coarse))
    sums = jnp.sum(jnp.concatenate(parts, axis=0), axis=1, keepdims=True)
    qq, rq, qv, vv, rv, first, second = [sums[j : j + 1, :] for j in range(7)]
    alpha = rq / qq
    beta = qv / qq
    kappa = (rv - alpha * qv) / (vv - beta * qv)
    scale = alpha - kappa * beta
    shift = scale * first + kappa * second
    result = [scale * smooth_ref[i] + (kappa * second_ref[i] + shift) for i in range(points)]
    store_columns(field_ref, result, levels)
    if swap:
        result = swap_groups(result)
    for i in range(points):
        packed_ref[i] = result[i]


def per_device(
    forcing_vector,
    shift_weights,
    layer_link_factor,
    previous_kelvin_field,
    longwave_opacity,
    shortwave_opacity,
):
    tiles, groups = lax.axis_size("tile"), lax.axis_size("grp")
    levels, points, across = forcing_vector.shape
    padded = -(-levels // 8) * 8
    blocks = tiles * groups
    lanes = max(across, blocks)
    width = across // tiles
    swap = tiles == points
    flat = (levels * points, across)

    def to_tiles(value):
        return lax.all_to_all(value, "tile", split_axis=0, concat_axis=0, tiled=True)

    def gather(value):
        return lax.all_to_all(value, ("tile", "grp"), split_axis=0, concat_axis=0, tiled=True)

    def part(kernel, *settings):
        return lambda *refs: kernel(*settings, *refs)

    kelvin = previous_kelvin_field
    if swap:
        (kelvin,) = call(
            part(pack_kernel, levels), [(points, padded, across)], kelvin.reshape(flat)
        )
        kelvin = to_tiles(kelvin)
    else:
        kelvin = kelvin.reshape(levels, points, tiles, width).transpose(2, 1, 0, 3)
        kelvin = to_tiles(kelvin).transpose(1, 2, 0, 3).reshape(points, levels, across)
        kelvin = jnp.pad(kelvin, ((0, 0), (0, padded - levels), (0, 0)))

    vectors = (layer_link_factor, longwave_opacity, shortwave_opacity)
    rows = jnp.stack([jnp.pad(v, (0, across - v.shape[0])) for v in vectors])
    rows = jnp.pad(rows, ((0, 8 - len(vectors)), (0, 0)))
    inverse, matrix, absorbed = call(
        part(tables_kernel, levels), [(padded, across)] * 3, rows
    )
    global_row = lax.axis_index("grp") * across + jnp.arange(across)
    latitude = ((global_row.astype(F32) + 0.5) / (across * groups) - 0.5) * (math.pi / 2)
    cosine = jnp.cos(latitude - 0.4)[None, :]

    forcing = forcing_vector.reshape(flat)
    weights = shift_weights.reshape(flat)
    field = (points, padded, across)
    residual, smooth, rim, west, east, message = call(
        part(smooth_kernel, levels, swap),
        [field, field, (padded, across), (3, padded, across), (3, padded, across), (blocks, 8, across)],
        kelvin,
        forcing,
        weights,
        inverse,
        matrix,
        absorbed,
        cosine,
    )
    received = gather(message).reshape(blocks * 8, across)
    forward = [(i, (i + 1) % tiles) for i in range(tiles)]
    backward = [(j, i) for i, j in forward]
    upward = [(i, (i + 1) % groups) for i in range(groups)]
    downward = [(j, i) for i, j in upward]
    from_west = lax.ppermute(east, "tile", forward)
    from_east = lax.ppermute(west, "tile", backward)
    from_south = lax.ppermute(rim, "grp", upward)
    from_north = lax.ppermute(rim, "grp", downward)
    second, steps, coarse, message = call(
        part(second_kernel, levels, tiles, groups),
        [field, (saved_rows(tiles, groups), lanes), (1, lanes), (blocks, across)],
        received,
        from_west,
        from_east,
        from_south,
        from_north,
        rim,
        smooth,
        residual,
        weights,
        inverse,
    )
    received = gather(message)
    solution_field, packed = call(
        part(final_kernel, levels, tiles, groups, swap),
        [flat, field],
        received,
        steps,
        coarse,
        smooth,
        second,
    )
    if swap:
        packed = to_tiles(packed)
        (state,) = call(part(unpack_kernel, levels), [flat], packed)
        state = state.reshape(levels, points, across)
    else:
        packed = packed[:, :levels].reshape(points, levels, tiles, width).transpose(2, 1, 0, 3)
        state = to_tiles(packed).transpose(2, 1, 0, 3).reshape(levels, points, across)
    return solution_field.reshape(levels, points, across), state


def solution(mesh):
    return jax.shard_map(
        per_device,
        mesh=mesh,
        in_specs=(
            P(None, "tile", "grp"),
            P(None, "tile", "grp"),
            P(),
            P(None, None, ("tile", "grp")),
            P(),
            P(),
        ),
        out_specs=(P(None, "tile", "grp"), P(None, None, ("tile", "grp"))),
        check_vma=False,
    )
```

time: 286 us -> 56.9 us (0.20)
  blocking collectives: 168 us -> 18.5 us
  other arithmetic: 35.2 us -> 0.06 us
  local copies, waits for them, and re-layouts: 21.6 us -> 1.61 us
  waiting for transfers between devices: 22.8 us -> 11.9 us
  starting transfers between devices: 26.3 us -> 15.6 us
  Pallas kernels: 0 us -> 8.14 us
  between operations: 8.08 us -> 0.7 us
    unnamed x2 -> x0, blocking collectives: 78 us -> none
    psum x2 -> x0, blocking collectives: 76.4 us -> none  [per_device(): totals = lax.psum(partial_value, ('tile', 'grp'))]
    another operation x14 -> x1, other arithmetic: 23.3 us -> 0.01 us  [per_device(): rows = jnp.stack([jnp.pad(v, (0, across - v.shape[0])) for v in vectors])]
    ppermute x16 -> x4, waiting for transfers between devices: 22.8 us -> 5.76 us  [the longest x1 4.12 us: per_device(): from_south = lax.ppermute(rim, 'grp', upward)]
    ppermute x16 -> x4, starting transfers between devices: 21.2 us -> 6.32 us  [the longest x1 3.62 us: per_device(): from_north = lax.ppermute(rim, 'grp', downward)]
    unnamed x49 -> x12, local copies, waits for them, and re-layouts: 11.1 us -> 1.6 us
    pallas_call x0 -> x6, Pallas kernels: none -> 8.14 us  [call(): pl.pallas_call(kernel, out_shape=[jax.ShapeDtypeStruct(shape, F32) for sh...]
    slice x39 -> x0, local copies, waits for them, and re-layouts: 6.74 us -> none  [the longest x10 1.66 us: with_halo(): first = lax.slice_in_dim(value, 0, width, axis=dim)]
  transfers between devices with their start and end apart: 17 -> 6, of which waited for: 11 -> 3; matrix products, arithmetic and copies ran while one was open for 6% -> 0% of each run, Pallas kernels for 0% -> 1%
where the time goes in v1:
time: 56.9 us; the launch traced here: 56.6 us
  blocking collectives  18.5 us (33%)
  starting transfers between devices  15.6 us (27%)
  waiting for transfers between devices  11.9 us (21%)
  Pallas kernels  8.14 us (14%)
  local copies, waits for them, and re-layouts  1.61 us (3%)
  between operations  0.7 us (1%)
    all_to_all x1, blocking collectives, to_tiles(): lax.all_to_all(value, 'tile', split_axis=0, concat_axis=0, tiled=True)  9.65 us
    all_to_all x1, blocking collectives, gather(): lax.all_to_all(value, ('tile', 'grp'), split_axis=0, concat_axis=0, tiled...  8.86 us
    pallas_call x6, Pallas kernels, call(): pl.pallas_call(kernel, out_shape=[jax.ShapeDtypeStruct(shape, F32) for sh...  8.14 us
    all_to_all x1, waiting for transfers between devices, to_tiles(): lax.all_to_all(value, 'tile', split_axis=0, concat_axis=0, tiled=True)  6.18 us
    all_to_all x1, starting transfers between devices, to_tiles(): lax.all_to_all(value, 'tile', split_axis=0, concat_axis=0, tiled=True)  5.31 us
    ppermute x1, waiting for transfers between devices, per_device(): from_south = lax.ppermute(rim, 'grp', upward)  4.12 us
    all_to_all x1, starting transfers between devices, gather(): lax.all_to_all(value, ('tile', 'grp'), split_axis=0, concat_axis=0, tiled...  3.97 us
    ppermute x1, starting transfers between devices, per_device(): from_north = lax.ppermute(rim, 'grp', downward)  3.62 us
  transfers between devices with their start and end apart: 6, of which 3 were waited for; matrix products, arithmetic and copies ran while one was open for 0% of the time, Pallas kernels for 1%

profile of v1, /device:TPU:0, one launch (start us, length us, event | category | flops | bytes accessed | tf_op | source)
XLA Modules:
  0.0 56.6 jit_solution(14896585415042180662)
XLA Ops:
  0.6 0.0 copy-start.2
  0.6 0.9 %copy-done.2 = f32[70,8,128]{2,1,0:T(8,128)S(1)} copy-done((f32[70,8,128]{2,1,0:T(8,128)S(1)}, f32[70,8,128]{2,1,0:T(8,128)}, u32[]{:S(2)}) %copy-start.2) | copy-done | bytes 286744
  1.6 1.0 %shard_map.77 = f32[8,72,128]{2,1,0:T(8,128)} custom-call(f32[560,128]{1,0:T(8,128)S(1)} %bitcast.20), custom_call_target="tpu_custom_call" | custom-call | tf_op jit(solution)/shard_map/pallas_call | solution.py:29
  2.6 0.0 copy-start.3
  2.6 0.0 copy-start.4
  2.6 0.0 copy-start
  2.6 0.0 copy-start.1
  2.6 5.3 %all-to-all-start = ((f32[8,72,128]{2,1,0:T(8,128)}), f32[8,72,128]{2,1,0:T(8,128)S(1)}, u32[]{:S(2)}, u32[]{:S(2)}) async-start(f32[8,72,128]{2,1,0:T(8,128)} %shard_map.77), calls=%async_computation | async-start | bytes 589824 | tf_op jit(solution)/shard_map/all_to_all | solution.py:645
  8.0 0.0 copy-done.3
  8.0 0.0 copy-done.4
  8.0 0.0 copy-start.5
  8.0 0.6 %copy-done.5 = f32[69]{0:T(128)S(1)} copy-done((f32[69]{0:T(128)S(1)}, f32[69]{0:T(128)}, u32[]{:S(2)}) %copy-start.5) | copy-done | bytes 300
  8.7 0.4 shard_map.78
  9.1 6.2 %all-to-all-done.refs_0_ = f32[8,72,128]{2,1,0:T(8,128)S(1)} async-done(((f32[8,72,128]{2,1,0:T(8,128)}), f32[8,72,128]{2,1,0:T(8,128)S(1)}, u32[]{:S(2)}, u32[]{:S(2)}) %all-to-all-start) | async-done | bytes 294944 | tf_op jit(solution)/shard_map/all_to_all | solution.py:645
  15.3 0.0 copy-done
  15.3 0.0 copy-done.1
  15.3 1.9 %shard_map.79 = (f32[8,72,128]{2,1,0:T(8,128)S(1)}, f32[8,72,128]{2,1,0:T(8,128)S(1)}, f32[72,128]{1,0:T(8,128)S(1)}, f32[3,72,128]{2,1,0:T(8,128)S(1)}, f32[3,7...) custom-call(f32[8,72,128]{2,1,0:T(8,128)S(1)} %all-to-all-done.refs_0_, f32[560,128]{1,0:T(8,128)S(1)} %bitcast.19, ...), custom_call_target="tpu_custom_call" | custom-call | tf_op jit(solution)/shard_map/pallas_call | solution.py:29
  17.1 4.0 %all-to-all-start.1 = ((f32[32,8,128]{2,1,0:T(8,128)}), f32[32,8,128]{2,1,0:T(8,128)S(1)}, u32[]{:S(2)}, u32[]{:S(2)}) async-start(f32[32,8,128]{2,1,0:T(8,128)} %get-tuple-element.20), calls=%async_computation.1 | async-start | bytes 262144 | tf_op jit(solution)/shard_map/all_to_all | solution.py:648
  21.1 0.3 collective-permute-start
  21.4 2.4 %collective-permute-start.1 = (f32[3,72,128]{2,1,0:T(8,128)S(1)}, f32[3,72,128]{2,1,0:T(8,128)S(1)}, u32[]{:S(2)}, u32[]{:S(2)}) collective-permute-start(f32[3,72,128]{2,1,0:T(8,128)S(1)} %get-tuple-element.22), channel_id=1, source_target_pairs={{4,0},{8,4},{12,8},{16,12},{20,16},{24,20},{28,24},{0,28},{5,1},{9... | collective-permute-start | bytes 331784 | tf_op jit(solution)/shard_map/ppermute | solution.py:694
  23.8 3.6 %collective-permute-start.3 = (f32[72,128]{1,0:T(8,128)S(1)}, f32[72,128]{1,0:T(8,128)S(1)}, u32[]{:S(2)}, u32[]{:S(2)}) collective-permute-start(f32[72,128]{1,0:T(8,128)S(1)} %get-tuple-element.23.refs_5_), channel_id=1, source_target_pairs={{1,0},{2,1},{3,2},{0,3},{5,4},{6,5},{7,6},{4,7},{9,8},{10,9},{11,1... | collective-permute-start | bytes 110600 | tf_op jit(solution)/shard_map/ppermute | solution.py:696
  27.4 0.0 collective-permute-start.2
  27.4 1.6 %collective-permute-done.3.refs_4_ = f32[72,128]{1,0:T(8,128)S(1)} collective-permute-done((f32[72,128]{1,0:T(8,128)S(1)}, f32[72,128]{1,0:T(8,128)S(1)}, u32[]{:S(2)}, u32[]{:S(2)}) %collective-permute-start.3) | collective-permute-done | bytes 36896 | tf_op jit(solution)/shard_map/ppermute | solution.py:696
  29.1 4.1 %collective-permute-done.2.refs_3_ = f32[72,128]{1,0:T(8,128)S(1)} collective-permute-done((f32[72,128]{1,0:T(8,128)S(1)}, f32[72,128]{1,0:T(8,128)S(1)}, u32[]{:S(2)}, u32[]{:S(2)}) %collective-permute-start.2) | collective-permute-done | bytes 36896 | tf_op jit(solution)/shard_map/ppermute | solution.py:695
  33.2 0.0 collective-permute-done.refs_1_
  33.2 0.0 collective-permute-done.1.refs_2_
  33.2 0.0 all-to-all-done.1
  33.2 2.2 %shard_map.80 = (f32[8,72,128]{2,1,0:T(8,128)S(1)}, f32[112,128]{1,0:T(8,128)S(1)}, f32[1,128]{1,0:T(1,128)S(1)}, f32[32,128]{1,0:T(8,128)S(1)}) custom-call(f32[256,128]{1,0:T(8,128)S(1)} %bitcast.18, f32[3,72,128]{2,1,0:T(8,128)S(1)} %collective-permute-done.refs_1_, f32[3,72,128]{2,1,0:T(8,128)S(1)} %collective-permute-done.1.refs_2_, ...), custom_call_target="tpu_custom_call" | custom-call | tf_op jit(solution)/shard_map/pallas_call | solution.py:29
  35.4 8.9 %all_to_all.26 = f32[32,1,128]{2,1,0:T(1,128)S(1)} all-to-all(f32[32,1,128]{2,1,0:T(1,128)S(1)} %bitcast.22), channel_id=1, replica_groups=mesh['tile'=8,'grp'=4] {'tile','grp'}, dimensions={0} | all-to-all | bytes 32768 | tf_op jit(solution)/shard_map/all_to_all | solution.py:648
  44.3 1.6 %shard_map.81 = (f32[560,128]{1,0:T(8,128)}, f32[8,72,128]{2,1,0:T(8,128)S(1)}) custom-call(f32[32,128]{1,0:T(8,128)S(1)} %bitcast.21, f32[112,128]{1,0:T(8,128)S(1)} %get-tuple-element.27.refs_1_, f32[1,128]{1,0:T(1,128)S(1)} %get-tuple-element.28.refs_2_, f32[8,72,128]{2,1,0:T(8,128)S(1)} %get-tuple-element.24.refs_6_.refs_3_, ...), custom_call_target="tpu_custom_call" | custom-call | tf_op jit(solution)/shard_map/pallas_call | solution.py:29
  45.9 9.7 %all_to_all.27.refs_0_ = f32[8,72,128]{2,1,0:T(8,128)S(1)} all-to-all(f32[8,72,128]{2,1,0:T(8,128)S(1)} %get-tuple-element.31), channel_id=1, replica_groups=mesh['tile'=8,'grp'=4] {'tile'}, dimensions={0} | all-to-all | bytes 589824 | tf_op jit(solution)/shard_map/all_to_all | solution.py:645
  55.5 1.1 %shard_map.82 = f32[560,128]{1,0:T(8,128)} custom-call(f32[8,72,128]{2,1,0:T(8,128)S(1)} %all_to_all.27.refs_0_), custom_call_target="tpu_custom_call" | custom-call | tf_op jit(solution)/shard_map/pallas_call | solution.py:29
  (4 shorter events, 0.1 us)
Async XLA Ops:
  0.6 1.0 %copy-start.2 = (f32[70,8,128]{2,1,0:T(8,128)S(1)}, f32[70,8,128]{2,1,0:T(8,128)}, u32[]{:S(2)}) copy-start(f32[70,8,128]{2,1,0:T(8,128)} %param.9) | copy-start | bytes 860164
  2.6 5.3 %copy-start.3 = (f32[70]{0:T(128)S(1)}, f32[70]{0:T(128)}, u32[]{:S(2)}) copy-start(f32[70]{0:T(128)} %param.11) | copy-start | bytes 844
  2.6 5.3 %copy-start.4 = (f32[70]{0:T(128)S(1)}, f32[70]{0:T(128)}, u32[]{:S(2)}) copy-start(f32[70]{0:T(128)} %param.10) | copy-start | bytes 844
  2.6 12.6 %copy-start = (f32[70,8,128]{2,1,0:T(8,128)S(1)}, f32[70,8,128]{2,1,0:T(8,128)}, u32[]{:S(2)}) copy-start(f32[70,8,128]{2,1,0:T(8,128)} %param.7) | copy-start | bytes 860164
  2.6 12.6 %copy-start.1 = (f32[70,8,128]{2,1,0:T(8,128)S(1)}, f32[70,8,128]{2,1,0:T(8,128)}, u32[]{:S(2)}) copy-start(f32[70,8,128]{2,1,0:T(8,128)} %param.6) | copy-start | bytes 860164
  2.6 12.6 %all-to-all-start = ((f32[8,72,128]{2,1,0:T(8,128)}), f32[8,72,128]{2,1,0:T(8,128)S(1)}, u32[]{:S(2)}, u32[]{:S(2)}) async-start(f32[8,72,128]{2,1,0:T(8,128)} %shard_map.77), calls=%async_computation | async-start | bytes 589824 | tf_op jit(solution)/shard_map/all_to_all | solution.py:645
  8.0 0.7 %copy-start.5 = (f32[69]{0:T(128)S(1)}, f32[69]{0:T(128)}, u32[]{:S(2)}) copy-start(f32[69]{0:T(128)} %param.8) | copy-start | bytes 832
  17.1 16.1 %all-to-all-start.1 = ((f32[32,8,128]{2,1,0:T(8,128)}), f32[32,8,128]{2,1,0:T(8,128)S(1)}, u32[]{:S(2)}, u32[]{:S(2)}) async-start(f32[32,8,128]{2,1,0:T(8,128)} %get-tuple-element.20), calls=%async_computation.1 | async-start | bytes 262144 | tf_op jit(solution)/shard_map/all_to_all | solution.py:648
  21.1 12.1 %collective-permute-start = (f32[3,72,128]{2,1,0:T(8,128)S(1)}, f32[3,72,128]{2,1,0:T(8,128)S(1)}, u32[]{:S(2)}, u32[]{:S(2)}) collective-permute-start(f32[3,72,128]{2,1,0:T(8,128)S(1)} %get-tuple-element.21), channel_id=1, source_target_pairs={{0,4},{4,8},{8,12},{12,16},{16,20},{20,24},{24,28},{28,0},{1,5},{5... | collective-permute-start | bytes 331784 | tf_op jit(solution)/shard_map/ppermute | solution.py:693
  21.4 11.8 %collective-permute-start.1 = (f32[3,72,128]{2,1,0:T(8,128)S(1)}, f32[3,72,128]{2,1,0:T(8,128)S(1)}, u32[]{:S(2)}, u32[]{:S(2)}) collective-permute-start(f32[3,72,128]{2,1,0:T(8,128)S(1)} %get-tuple-element.22), channel_id=1, source_target_pairs={{4,0},{8,4},{12,8},{16,12},{20,16},{24,20},{28,24},{0,28},{5,1},{9... | collective-permute-start | bytes 331784 | tf_op jit(solution)/shard_map/ppermute | solution.py:694
  23.8 5.3 %collective-permute-start.3 = (f32[72,128]{1,0:T(8,128)S(1)}, f32[72,128]{1,0:T(8,128)S(1)}, u32[]{:S(2)}, u32[]{:S(2)}) collective-permute-start(f32[72,128]{1,0:T(8,128)S(1)} %get-tuple-element.23.refs_5_), channel_id=1, source_target_pairs={{1,0},{2,1},{3,2},{0,3},{5,4},{6,5},{7,6},{4,7},{9,8},{10,9},{11,1... | collective-permute-start | bytes 110600 | tf_op jit(solution)/shard_map/ppermute | solution.py:696
  27.4 5.8 %collective-permute-start.2 = (f32[72,128]{1,0:T(8,128)S(1)}, f32[72,128]{1,0:T(8,128)S(1)}, u32[]{:S(2)}, u32[]{:S(2)}) collective-permute-start(f32[72,128]{1,0:T(8,128)S(1)} %get-tuple-element.23.refs_5_), channel_id=1, source_target_pairs={{0,1},{1,2},{2,3},{3,0},{4,5},{5,6},{6,7},{7,4},{8,9},{9,10},{10,1... | collective-permute-start | bytes 110600 | tf_op jit(solution)/shard_map/ppermute | solution.py:695

commit v2 on v1

--- a/solution.py
+++ b/solution.py
@@ -9,6 +9,8 @@
 
 F32 = jnp.float32
 HIGHEST = lax.Precision.HIGHEST
+MESSAGE_ROWS = 4
+LAST_ROWS = 4
 VMEM = pl.BlockSpec(memory_space=pltpu.VMEM)
 
 
@@ -25,12 +27,13 @@
     return jnp.sum(value, axis=(0, 1), keepdims=True)
 
 
-def call(kernel, outs, *args):
+def call(kernel, outs, *args, scratch=()):
     return pl.pallas_call(
         kernel,
         out_shape=[jax.ShapeDtypeStruct(shape, F32) for shape in outs],
         in_specs=[VMEM] * len(args),
         out_specs=[VMEM] * len(outs),
+        scratch_shapes=[pltpu.VMEM(shape, F32) for shape in scratch],
         compiler_params=pltpu.CompilerParams(vmem_limit_bytes=32 * 1024 * 1024),
     )(*args)
 
@@ -71,11 +74,6 @@
     points, padded, _ = out_ref.shape
     for s, tile in enumerate(swap_groups(load_columns(x_ref, points, levels, padded))):
         out_ref[s] = tile
-
-
-def unpack_kernel(levels, x_ref, out_ref):
-    points = x_ref.shape[0]
-    store_columns(out_ref, swap_groups([x_ref[s] for s in range(points)]), levels)
 
 
 def tables_kernel(levels, rows_ref, inverse_ref, matrix_ref, absorbed_ref):
@@ -154,6 +152,8 @@
 
 def smooth_kernel(
     levels,
+    tiles,
+    groups,
     swap,
     kelvin_ref,
     forcing_ref,
@@ -164,9 +164,6 @@
     cosine_ref,
     residual_ref,
     smooth_ref,
-    rim_ref,
-    west_ref,
-    east_ref,
     message_ref,
 ):
     points, padded, across = residual_ref.shape
@@ -195,16 +192,6 @@
     for i in range(points):
         residual_ref[i] = residual[i]
         smooth_ref[i] = smooth[i]
-    west_ref[0], west_ref[1], west_ref[2] = smooth[0], smooth[1], weight[0]
-    east_ref[0], east_ref[1], east_ref[2] = smooth[-2], smooth[-1], weight[-1]
-    stride = across // points
-    lane = iota((padded, across), 1)
-    rim = jnp.zeros((padded, across), F32)
-    for i in range(points):
-        place = (lane - stride * i + 2) & (across - 1)
-        rim = jnp.where(place < 4, turn(smooth[i], stride * i), rim)
-        rim = jnp.where((place == 5) | (place == 6), turn(weight[i], stride * i + 4), rim)
-    rim_ref[...] = rim
     folded = [fold(tile) for tile in smooth]
     loss = add_all([fold(a * b) for a, b in zip(smooth, weight)])
     mass = add_all([fold(tile) for tile in weight])
@@ -221,21 +208,67 @@
         ],
         across,
     )
-    levels_row = jnp.concatenate([rim, jnp.zeros((across - padded, across), F32)], axis=0).T
-    last = stride * (points - 1)
-    message = jnp.concatenate(
-        [
-            levels_row[0:1],
-            levels_row[across - 1 : across],
-            levels_row[last : last + 1],
-            levels_row[last - 1 : last],
-            scalars,
-            jnp.zeros((3, across), F32),
-        ],
-        axis=0,
-    )
-    for n in range(message_ref.shape[0]):
-        message_ref[n] = message
+    lane = iota((padded, across), 1)
+    corner = jnp.where((lane == 0) | (lane == across - 1), smooth[0], turn(smooth[-1], 2))
+    rows = jnp.concatenate([corner, jnp.zeros((across - padded, across), F32)], axis=0).T
+    scalars = turn(scalars, padded)
+    message_ref[...] = jnp.zeros(message_ref.shape, F32)
+    message_ref[:, 0, :] = jnp.broadcast_to(scalars, (message_ref.shape[0], across))
+    corners = (0, 2, across - 1, 1)
+    for place, corner in zip(neighbours(tiles, groups)[5:], corners):
+        message_ref[pl.ds(place, 1), 0, :] = rows[corner : corner + 1] + scalars
+
+
+def rim_kernel(levels, smooth_ref, weight_ref, rim_ref):
+    points, padded, across = smooth_ref.shape
+    weight = load_columns(weight_ref, points, levels, padded)
+    stride = across // points
+    lane = iota((padded, across), 1)
+    rim = jnp.zeros((padded, across), F32)
+    for i in range(points):
+        place = (lane - stride * i + 2) & (across - 1)
+        rim = jnp.where(place < 4, turn(smooth_ref[i], stride * i), rim)
+        rim = jnp.where((place == 5) | (place == 6), turn(weight[i], stride * i + 4), rim)
+    rim_ref[...] = rim
+
+
+def side_kernel(levels, swap, smooth_ref, weight_ref, _, inner_ref, outer_ref, *packed_ref):
+    points, padded, _ = smooth_ref.shape
+    even = lax.rem(lax.axis_index("tile"), 2) == 0
+    for j, place in enumerate((0, 1)):
+        west, east = smooth_ref[place], smooth_ref[points - 2 + place]
+        inner_ref[j] = jnp.where(even, east, west)
+        outer_ref[j] = jnp.where(even, west, east)
+    extra = jnp.zeros((padded - levels, inner_ref.shape[2]), F32)
+    west, east = [
+        jnp.concatenate([weight_ref[pl.ds(i, levels, stride=points), :], extra], axis=0)
+        for i in (0, points - 1)
+    ]
+    inner_ref[2] = jnp.where(even, east, west)
+    outer_ref[2] = jnp.where(even, west, east)
+    if swap:
+        for s, tile in enumerate(swap_groups([smooth_ref[i] for i in range(points)])):
+            packed_ref[0][s] = tile
+
+
+def send_kernel(smooth_ref, second_ref, *out_refs):
+    *out_refs, packed_ref = out_refs
+    points = second_ref.shape[0]
+    for s, tile in enumerate(swap_groups([second_ref[i] for i in range(points)])):
+        packed_ref[s] = tile
+    tile = lax.axis_index("tile")
+    for k, out_ref in enumerate(out_refs):
+        out_ref[0] = smooth_ref[tile ^ k]
+        out_ref[1] = packed_ref[tile ^ k]
+
+
+def neighbours(tiles, groups):
+    tile, group = lax.axis_index("tile"), lax.axis_index("grp")
+    west, east = lax.rem(tile + tiles - 1, tiles), lax.rem(tile + 1, tiles)
+    south, north = jnp.maximum(group - 1, 0), jnp.minimum(group + 1, groups - 1)
+    pairs = [(tile, group), (west, group), (east, group), (tile, south), (tile, north)]
+    pairs += [(west, south), (east, south), (west, north), (east, north)]
+    return [x * groups + y for x, y in pairs]
 
 
 def small_inverse(block):
@@ -374,33 +407,10 @@
     return list(zip(blocks[:-1:2], blocks[1::2])), blocks[-1]
 
 
-def second_kernel(
-    levels,
-    tiles,
-    groups,
-    received_ref,
-    from_west_ref,
-    from_east_ref,
-    from_south_ref,
-    from_north_ref,
-    rim_ref,
-    smooth_ref,
-    residual_ref,
-    weight_ref,
-    inverse_ref,
-    second_ref,
-    steps_ref,
-    coarse_ref,
-    message_ref,
-):
-    points, padded, across = smooth_ref.shape
-    blocks = tiles * groups
-    stride = across // points
-    tile_index, group_index = lax.axis_index("tile"), lax.axis_index("grp")
-    at_south, at_north = group_index == 0, group_index == groups - 1
-
-    scalars = by_block(received_ref[pl.ds(4, blocks, stride=8), :])
-    base, west, east, south, north, mass = [scalars[j : j + 1, :] for j in range(6)]
+def coarse_kernel(levels, points, tiles, groups, received_ref, steps_ref, coarse_ref):
+    padded = -(-levels // 8) * 8
+    scalars = by_block(received_ref[:, 0, :])
+    base, west, east, south, north, mass = [scalars[padded + j : padded + j + 1, :] for j in range(6)]
     residue = iota(base.shape, 1) % groups
     facing_south = jnp.where(residue == 0, south, turn(north, 1))
     facing_north = jnp.where(residue == groups - 1, north, turn(south, -1))
@@ -411,30 +421,41 @@
         + (facing_north - north)
     )
     steps, last = coarse_factor(
-        mass, tiles, groups, float(levels * across), float(levels * points)
+        mass, tiles, groups, float(levels * received_ref.shape[2]), float(levels * points)
     )
     coarse = coarse_solve(steps, last, sums, groups)
     save_steps(steps_ref, steps, last)
     coarse_ref[...] = coarse
 
-    west_tile = lax.rem(tile_index + tiles - 1, tiles)
-    east_tile = lax.rem(tile_index + 1, tiles)
-    south_group = jnp.maximum(group_index - 1, 0)
-    north_group = jnp.minimum(group_index + 1, groups - 1)
-    places = [
-        tile * groups + group
-        for tile, group in (
-            (tile_index, group_index),
-            (west_tile, group_index),
-            (east_tile, group_index),
-            (tile_index, south_group),
-            (tile_index, north_group),
-            (west_tile, south_group),
-            (east_tile, south_group),
-            (west_tile, north_group),
-            (east_tile, north_group),
-        )
-    ]
+
+def second_kernel(
+    levels,
+    tiles,
+    groups,
+    received_ref,
+    inner_ref,
+    outer_ref,
+    low_ref,
+    high_ref,
+    rim_ref,
+    smooth_ref,
+    residual_ref,
+    weight_ref,
+    inverse_ref,
+    coarse_ref,
+    second_ref,
+    message_ref,
+):
+    points, padded, across = smooth_ref.shape
+    blocks = tiles * groups
+    stride = across // points
+    group_index = lax.axis_index("grp")
+    even_tile = lax.rem(lax.axis_index("tile"), 2) == 0
+    even_group = lax.rem(group_index, 2) == 0
+    at_south, at_north = group_index == 0, group_index == groups - 1
+
+    coarse = coarse_ref[...]
+    places = neighbours(tiles, groups)
     lane = iota(coarse.shape, 1)
     picked = [jnp.sum(jnp.where(lane == place, coarse, 0.0), axis=1, keepdims=True) for place in places]
     shape = (padded, across)
@@ -443,12 +464,8 @@
         jnp.where(real, value, 0.0) for value in picked
     ]
 
-    corner_rows = [
-        received_ref[pl.ds(8 * places[5] + 3, 1), :],
-        received_ref[pl.ds(8 * places[6] + 1, 1), :],
-        received_ref[pl.ds(8 * places[7] + 2, 1), :],
-        received_ref[pl.ds(8 * places[8], 1), :],
-    ]
+    corner_rows = [received_ref[pl.ds(place, 1), 0, :] for place in places[5:]]
+    corner_rows = [jnp.where(iota(row.shape, 1) < padded, row, 0.0) for row in corner_rows]
     corners = jnp.concatenate(corner_rows + [jnp.zeros((across - 4, across), F32)], axis=0).T
     c_sw, c_se, c_nw, c_ne = [corners[:padded, j : j + 1] for j in range(4)]
 
@@ -461,12 +478,10 @@
         return low + high
 
     weight = load_columns(weight_ref, points, levels, padded)
-    weight = [from_west_ref[2]] + weight + [from_east_ref[2]]
-    field = (
-        [from_west_ref[0], from_west_ref[1]]
-        + [smooth_ref[i] for i in range(points)]
-        + [from_east_ref[0], from_east_ref[1]]
-    )
+    from_west = [jnp.where(even_tile, outer_ref[j], inner_ref[j]) for j in range(3)]
+    from_east = [jnp.where(even_tile, inner_ref[j], outer_ref[j]) for j in range(3)]
+    weight = from_west[2:] + weight + from_east[2:]
+    field = from_west[:2] + [smooth_ref[i] for i in range(points)] + from_east[:2]
 
     def spread_image(tile_weight, here, ends, low, high):
         value = tile_weight * here
@@ -474,7 +489,9 @@
             value = value + add_all([here - there for there in ends])
         return value + jnp.where(first, here - low, jnp.where(final, here - high, 0.0))
 
-    rim, from_south, from_north = rim_ref[...], from_south_ref[...], from_north_ref[...]
+    rim, low, high = rim_ref[...], low_ref[...], high_ref[...]
+    from_south = jnp.where(even_group, high, low)
+    from_north = jnp.where(even_group, low, high)
     lows = [c_sw] + [turn(from_south, 1 - stride * i) for i in range(points)] + [c_se]
     highs = [c_nw] + [turn(from_north, -1 - stride * i) for i in range(points)] + [c_ne]
     near = [(e_west, (own,), e_sw, e_nw)] + [(own, (), e_south, e_north)] * points
@@ -561,7 +578,8 @@
         ]
     out.append(add_all(left))
     row = scalars_row(out, across)
-    message_ref[...] = jnp.broadcast_to(row, message_ref.shape)
+    message_ref[...] = jnp.zeros(message_ref.shape, F32)
+    message_ref[:, 0, :] = jnp.broadcast_to(row, (blocks, across))
 
 
 def final_kernel(
@@ -574,12 +592,15 @@
     coarse_ref,
     smooth_ref,
     second_ref,
-    field_ref,
-    packed_ref,
+    *refs,
 ):
+    if swap:
+        *part_refs, field_ref, state_ref, scratch_ref = refs
+    else:
+        field_ref, state_ref = refs
     points, padded, across = smooth_ref.shape
     blocks = tiles * groups
-    rows = by_block(received_ref[...])
+    rows = by_block(received_ref[:, 0, :])
     rows = [rows[j : j + 1, :] for j in range(26)]
     steps, last = load_steps(steps_ref, tiles, groups)
     coarse = coarse_solve(steps, last, rows[25], groups)
@@ -598,7 +619,7 @@
         + (2.0 * levels) * ((j_w + j_e) * (j_s + j_n))
     )
     lane = iota(coarse.shape, 1)
-    place = lax.axis_index("tile") * groups + lax.axis_index("grp")
+    tile, group = lax.axis_index("tile"), lax.axis_index("grp")
     parts = [
         rows[0],
         rows[1],
@@ -607,21 +628,29 @@
         rows[4] + against(15),
     ]
     parts = [jnp.where(lane < blocks, part, 0.0) for part in parts]
-    parts += [jnp.where(lane == place, value, 0.0) for value in (coarse_ref[...], coarse)]
-    parts.append(jnp.zeros_like(coarse))
+    parts += [jnp.zeros_like(coarse)] * 3
     sums = jnp.sum(jnp.concatenate(parts, axis=0), axis=1, keepdims=True)
-    qq, rq, qv, vv, rv, first, second = [sums[j : j + 1, :] for j in range(7)]
+    qq, rq, qv, vv, rv = [sums[j : j + 1, :] for j in range(5)]
     alpha = rq / qq
     beta = qv / qq
     kappa = (rv - alpha * qv) / (vv - beta * qv)
     scale = alpha - kappa * beta
-    shift = scale * first + kappa * second
-    result = [scale * smooth_ref[i] + (kappa * second_ref[i] + shift) for i in range(points)]
+    constant = scale * coarse_ref[...] + kappa * coarse
+    others = points if swap else 1
+    parts = [jnp.where(lane == (tile ^ k) * groups + group, constant, 0.0) for k in range(others)]
+    parts += [jnp.zeros_like(coarse)] * (-others % 8)
+    shifts = jnp.sum(jnp.concatenate(parts, axis=0), axis=1, keepdims=True)
+    shifts = [shifts[k : k + 1, :] for k in range(others)]
+    result = [scale * smooth_ref[i] + (kappa * second_ref[i] + shifts[0]) for i in range(points)]
     store_columns(field_ref, result, levels)
     if swap:
-        result = swap_groups(result)
-    for i in range(points):
-        packed_ref[i] = result[i]
+        for k, part_ref in enumerate(part_refs):
+            scratch_ref[tile ^ k] = scale * part_ref[0] + (kappa * part_ref[1] + shifts[k])
+        result = swap_groups([scratch_ref[s] for s in range(points)])
+        store_columns(state_ref, result, levels)
+    else:
+        for i in range(points):
+            state_ref[i] = result[i]
 
 
 def per_device(
@@ -674,9 +703,10 @@
     forcing = forcing_vector.reshape(flat)
     weights = shift_weights.reshape(flat)
     field = (points, padded, across)
-    residual, smooth, rim, west, east, message = call(
-        part(smooth_kernel, levels, swap),
-        [field, field, (padded, across), (3, padded, across), (3, padded, across), (blocks, 8, across)],
+    message = (blocks, MESSAGE_ROWS, across)
+    residual, smooth, message = call(
+        part(smooth_kernel, levels, tiles, groups, swap),
+        [field, field, message],
         kelvin,
         forcing,
         weights,
@@ -685,47 +715,68 @@
         absorbed,
         cosine,
     )
-    received = gather(message).reshape(blocks * 8, across)
-    forward = [(i, (i + 1) % tiles) for i in range(tiles)]
-    backward = [(j, i) for i, j in forward]
-    upward = [(i, (i + 1) % groups) for i in range(groups)]
-    downward = [(j, i) for i, j in upward]
-    from_west = lax.ppermute(east, "tile", forward)
-    from_east = lax.ppermute(west, "tile", backward)
-    from_south = lax.ppermute(rim, "grp", upward)
-    from_north = lax.ppermute(rim, "grp", downward)
-    second, steps, coarse, message = call(
+    tile, side = (padded, across), (3, padded, across)
+    (rim,) = call(part(rim_kernel, levels), [tile], smooth, weights)
+    inner, outer, *packed = call(
+        part(side_kernel, levels, swap), [side, side] + [field] * swap, smooth, weights, rim
+    )
+    received = gather(message)
+
+    def inner_pairs(size):
+        return [(i, i ^ 1) for i in range(size) if i ^ 1 < size]
+
+    def outer_pairs(size, around):
+        pairs = [(i, (i + 1) % size) for i in range(1, size, 2) if around or i + 1 < size]
+        return pairs + [(j, i) for i, j in pairs]
+
+    inner = lax.ppermute(inner, "tile", inner_pairs(tiles))
+    outer = lax.ppermute(outer, "tile", outer_pairs(tiles, True))
+    low = lax.ppermute(rim, "grp", inner_pairs(groups))
+    high = lax.ppermute(rim, "grp", outer_pairs(groups, False))
+    steps, coarse = call(
+        part(coarse_kernel, levels, points, tiles, groups),
+        [(saved_rows(tiles, groups), lanes), (1, lanes)],
+        received,
+    )
+    second, message = call(
         part(second_kernel, levels, tiles, groups),
-        [field, (saved_rows(tiles, groups), lanes), (1, lanes), (blocks, across)],
+        [field, (blocks, LAST_ROWS, across)],
         received,
-        from_west,
-        from_east,
-        from_south,
-        from_north,
+        inner,
+        outer,
+        low,
+        high,
         rim,
         smooth,
         residual,
         weights,
         inverse,
+        coarse,
     )
     received = gather(message)
-    solution_field, packed = call(
+    parts = []
+    if swap:
+        parts = list(
+            call(send_kernel, [(2, padded, across)] * tiles, packed[0], second, scratch=[field])
+        )
+        for k in range(1, tiles):
+            parts[k] = lax.ppermute(parts[k], "tile", [(i, i ^ k) for i in range(tiles)])
+    solution_field, state = call(
         part(final_kernel, levels, tiles, groups, swap),
-        [flat, field],
+        [flat, flat if swap else field],
         received,
         steps,
         coarse,
         smooth,
         second,
-    )
-    if swap:
-        packed = to_tiles(packed)
-        (state,) = call(part(unpack_kernel, levels), [flat], packed)
-        state = state.reshape(levels, points, across)
-    else:
-        packed = packed[:, :levels].reshape(points, levels, tiles, width).transpose(2, 1, 0, 3)
-        state = to_tiles(packed).transpose(2, 1, 0, 3).reshape(levels, points, across)
-    return solution_field.reshape(levels, points, across), state
+        *parts,
+        scratch=[field] * swap,
+    )
+    if not swap:
+        state = state[:, :levels].reshape(points, levels, tiles, width).transpose(2, 1, 0, 3)
+        state = to_tiles(state).transpose(2, 1, 0, 3)
+    shape = (levels, points, across)
+    return solution_field.reshape(shape), state.reshape(shape)
 
 
 def solution(mesh):

time: 56.9 us -> 51.3 us (0.902)
  blocking collectives: 18.5 us -> 0 us
  starting transfers between devices: 15.6 us -> 27 us
  Pallas kernels: 8.14 us -> 9.24 us
    all_to_all x2 -> x0, blocking collectives: 18.5 us -> none  [the longest x1 9.65 us: to_tiles(): lax.all_to_all(value, 'tile', split_axis=0, concat_axis=0, tiled=True)]
    ppermute x4 -> x11, starting transfers between devices: 6.32 us -> 13.9 us  [the longest x7 6.14 us: per_device(): lax.ppermute(parts[k], 'tile', [(i, i ^ k) for i in range(tiles)])]
    all_to_all x1 -> x2, starting transfers between devices: 3.97 us -> 7.8 us  [gather(): lax.all_to_all(value, ('tile', 'grp'), split_axis=0, concat_axis=0, tiled...]
    pallas_call x6 -> x9, Pallas kernels: 8.14 us -> 9.24 us  [call(): pl.pallas_call(kernel, out_shape=[jax.ShapeDtypeStruct(shape, F32) for sh...]
    ppermute x4 -> x11, waiting for transfers between devices: 5.76 us -> 6.06 us  [the longest x7 4.98 us: per_device(): lax.ppermute(parts[k], 'tile', [(i, i ^ k) for i in range(tiles)])]
  transfers between devices with their start and end apart: 6 -> 14, of which waited for: 3 -> 4; matrix products, arithmetic and copies ran while one was open for 0% -> 0% of each run, Pallas kernels for 1% -> 3%
where the time goes in v2:
time: 51.3 us; the launch traced here: 51 us
  starting transfers between devices  27 us (53%)
  waiting for transfers between devices  12.2 us (24%)
  Pallas kernels  9.24 us (18%)
  local copies, waits for them, and re-layouts  1.61 us (3%)
  between operations  0.76 us (1%)
    pallas_call x9, Pallas kernels, call(): pl.pallas_call(kernel, out_shape=[jax.ShapeDtypeStruct(shape, F32) for sh...  9.24 us
    all_to_all x2, starting transfers between devices, gather(): lax.all_to_all(value, ('tile', 'grp'), split_axis=0, concat_axis=0, tiled...  7.8 us
    all_to_all x1, waiting for transfers between devices, to_tiles(): lax.all_to_all(value, 'tile', split_axis=0, concat_axis=0, tiled=True)  6.18 us
    ppermute x7, starting transfers between devices, per_device(): lax.ppermute(parts[k], 'tile', [(i, i ^ k) for i in range(tiles)])  6.14 us
    all_to_all x1, starting transfers between devices, to_tiles(): lax.all_to_all(value, 'tile', split_axis=0, concat_axis=0, tiled=True)  5.31 us
    ppermute x7, waiting for transfers between devices, per_device(): lax.ppermute(parts[k], 'tile', [(i, i ^ k) for i in range(tiles)])  4.98 us
    ppermute x1, starting transfers between devices, per_device(): low = lax.ppermute(rim, 'grp', inner_pairs(groups))  4.27 us
    ppermute x1, starting transfers between devices, per_device(): outer = lax.ppermute(outer, 'tile', outer_pairs(tiles, True))  2.53 us
  transfers between devices with their start and end apart: 14, of which 4 were waited for; matrix products, arithmetic and copies ran while one was open for 0% of the time, Pallas kernels for 3%

profile of v2, /device:TPU:0, one launch (start us, length us, event | category | flops | bytes accessed | tf_op | source)
XLA Modules:
  0.0 51.0 jit_solution(10912784213136641092)
XLA Ops:
  0.6 0.0 copy-start.2
  0.6 0.9 %copy-done.2 = f32[70,8,128]{2,1,0:T(8,128)S(1)} copy-done((f32[70,8,128]{2,1,0:T(8,128)S(1)}, f32[70,8,128]{2,1,0:T(8,128)}, u32[]{:S(2)}) %copy-start.2) | copy-done | bytes 286744
  1.6 1.0 %shard_map.77 = f32[8,72,128]{2,1,0:T(8,128)} custom-call(f32[560,128]{1,0:T(8,128)S(1)} %bitcast.16), custom_call_target="tpu_custom_call" | custom-call | tf_op jit(solution)/shard_map/pallas_call | solution.py:31
  2.6 0.0 copy-start.3
  2.6 0.0 copy-start.4
  2.6 0.0 copy-start
  2.6 0.0 copy-start.1
  2.6 5.3 %all-to-all-start = ((f32[8,72,128]{2,1,0:T(8,128)}), f32[8,72,128]{2,1,0:T(8,128)S(1)}, u32[]{:S(2)}, u32[]{:S(2)}) async-start(f32[8,72,128]{2,1,0:T(8,128)} %shard_map.77), calls=%async_computation | async-start | bytes 589824 | tf_op jit(solution)/shard_map/all_to_all | solution.py:674
  8.0 0.0 copy-done.3
  8.0 0.0 copy-done.4
  8.0 0.0 copy-start.5
  8.0 0.6 %copy-done.5 = f32[69]{0:T(128)S(1)} copy-done((f32[69]{0:T(128)S(1)}, f32[69]{0:T(128)}, u32[]{:S(2)}) %copy-start.5) | copy-done | bytes 300
  8.7 0.4 shard_map.78
  9.1 6.2 %all-to-all-done.refs_0_ = f32[8,72,128]{2,1,0:T(8,128)S(1)} async-done(((f32[8,72,128]{2,1,0:T(8,128)}), f32[8,72,128]{2,1,0:T(8,128)S(1)}, u32[]{:S(2)}, u32[]{:S(2)}) %all-to-all-start) | async-done | bytes 294944 | tf_op jit(solution)/shard_map/all_to_all | solution.py:674
  15.2 0.0 copy-done
  15.3 0.0 copy-done.1
  15.3 1.9 %shard_map.79 = (f32[8,72,128]{2,1,0:T(8,128)S(1)}, f32[8,72,128]{2,1,0:T(8,128)S(1)}, f32[32,4,128]{2,1,0:T(4,128)}) custom-call(f32[8,72,128]{2,1,0:T(8,128)S(1)} %all-to-all-done.refs_0_, f32[560,128]{1,0:T(8,128)S(1)} %bitcast.15, f32[560,128]{1,0:T(8,128)S(1)} %bitcast.11, f32[72,128]{1,0:T(8,128)S(1)} %get-tuple-element.25.refs_3_.refs_9_, ...), custom_call_target="tpu_custom_call" | custom-call | tf_op jit(solution)/shard_map/pallas_call | solution.py:31
  17.1 4.0 %all-to-all-start.1 = ((f32[32,4,128]{2,1,0:T(4,128)}), f32[32,4,128]{2,1,0:T(4,128)S(1)}, u32[]{:S(2)}, u32[]{:S(2)}) async-start(f32[32,4,128]{2,1,0:T(4,128)} %get-tuple-element.28), calls=%async_computation.1 | async-start | bytes 131072 | tf_op jit(solution)/shard_map/all_to_all | solution.py:677
  21.1 0.2 shard_map.80.refs_2_.refs_5_
  21.3 0.3 shard_map.81
  21.7 0.3 collective-permute-start
  22.0 2.5 %collective-permute-start.1 = (f32[3,72,128]{2,1,0:T(8,128)S(1)}, f32[3,72,128]{2,1,0:T(8,128)S(1)}, u32[]{:S(2)}, u32[]{:S(2)}) collective-permute-start(f32[3,72,128]{2,1,0:T(8,128)S(1)} %get-tuple-element.31), channel_id=1, source_target_pairs={{4,8},{12,16},{20,24},{28,0},{8,4},{16,12},{24,20},{0,28},{5,9},{1... | collective-permute-start | bytes 331784 | tf_op jit(solution)/shard_map/ppermute | solution.py:733
  24.5 0.7 %collective-permute-start.3 = (f32[72,128]{1,0:T(8,128)S(1)}, f32[72,128]{1,0:T(8,128)S(1)}, u32[]{:S(2)}, u32[]{:S(2)}) collective-permute-start(f32[72,128]{1,0:T(8,128)S(1)} %shard_map.80.refs_2_.refs_5_), channel_id=1, source_target_pairs={{1,2},{2,1},{5,6},{6,5},{9,10},{10,9},{13,14},{14,13},{17,18},{18,... | collective-permute-start | bytes 110600 | tf_op jit(solution)/shard_map/ppermute | solution.py:735
  25.2 4.3 %collective-permute-start.2 = (f32[72,128]{1,0:T(8,128)S(1)}, f32[72,128]{1,0:T(8,128)S(1)}, u32[]{:S(2)}, u32[]{:S(2)}) collective-permute-start(f32[72,128]{1,0:T(8,128)S(1)} %shard_map.80.refs_2_.refs_5_), channel_id=1, source_target_pairs={{0,1},{1,0},{2,3},{3,2},{4,5},{5,4},{6,7},{7,6},{8,9},{9,8},{10,11... | collective-permute-start | bytes 110600 | tf_op jit(solution)/shard_map/ppermute | solution.py:734
  29.5 0.0 all-to-all-done.1.refs_0_
  29.5 0.9 %shard_map.82 = (f32[112,128]{1,0:T(8,128)S(1)}, f32[1,128]{1,0:T(1,128)S(1)}) custom-call(f32[32,4,128]{2,1,0:T(4,128)S(1)} %all-to-all-done.1.refs_0_), custom_call_target="tpu_custom_call" | custom-call | tf_op jit(solution)/shard_map/pallas_call | solution.py:31
  30.3 0.0 collective-permute-done.3.refs_4_
  30.3 1.1 %collective-permute-done.2.refs_3_ = f32[72,128]{1,0:T(8,128)S(1)} collective-permute-done((f32[72,128]{1,0:T(8,128)S(1)}, f32[72,128]{1,0:T(8,128)S(1)}, u32[]{:S(2)}, u32[]{:S(2)}) %collective-permute-start.2) | collective-permute-done | bytes 36896 | tf_op jit(solution)/shard_map/ppermute | solution.py:734
  31.4 0.0 collective-permute-done.refs_1_
  31.4 0.0 collective-permute-done.1.refs_2_
  31.4 2.2 %shard_map.83 = (f32[8,72,128]{2,1,0:T(8,128)S(1)}, f32[32,4,128]{2,1,0:T(4,128)}) custom-call(f32[32,4,128]{2,1,0:T(4,128)S(1)} %all-to-all-done.1.refs_0_, f32[3,72,128]{2,1,0:T(8,128)S(1)} %collective-permute-done.refs_1_, f32[3,72,128]{2,1,0:T(8,128)S(1)} %collective-permute-done.1.refs_2_, f32[72,128]{1,0:T(8,128)S(1)} %collective-permute-done.2.refs_3_, ...), custom_call_target="tpu_custom_call" | custom-call | tf_op jit(solution)/shard_map/pallas_call | solution.py:31
  33.6 0.4 shard_map.84
  34.0 0.1 collective-permute-start.4
  34.1 0.1 collective-permute-start.5
  34.1 3.8 %all-to-all-start.2 = ((f32[32,4,128]{2,1,0:T(4,128)}), f32[32,4,128]{2,1,0:T(4,128)S(1)}, u32[]{:S(2)}, u32[]{:S(2)}) async-start(f32[32,4,128]{2,1,0:T(4,128)} %get-tuple-element.34), calls=%async_computation.2 | async-start | bytes 131072 | tf_op jit(solution)/shard_map/all_to_all | solution.py:677
  38.0 1.6 %collective-permute-start.6 = (f32[2,72,128]{2,1,0:T(8,128)S(1)}, f32[2,72,128]{2,1,0:T(8,128)S(1)}, u32[]{:S(2)}, u32[]{:S(2)}) collective-permute-start(f32[2,72,128]{2,1,0:T(8,128)S(1)} %get-tuple-element.41), channel_id=1, source_target_pairs={{0,12},{4,8},{8,4},{12,0},{16,28},{20,24},{24,20},{28,16},{1,13},{... | collective-permute-start | bytes 221192 | tf_op jit(solution)/shard_map/ppermute | solution.py:763
  39.6 1.5 %collective-permute-start.7 = (f32[2,72,128]{2,1,0:T(8,128)S(1)}, f32[2,72,128]{2,1,0:T(8,128)S(1)}, u32[]{:S(2)}, u32[]{:S(2)}) collective-permute-start(f32[2,72,128]{2,1,0:T(8,128)S(1)} %get-tuple-element.42), channel_id=1, source_target_pairs={{0,16},{4,20},{8,24},{12,28},{16,0},{20,4},{24,8},{28,12},{1,17},{... | collective-permute-start | bytes 221192 | tf_op jit(solution)/shard_map/ppermute | solution.py:763
  41.0 0.2 collective-permute-start.8
  41.3 0.0 collective-permute-done.4.refs_6_
  41.3 1.5 %collective-permute-start.9 = (f32[2,72,128]{2,1,0:T(8,128)S(1)}, f32[2,72,128]{2,1,0:T(8,128)S(1)}, u32[]{:S(2)}, u32[]{:S(2)}) collective-permute-start(f32[2,72,128]{2,1,0:T(8,128)S(1)} %get-tuple-element.44), channel_id=1, source_target_pairs={{0,24},{4,28},{8,16},{12,20},{16,8},{20,12},{24,0},{28,4},{1,25},{... | collective-permute-start | bytes 221192 | tf_op jit(solution)/shard_map/ppermute | solution.py:763
  42.7 0.0 collective-permute-done.5.refs_7_
  42.7 1.2 %collective-permute-start.10 = (f32[2,72,128]{2,1,0:T(8,128)S(1)}, f32[2,72,128]{2,1,0:T(8,128)S(1)}, u32[]{:S(2)}, u32[]{:S(2)}) collective-permute-start(f32[2,72,128]{2,1,0:T(8,128)S(1)} %get-tuple-element.45), channel_id=1, source_target_pairs={{0,28},{4,24},{8,20},{12,16},{16,12},{20,8},{24,4},{28,0},{1,29},{... | collective-permute-start | bytes 221192 | tf_op jit(solution)/shard_map/ppermute | solution.py:763
  44.0 0.0 collective-permute-done.6.refs_8_
  44.0 0.8 %collective-permute-done.7.refs_9_ = f32[2,72,128]{2,1,0:T(8,128)S(1)} collective-permute-done((f32[2,72,128]{2,1,0:T(8,128)S(1)}, f32[2,72,128]{2,1,0:T(8,128)S(1)}, u32[]{:S(2)}, u32[]{:S(2)}) %collective-permute-start.7) | collective-permute-done | bytes 73760 | tf_op jit(solution)/shard_map/ppermute | solution.py:763
  44.8 4.2 %collective-permute-done.8.refs_10_ = f32[2,72,128]{2,1,0:T(8,128)S(1)} collective-permute-done((f32[2,72,128]{2,1,0:T(8,128)S(1)}, f32[2,72,128]{2,1,0:T(8,128)S(1)}, u32[]{:S(2)}, u32[]{:S(2)}) %collective-permute-start.8) | collective-permute-done | bytes 73760 | tf_op jit(solution)/shard_map/ppermute | solution.py:763
  48.9 0.0 collective-permute-done.9.refs_11_
  48.9 0.0 collective-permute-done.10.refs_12_
  49.0 0.0 all-to-all-done.2.refs_0_
  49.0 2.0 %shard_map.85 = (f32[560,128]{1,0:T(8,128)}, f32[560,128]{1,0:T(8,128)}) custom-call(f32[32,4,128]{2,1,0:T(4,128)S(1)} %all-to-all-done.2.refs_0_, f32[112,128]{1,0:T(8,128)S(1)} %get-tuple-element.35.refs_1_, f32[1,128]{1,0:T(1,128)S(1)} %get-tuple-element.33.refs_10_.refs_2_, f32[8,72,128]{2,1,0:T(8,128)S(1)} %get-tuple-element.29.refs_0_.refs_6_.refs_3_, ...), custom_call_target="tpu_custom_call" | custom-call | tf_op jit(solution)/shard_map/pallas_call | solution.py:31
  (4 shorter events, 0.1 us)
Async XLA Ops:
  0.6 1.0 %copy-start.2 = (f32[70,8,128]{2,1,0:T(8,128)S(1)}, f32[70,8,128]{2,1,0:T(8,128)}, u32[]{:S(2)}) copy-start(f32[70,8,128]{2,1,0:T(8,128)} %param.9) | copy-start | bytes 860164
  2.6 5.3 %copy-start.3 = (f32[70]{0:T(128)S(1)}, f32[70]{0:T(128)}, u32[]{:S(2)}) copy-start(f32[70]{0:T(128)} %param.11) | copy-start | bytes 844
  2.6 5.3 %copy-start.4 = (f32[70]{0:T(128)S(1)}, f32[70]{0:T(128)}, u32[]{:S(2)}) copy-start(f32[70]{0:T(128)} %param.10) | copy-start | bytes 844
  2.6 12.6 %copy-start = (f32[70,8,128]{2,1,0:T(8,128)S(1)}, f32[70,8,128]{2,1,0:T(8,128)}, u32[]{:S(2)}) copy-start(f32[70,8,128]{2,1,0:T(8,128)} %param.7) | copy-start | bytes 860164
  2.6 12.6 %copy-start.1 = (f32[70,8,128]{2,1,0:T(8,128)S(1)}, f32[70,8,128]{2,1,0:T(8,128)}, u32[]{:S(2)}) copy-start(f32[70,8,128]{2,1,0:T(8,128)} %param.6) | copy-start | bytes 860164
  2.6 12.6 %all-to-all-start = ((f32[8,72,128]{2,1,0:T(8,128)}), f32[8,72,128]{2,1,0:T(8,128)S(1)}, u32[]{:S(2)}, u32[]{:S(2)}) async-start(f32[8,72,128]{2,1,0:T(8,128)} %shard_map.77), calls=%async_computation | async-start | bytes 589824 | tf_op jit(solution)/shard_map/all_to_all | solution.py:674
  8.0 0.7 %copy-start.5 = (f32[69]{0:T(128)S(1)}, f32[69]{0:T(128)}, u32[]{:S(2)}) copy-start(f32[69]{0:T(128)} %param.8) | copy-start | bytes 832
  17.1 12.3 %all-to-all-start.1 = ((f32[32,4,128]{2,1,0:T(4,128)}), f32[32,4,128]{2,1,0:T(4,128)S(1)}, u32[]{:S(2)}, u32[]{:S(2)}) async-start(f32[32,4,128]{2,1,0:T(4,128)} %get-tuple-element.28), calls=%async_computation.1 | async-start | bytes 131072 | tf_op jit(solution)/shard_map/all_to_all | solution.py:677
  21.7 9.7 %collective-permute-start = (f32[3,72,128]{2,1,0:T(8,128)S(1)}, f32[3,72,128]{2,1,0:T(8,128)S(1)}, u32[]{:S(2)}, u32[]{:S(2)}) collective-permute-start(f32[3,72,128]{2,1,0:T(8,128)S(1)} %get-tuple-element.30), channel_id=1, source_target_pairs={{0,4},{4,0},{8,12},{12,8},{16,20},{20,16},{24,28},{28,24},{1,5},{5... | collective-permute-start | bytes 331784 | tf_op jit(solution)/shard_map/ppermute | solution.py:732
  22.0 9.4 %collective-permute-start.1 = (f32[3,72,128]{2,1,0:T(8,128)S(1)}, f32[3,72,128]{2,1,0:T(8,128)S(1)}, u32[]{:S(2)}, u32[]{:S(2)}) collective-permute-start(f32[3,72,128]{2,1,0:T(8,128)S(1)} %get-tuple-element.31), channel_id=1, source_target_pairs={{4,8},{12,16},{20,24},{28,0},{8,4},{16,12},{24,20},{0,28},{5,9},{1... | collective-permute-start | bytes 331784 | tf_op jit(solution)/shard_map/ppermute | solution.py:733
  24.5 5.8 %collective-permute-start.3 = (f32[72,128]{1,0:T(8,128)S(1)}, f32[72,128]{1,0:T(8,128)S(1)}, u32[]{:S(2)}, u32[]{:S(2)}) collective-permute-start(f32[72,128]{1,0:T(8,128)S(1)} %shard_map.80.refs_2_.refs_5_), channel_id=1, source_target_pairs={{1,2},{2,1},{5,6},{6,5},{9,10},{10,9},{13,14},{14,13},{17,18},{18,... | collective-permute-start | bytes 110600 | tf_op jit(solution)/shard_map/ppermute | solution.py:735
  25.2 6.2 %collective-permute-start.2 = (f32[72,128]{1,0:T(8,128)S(1)}, f32[72,128]{1,0:T(8,128)S(1)}, u32[]{:S(2)}, u32[]{:S(2)}) collective-permute-start(f32[72,128]{1,0:T(8,128)S(1)} %shard_map.80.refs_2_.refs_5_), channel_id=1, source_target_pairs={{0,1},{1,0},{2,3},{3,2},{4,5},{5,4},{6,7},{7,6},{8,9},{9,8},{10,11... | collective-permute-start | bytes 110600 | tf_op jit(solution)/shard_map/ppermute | solution.py:734
  34.0 7.3 %collective-permute-start.4 = (f32[2,72,128]{2,1,0:T(8,128)S(1)}, f32[2,72,128]{2,1,0:T(8,128)S(1)}, u32[]{:S(2)}, u32[]{:S(2)}) collective-permute-start(f32[2,72,128]{2,1,0:T(8,128)S(1)} %get-tuple-element.39), channel_id=1, source_target_pairs={{0,4},{4,0},{8,12},{12,8},{16,20},{20,16},{24,28},{28,24},{1,5},{5... | collective-permute-start | bytes 221192 | tf_op jit(solution)/shard_map/ppermute | solution.py:763
  34.1 8.7 %collective-permute-start.5 = (f32[2,72,128]{2,1,0:T(8,128)S(1)}, f32[2,72,128]{2,1,0:T(8,128)S(1)}, u32[]{:S(2)}, u32[]{:S(2)}) collective-permute-start(f32[2,72,128]{2,1,0:T(8,128)S(1)} %get-tuple-element.40), channel_id=1, source_target_pairs={{0,8},{4,12},{8,0},{12,4},{16,24},{20,28},{24,16},{28,20},{1,9},{5... | collective-permute-start | bytes 221192 | tf_op jit(solution)/shard_map/ppermute | solution.py:763
  34.1 14.8 %all-to-all-start.2 = ((f32[32,4,128]{2,1,0:T(4,128)}), f32[32,4,128]{2,1,0:T(4,128)S(1)}, u32[]{:S(2)}, u32[]{:S(2)}) async-start(f32[32,4,128]{2,1,0:T(4,128)} %get-tuple-element.34), calls=%async_computation.2 | async-start | bytes 131072 | tf_op jit(solution)/shard_map/all_to_all | solution.py:677
  38.0 6.0 %collective-permute-start.6 = (f32[2,72,128]{2,1,0:T(8,128)S(1)}, f32[2,72,128]{2,1,0:T(8,128)S(1)}, u32[]{:S(2)}, u32[]{:S(2)}) collective-permute-start(f32[2,72,128]{2,1,0:T(8,128)S(1)} %get-tuple-element.41), channel_id=1, source_target_pairs={{0,12},{4,8},{8,4},{12,0},{16,28},{20,24},{24,20},{28,16},{1,13},{... | collective-permute-start | bytes 221192 | tf_op jit(solution)/shard_map/ppermute | solution.py:763
  39.6 5.2 %collective-permute-start.7 = (f32[2,72,128]{2,1,0:T(8,128)S(1)}, f32[2,72,128]{2,1,0:T(8,128)S(1)}, u32[]{:S(2)}, u32[]{:S(2)}) collective-permute-start(f32[2,72,128]{2,1,0:T(8,128)S(1)} %get-tuple-element.42), channel_id=1, source_target_pairs={{0,16},{4,20},{8,24},{12,28},{16,0},{20,4},{24,8},{28,12},{1,17},{... | collective-permute-start | bytes 221192 | tf_op jit(solution)/shard_map/ppermute | solution.py:763
  41.0 7.9 %collective-permute-start.8 = (f32[2,72,128]{2,1,0:T(8,128)S(1)}, f32[2,72,128]{2,1,0:T(8,128)S(1)}, u32[]{:S(2)}, u32[]{:S(2)}) collective-permute-start(f32[2,72,128]{2,1,0:T(8,128)S(1)} %get-tuple-element.43), channel_id=1, source_target_pairs={{0,20},{4,16},{8,28},{12,24},{16,4},{20,0},{24,12},{28,8},{1,21},{... | collective-permute-start | bytes 221192 | tf_op jit(solution)/shard_map/ppermute | solution.py:763
  41.3 7.7 %collective-permute-start.9 = (f32[2,72,128]{2,1,0:T(8,128)S(1)}, f32[2,72,128]{2,1,0:T(8,128)S(1)}, u32[]{:S(2)}, u32[]{:S(2)}) collective-permute-start(f32[2,72,128]{2,1,0:T(8,128)S(1)} %get-tuple-element.44), channel_id=1, source_target_pairs={{0,24},{4,28},{8,16},{12,20},{16,8},{20,12},{24,0},{28,4},{1,25},{... | collective-permute-start | bytes 221192 | tf_op jit(solution)/shard_map/ppermute | solution.py:763
  42.7 6.2 %collective-permute-start.10 = (f32[2,72,128]{2,1,0:T(8,128)S(1)}, f32[2,72,128]{2,1,0:T(8,128)S(1)}, u32[]{:S(2)}, u32[]{:S(2)}) collective-permute-start(f32[2,72,128]{2,1,0:T(8,128)S(1)} %get-tuple-element.45), channel_id=1, source_target_pairs={{0,28},{4,24},{8,20},{12,16},{16,12},{20,8},{24,4},{28,0},{1,29},{... | collective-permute-start | bytes 221192 | tf_op jit(solution)/shard_map/ppermute | solution.py:763

commit v3 on v2

--- a/solution.py
+++ b/solution.py
@@ -10,8 +10,9 @@
 F32 = jnp.float32
 HIGHEST = lax.Precision.HIGHEST
 MESSAGE_ROWS = 4
-LAST_ROWS = 4
+LAST_ROWS = 8
 VMEM = pl.BlockSpec(memory_space=pltpu.VMEM)
+HBM = pl.BlockSpec(memory_space=pltpu.HBM)
 
 
 def iota(shape, dim):
@@ -27,13 +28,14 @@
     return jnp.sum(value, axis=(0, 1), keepdims=True)
 
 
-def call(kernel, outs, *args, scratch=()):
+def call(kernel, outs, *args, scratch=(), copies=0):
     return pl.pallas_call(
         kernel,
         out_shape=[jax.ShapeDtypeStruct(shape, F32) for shape in outs],
-        in_specs=[VMEM] * len(args),
+        in_specs=[HBM if copies else VMEM] * len(args),
         out_specs=[VMEM] * len(outs),
-        scratch_shapes=[pltpu.VMEM(shape, F32) for shape in scratch],
+        scratch_shapes=[pltpu.VMEM(shape, F32) for shape in scratch]
+        + [pltpu.SemaphoreType.DMA((copies,))] * bool(copies),
         compiler_params=pltpu.CompilerParams(vmem_limit_bytes=32 * 1024 * 1024),
     )(*args)
 
@@ -70,20 +72,37 @@
     return tiles
 
 
-def pack_kernel(levels, x_ref, out_ref):
-    points, padded, _ = out_ref.shape
+def pack_kernel(levels, x_ref, *out_refs):
+    *out_refs, packed_ref = out_refs
+    points, padded, _ = packed_ref.shape
     for s, tile in enumerate(swap_groups(load_columns(x_ref, points, levels, padded))):
-        out_ref[s] = tile
-
-
-def tables_kernel(levels, rows_ref, inverse_ref, matrix_ref, absorbed_ref):
+        packed_ref[s] = tile
+    tile = lax.axis_index("tile")
+    for k, out_ref in enumerate(out_refs):
+        out_ref[...] = packed_ref[tile ^ k]
+
+
+def tables_kernel(levels, *refs):
+    *vector_refs, inverse_ref, matrix_ref, absorbed_ref = refs[:6]
+    *buffer_refs, sems = refs[6:]
+    copies = [
+        pltpu.make_async_copy(vector_ref, buffer_ref, sems.at[n])
+        for n, (vector_ref, buffer_ref) in enumerate(zip(vector_refs, buffer_refs))
+    ]
+    for copy in copies:
+        copy.start()
+    for copy in copies:
+        copy.wait()
     shape = inverse_ref.shape
     sub, lane = iota(shape, 0), iota(shape, 1)
 
     def column(row, mask):
         return jnp.broadcast_to(jnp.sum(jnp.where(mask, row, 0.0), axis=1, keepdims=True), shape)
 
-    link, thermal, solar = rows_ref[0:1, :], rows_ref[1:2, :], rows_ref[2:3, :]
+    link, thermal, solar = [
+        jnp.concatenate([ref[...], jnp.zeros((1, shape[1] - ref.shape[1]), F32)], axis=1)
+        for ref in buffer_refs
+    ]
     lower = column(link, lane == sub - 1)
     upper = column(link, lane == sub)
     diagonal = 4.0 + lower + upper
@@ -150,51 +169,76 @@
     return parts[0]
 
 
-def smooth_kernel(
+def dot(matrix, tiles):
+    across = tiles[0].shape[1]
+    field = jnp.concatenate(tiles, axis=1)
+    field = jnp.dot(matrix, field, precision=HIGHEST, preferred_element_type=F32)
+    return [field[:, i * across : (i + 1) * across] for i in range(len(tiles))]
+
+
+def prepare_kernel(
     levels,
-    tiles,
-    groups,
-    swap,
-    kelvin_ref,
     forcing_ref,
     weight_ref,
     inverse_ref,
     matrix_ref,
     absorbed_ref,
     cosine_ref,
-    residual_ref,
-    smooth_ref,
-    message_ref,
+    forced_ref,
+    weight_out_ref,
+    base_ref,
+    matrices_ref,
+    rows_ref,
+    unit_ref,
 ):
+    points, padded, across = forced_ref.shape
+    inverse = inverse_ref[:, :padded]
+    sun = absorbed_ref[...] * cosine_ref[...]
+    forced = [tile + sun for tile in load_columns(forcing_ref, points, levels, padded)]
+    for i, tile in enumerate(dot(inverse, forced)):
+        forced_ref[i] = forced[i]
+        base_ref[i] = tile
+    weight = load_columns(weight_ref, points, levels, padded)
+    for i, tile in enumerate(weight):
+        weight_out_ref[i] = tile
+    matrices_ref[0:padded] = matrix_ref[...]
+    matrices_ref[padded:] = dot(inverse, [matrix_ref[...]])[0]
+    unit_ref[...] = jnp.broadcast_to(
+        jnp.sum(inverse_ref[...], axis=1, keepdims=True), unit_ref.shape
+    )
+    rows_ref[0:8] = add_all([fold(tile) for tile in weight])
+    solar = jnp.sum(fold(sun), axis=0, keepdims=True)
+    rows_ref[8:16] = jnp.broadcast_to(solar, (8, across))
+
+
+def smooth_kernel(levels, tiles, groups, swap, *refs):
+    *kelvin_refs, forced_ref, weight_ref, base_ref, matrices_ref, rows_ref, unit_ref = refs[: -3 - swap]
+    residual_ref, smooth_ref, message_ref = refs[-3 - swap : len(refs) - swap]
     points, padded, across = residual_ref.shape
-    kelvin = [kelvin_ref[i] for i in range(points)]
     if swap:
-        kelvin = swap_groups(kelvin)
+        scratch_ref = refs[-1]
+        tile = lax.axis_index("tile")
+        for k, part_ref in enumerate(kelvin_refs):
+            scratch_ref[tile ^ k] = part_ref[...]
+        kelvin = swap_groups([scratch_ref[i] for i in range(points)])
+    else:
+        kelvin = [kelvin_refs[0][i] for i in range(points)]
     squares = [tile * tile for tile in kelvin]
-    emission = jnp.concatenate([tile * tile for tile in squares], axis=1)
-    heating = jnp.dot(matrix_ref[:, :padded], emission, precision=HIGHEST, preferred_element_type=F32)
-    sun = absorbed_ref[...] * cosine_ref[...]
-    forcing = load_columns(forcing_ref, points, levels, padded)
-    weight = load_columns(weight_ref, points, levels, padded)
-    real = iota(sun.shape, 0) < levels
-    residual = []
+    both = dot(matrices_ref[:, :padded], [tile * tile for tile in squares])
+    real = iota((padded, across), 0) < levels
+    solar, unit = rows_ref[8:9, :], unit_ref[...]
+    residual, smooth = [], []
     for i in range(points):
-        heat = heating[:, i * across : (i + 1) * across] + sun
-        mean = jnp.sum(fold(heat), axis=0, keepdims=True) * (1.0 / levels)
-        residual.append(forcing[i] + jnp.where(real, heat - mean, 0.0))
-    smooth = jnp.dot(
-        inverse_ref[:, :padded],
-        jnp.concatenate(residual, axis=1),
-        precision=HIGHEST,
-        preferred_element_type=F32,
-    )
-    smooth = [smooth[:, i * across : (i + 1) * across] for i in range(points)]
-    for i in range(points):
+        heat = both[i][:padded]
+        mean = (jnp.sum(fold(heat), axis=0, keepdims=True) + solar) * (1.0 / levels)
+        residual.append(forced_ref[i] + jnp.where(real, heat - mean, 0.0))
+        smooth.append(base_ref[i] + (both[i][padded:] - unit * mean))
         residual_ref[i] = residual[i]
         smooth_ref[i] = smooth[i]
+    weight = [weight_ref[i] for i in range(points)]
     folded = [fold(tile) for tile in smooth]
     loss = add_all([fold(a * b) for a, b in zip(smooth, weight)])
-    mass = add_all([fold(tile) for tile in weight])
+    mass = rows_ref[0:8, :]
     every = add_all(folded)
     lane = iota(every.shape, 1)
     scalars = scalars_row(
@@ -219,31 +263,26 @@
         message_ref[pl.ds(place, 1), 0, :] = rows[corner : corner + 1] + scalars
 
 
-def rim_kernel(levels, smooth_ref, weight_ref, rim_ref):
+def rim_kernel(smooth_ref, weight_ref, rim_ref):
     points, padded, across = smooth_ref.shape
-    weight = load_columns(weight_ref, points, levels, padded)
     stride = across // points
     lane = iota((padded, across), 1)
     rim = jnp.zeros((padded, across), F32)
     for i in range(points):
         place = (lane - stride * i + 2) & (across - 1)
         rim = jnp.where(place < 4, turn(smooth_ref[i], stride * i), rim)
-        rim = jnp.where((place == 5) | (place == 6), turn(weight[i], stride * i + 4), rim)
+        rim = jnp.where((place == 5) | (place == 6), turn(weight_ref[i], stride * i + 4), rim)
     rim_ref[...] = rim
 
 
-def side_kernel(levels, swap, smooth_ref, weight_ref, _, inner_ref, outer_ref, *packed_ref):
-    points, padded, _ = smooth_ref.shape
+def side_kernel(swap, smooth_ref, weight_ref, _, inner_ref, outer_ref, *packed_ref):
+    points = smooth_ref.shape[0]
     even = lax.rem(lax.axis_index("tile"), 2) == 0
     for j, place in enumerate((0, 1)):
         west, east = smooth_ref[place], smooth_ref[points - 2 + place]
         inner_ref[j] = jnp.where(even, east, west)
         outer_ref[j] = jnp.where(even, west, east)
-    extra = jnp.zeros((padded - levels, inner_ref.shape[2]), F32)
-    west, east = [
-        jnp.concatenate([weight_ref[pl.ds(i, levels, stride=points), :], extra], axis=0)
-        for i in (0, points - 1)
-    ]
+    west, east = weight_ref[0], weight_ref[points - 1]
     inner_ref[2] = jnp.where(even, east, west)
     outer_ref[2] = jnp.where(even, west, east)
     if swap:
@@ -477,7 +516,7 @@
         high = jnp.where(final, jnp.where(at_north, tile, high), turn(tile, -1))
         return low + high
 
-    weight = load_columns(weight_ref, points, levels, padded)
+    weight = [weight_ref[i] for i in range(points)]
     from_west = [jnp.where(even_tile, outer_ref[j], inner_ref[j]) for j in range(3)]
     from_east = [jnp.where(even_tile, inner_ref[j], outer_ref[j]) for j in range(3)]
     weight = from_west[2:] + weight + from_east[2:]
@@ -523,13 +562,7 @@
     is_south, is_north = inside == stride - 1, inside == 0
     ring = jnp.where(is_south, ring_south, jnp.where(is_north, ring_north, 0.0))
     ring_field = jnp.where(is_south, from_south, from_north)
-    second = jnp.dot(
-        inverse_ref[:, :padded],
-        jnp.concatenate(image + [ring], axis=1),
-        precision=HIGHEST,
-        preferred_element_type=F32,
-    )
-    second = [second[:, i * across : (i + 1) * across] for i in range(points + 3)]
+    second = dot(inverse_ref[:, :padded], image + [ring])
     ring = ring_field - second.pop()
     second = [field[i + 1] - tile for i, tile in enumerate(second)]
 
@@ -592,12 +625,9 @@
     coarse_ref,
     smooth_ref,
     second_ref,
-    *refs,
+    field_ref,
+    other_ref,
 ):
-    if swap:
-        *part_refs, field_ref, state_ref, scratch_ref = refs
-    else:
-        field_ref, state_ref = refs
     points, padded, across = smooth_ref.shape
     blocks = tiles * groups
     rows = by_block(received_ref[:, 0, :])
@@ -636,7 +666,7 @@
     kappa = (rv - alpha * qv) / (vv - beta * qv)
     scale = alpha - kappa * beta
     constant = scale * coarse_ref[...] + kappa * coarse
-    others = points if swap else 1
+    others = tiles if swap else 1
     parts = [jnp.where(lane == (tile ^ k) * groups + group, constant, 0.0) for k in range(others)]
     parts += [jnp.zeros_like(coarse)] * (-others % 8)
     shifts = jnp.sum(jnp.concatenate(parts, axis=0), axis=1, keepdims=True)
@@ -644,13 +674,22 @@
     result = [scale * smooth_ref[i] + (kappa * second_ref[i] + shifts[0]) for i in range(points)]
     store_columns(field_ref, result, levels)
     if swap:
-        for k, part_ref in enumerate(part_refs):
-            scratch_ref[tile ^ k] = scale * part_ref[0] + (kappa * part_ref[1] + shifts[k])
-        result = swap_groups([scratch_ref[s] for s in range(points)])
-        store_columns(state_ref, result, levels)
+        rows = jnp.concatenate([scale, kappa] + shifts, axis=0)
+        rows = jnp.concatenate([rows, jnp.zeros((other_ref.shape[0] - rows.shape[0], 1), F32)], axis=0)
+        other_ref[...] = jnp.broadcast_to(rows, other_ref.shape)
     else:
         for i in range(points):
-            state_ref[i] = result[i]
+            other_ref[i] = result[i]
+
+
+def state_kernel(levels, scalars_ref, *refs):
+    *part_refs, state_ref, scratch_ref = refs
+    tile = lax.axis_index("tile")
+    scale, kappa = scalars_ref[0:1, :], scalars_ref[1:2, :]
+    for k, part_ref in enumerate(part_refs):
+        shift = scalars_ref[2 + k : 3 + k, :]
+        scratch_ref[tile ^ k] = scale * part_ref[0] + (kappa * part_ref[1] + shift)
+    store_columns(state_ref, swap_groups([scratch_ref[s] for s in range(len(part_refs))]), levels)
 
 
 def per_device(
@@ -681,20 +720,23 @@
 
     kelvin = previous_kelvin_field
     if swap:
-        (kelvin,) = call(
-            part(pack_kernel, levels), [(points, padded, across)], kelvin.reshape(flat)
-        )
-        kelvin = to_tiles(kelvin)
+        kelvin = list(call(
+            part(pack_kernel, levels), [(padded, across)] * tiles, kelvin.reshape(flat), scratch=[(points, padded, across)]
+        ))
+        for k in range(1, tiles):
+            kelvin[k] = lax.ppermute(kelvin[k], "tile", [(i, i ^ k) for i in range(tiles)])
     else:
         kelvin = kelvin.reshape(levels, points, tiles, width).transpose(2, 1, 0, 3)
         kelvin = to_tiles(kelvin).transpose(1, 2, 0, 3).reshape(points, levels, across)
-        kelvin = jnp.pad(kelvin, ((0, 0), (0, padded - levels), (0, 0)))
-
-    vectors = (layer_link_factor, longwave_opacity, shortwave_opacity)
-    rows = jnp.stack([jnp.pad(v, (0, across - v.shape[0])) for v in vectors])
-    rows = jnp.pad(rows, ((0, 8 - len(vectors)), (0, 0)))
+        kelvin = [jnp.pad(kelvin, ((0, 0), (0, padded - levels), (0, 0)))]
+
+    vectors = [v[None, :] for v in (layer_link_factor, longwave_opacity, shortwave_opacity)]
     inverse, matrix, absorbed = call(
-        part(tables_kernel, levels), [(padded, across)] * 3, rows
+        part(tables_kernel, levels),
+        [(padded, across)] * 3,
+        *vectors,
+        scratch=[v.shape for v in vectors],
+        copies=len(vectors),
     )
     global_row = lax.axis_index("grp") * across + jnp.arange(across)
     latitude = ((global_row.astype(F32) + 0.5) / (across * groups) - 0.5) * (math.pi / 2)
@@ -703,11 +745,9 @@
     forcing = forcing_vector.reshape(flat)
     weights = shift_weights.reshape(flat)
     field = (points, padded, across)
-    message = (blocks, MESSAGE_ROWS, across)
-    residual, smooth, message = call(
-        part(smooth_kernel, levels, tiles, groups, swap),
-        [field, field, message],
-        kelvin,
+    forced, weights, *prepared = call(
+        part(prepare_kernel, levels),
+        [field, field, field, (2 * padded, across), (16, across), (padded, across)],
         forcing,
         weights,
         inverse,
@@ -715,10 +755,19 @@
         absorbed,
         cosine,
     )
+    prepared = [forced, weights, *prepared]
+    message = (blocks, MESSAGE_ROWS, across)
+    residual, smooth, message = call(
+        part(smooth_kernel, levels, tiles, groups, swap),
+        [field, field, message],
+        *kelvin,
+        *prepared,
+        scratch=[field] * swap,
+    )
     tile, side = (padded, across), (3, padded, across)
-    (rim,) = call(part(rim_kernel, levels), [tile], smooth, weights)
+    (rim,) = call(rim_kernel, [tile], smooth, weights)
     inner, outer, *packed = call(
-        part(side_kernel, levels, swap), [side, side] + [field] * swap, smooth, weights, rim
+        part(side_kernel, swap), [side, side] + [field] * swap, smooth, weights, rim
     )
     received = gather(message)
 
@@ -763,15 +812,15 @@
             parts[k] = lax.ppermute(parts[k], "tile", [(i, i ^ k) for i in range(tiles)])
     solution_field, state = call(
         part(final_kernel, levels, tiles, groups, swap),
-        [flat, flat if swap else field],
+        [flat, (-(-(tiles + 2) // 8) * 8, across) if swap else field],
         received,
         steps,
         coarse,
         smooth,
         second,
-        *parts,
-        scratch=[field] * swap,
-    )
+    )
+    if swap:
+        (state,) = call(part(state_kernel, levels), [flat], state, *parts, scratch=[field])
     if not swap:
         state = state[:, :levels].reshape(points, levels, tiles, width).transpose(2, 1, 0, 3)
         state = to_tiles(state).transpose(2, 1, 0, 3)

time: 51.3 us -> 48.6 us (0.947)
  waiting for transfers between devices: 12.2 us -> 5.65 us
  starting transfers between devices: 27 us -> 29.5 us
  local copies, waits for them, and re-layouts: 1.61 us -> 2.58 us
    ppermute x0 -> x7, starting transfers between devices: none -> 7.65 us  [per_device(): lax.ppermute(kelvin[k], 'tile', [(i, i ^ k) for i in range(tiles)])]
    all_to_all x1 -> x0, waiting for transfers between devices: 6.18 us -> none  [to_tiles(): lax.all_to_all(value, 'tile', split_axis=0, concat_axis=0, tiled=True)]
    all_to_all x1 -> x0, starting transfers between devices: 5.31 us -> none  [to_tiles(): lax.all_to_all(value, 'tile', split_axis=0, concat_axis=0, tiled=True)]
    ppermute x7, waiting for transfers between devices: 4.98 us -> 1.81 us  [per_device(): lax.ppermute(parts[k], 'tile', [(i, i ^ k) for i in range(tiles)])]
    ppermute x0 -> x7, waiting for transfers between devices: none -> 1.58 us  [per_device(): lax.ppermute(kelvin[k], 'tile', [(i, i ^ k) for i in range(tiles)])]
    all_to_all x2, waiting for transfers between devices: 0.01 us -> 1.18 us  [gather(): lax.all_to_all(value, ('tile', 'grp'), split_axis=0, concat_axis=0, tiled...]
    unnamed x12, local copies, waits for them, and re-layouts: 1.6 us -> 2.58 us
    ppermute x7, starting transfers between devices: 6.14 us -> 6.96 us  [per_device(): lax.ppermute(parts[k], 'tile', [(i, i ^ k) for i in range(tiles)])]
  transfers between devices with their start and end apart: 14 -> 20, of which waited for: 4 -> 5; matrix products, arithmetic and copies ran while one was open for 0% -> 0% of each run, Pallas kernels for 3% -> 9%
where the time goes in v3:
time: 48.6 us; the launch traced here: 48.3 us
  starting transfers between devices  29.5 us (61%)
  Pallas kernels  9.69 us (20%)
  waiting for transfers between devices  5.65 us (12%)
  local copies, waits for them, and re-layouts  2.58 us (5%)
  between operations  0.79 us (2%)
    pallas_call x11, Pallas kernels, call(): pl.pallas_call(kernel, out_shape=[jax.ShapeDtypeStruct(shape, F32) for sh...  9.69 us
    ppermute x7, starting transfers between devices, per_device(): lax.ppermute(kelvin[k], 'tile', [(i, i ^ k) for i in range(tiles)])  7.65 us
    all_to_all x2, starting transfers between devices, gather(): lax.all_to_all(value, ('tile', 'grp'), split_axis=0, concat_axis=0, tiled...  7.13 us
    ppermute x7, starting transfers between devices, per_device(): lax.ppermute(parts[k], 'tile', [(i, i ^ k) for i in range(tiles)])  6.96 us
    ppermute x1, starting transfers between devices, per_device(): low = lax.ppermute(rim, 'grp', inner_pairs(groups))  4.27 us
    unnamed x12, local copies, waits for them, and re-layouts  2.58 us
    ppermute x1, starting transfers between devices, per_device(): outer = lax.ppermute(outer, 'tile', outer_pairs(tiles, True))  2.53 us
    ppermute x7, waiting for transfers between devices, per_device(): lax.ppermute(parts[k], 'tile', [(i, i ^ k) for i in range(tiles)])  1.81 us
  transfers between devices with their start and end apart: 20, of which 5 were waited for; matrix products, arithmetic and copies ran while one was open for 0% of the time, Pallas kernels for 9%

profile of v3, /device:TPU:0, one launch (start us, length us, event | category | flops | bytes accessed | tf_op | source)
XLA Modules:
  0.0 48.3 jit_solution(8121686931825353995)
XLA Ops:
  0.6 0.0 copy-start
  0.6 0.9 %copy-done = f32[70,8,128]{2,1,0:T(8,128)S(1)} copy-done((f32[70,8,128]{2,1,0:T(8,128)S(1)}, f32[70,8,128]{2,1,0:T(8,128)}, u32[]{:S(2)}) %copy-start) | copy-done | bytes 286744
  1.6 0.0 copy-start.1
  1.6 0.4 shard_map.77
  2.0 0.5 %collective-permute-start = (f32[72,128]{1,0:T(8,128)S(1)}, f32[72,128]{1,0:T(8,128)S(1)}, u32[]{:S(2)}, u32[]{:S(2)}) collective-permute-start(f32[72,128]{1,0:T(8,128)S(1)} %get-tuple-element.40), channel_id=1, source_target_pairs={{0,4},{4,0},{8,12},{12,8},{16,20},{20,16},{24,28},{28,24},{1,5},{5... | collective-permute-start | bytes 110600 | tf_op jit(solution)/shard_map/ppermute | solution.py:727
  2.5 2.6 %collective-permute-start.1 = (f32[72,128]{1,0:T(8,128)S(1)}, f32[72,128]{1,0:T(8,128)S(1)}, u32[]{:S(2)}, u32[]{:S(2)}) collective-permute-start(f32[72,128]{1,0:T(8,128)S(1)} %get-tuple-element.41), channel_id=1, source_target_pairs={{0,8},{4,12},{8,0},{12,4},{16,24},{20,28},{24,16},{28,20},{1,9},{5... | collective-permute-start | bytes 110600 | tf_op jit(solution)/shard_map/ppermute | solution.py:727
  5.0 0.1 collective-permute-start.2
  5.1 1.8 %collective-permute-start.3 = (f32[72,128]{1,0:T(8,128)S(1)}, f32[72,128]{1,0:T(8,128)S(1)}, u32[]{:S(2)}, u32[]{:S(2)}) collective-permute-start(f32[72,128]{1,0:T(8,128)S(1)} %get-tuple-element.43), channel_id=1, source_target_pairs={{0,16},{4,20},{8,24},{12,28},{16,0},{20,4},{24,8},{28,12},{1,17},{... | collective-permute-start | bytes 110600 | tf_op jit(solution)/shard_map/ppermute | solution.py:727
  6.9 0.0 collective-permute-start.4
  6.9 0.0 collective-permute-done.refs_1_
  6.9 2.6 %collective-permute-start.5 = (f32[72,128]{1,0:T(8,128)S(1)}, f32[72,128]{1,0:T(8,128)S(1)}, u32[]{:S(2)}, u32[]{:S(2)}) collective-permute-start(f32[72,128]{1,0:T(8,128)S(1)} %get-tuple-element.45), channel_id=1, source_target_pairs={{0,24},{4,28},{8,16},{12,20},{16,8},{20,12},{24,0},{28,4},{1,25},{... | collective-permute-start | bytes 110600 | tf_op jit(solution)/shard_map/ppermute | solution.py:727
  9.5 0.0 collective-permute-done.1.refs_2_
  9.5 0.1 collective-permute-start.6
  9.7 0.0 copy-start.3
  9.7 0.0 copy-start.4
  9.7 0.0 copy-start.5
  9.7 0.6 %copy-done.3 = f32[69]{0:T(128)S(1)} copy-done((f32[69]{0:T(128)S(1)}, f32[69]{0:T(128)}, u32[]{:S(2)}) %copy-start.3) | copy-done | bytes 300
  10.3 0.0 copy-done.4
  10.3 0.0 copy-done.5
  10.4 0.4 shard_map.78
  10.8 0.0 copy-done.1
  10.8 0.0 copy-start.2
  10.8 0.9 %copy-done.2 = f32[70,8,128]{2,1,0:T(8,128)S(1)} copy-done((f32[70,8,128]{2,1,0:T(8,128)S(1)}, f32[70,8,128]{2,1,0:T(8,128)}, u32[]{:S(2)}) %copy-start.2) | copy-done | bytes 286744
  11.7 0.5 %shard_map.79 = (f32[8,72,128]{2,1,0:T(8,128)S(1)}, f32[8,72,128]{2,1,0:T(8,128)S(1)}, f32[8,72,128]{2,1,0:T(8,128)S(1)}, f32[144,128]{1,0:T(8,128)S(1)}, f32[16,128]{1,0:T(8,128)S(1)}, /*index=5*/f32[72,128]{1,0:T(8,128)S(1)}) custom-call(f32[560,128]{1,0:T(8,128)S(1)} %bitcast.9, f32[560,128]{1,0:T(8,128)S(1)} %bitcast.10, ...), custom_call_target="tpu_custom_call" | custom-call | tf_op jit(solution)/shard_map/pallas_call | solution.py:32
  12.2 0.0 collective-permute-done.2.refs_3_
  12.2 0.0 collective-permute-done.3.refs_4_
  12.2 0.0 collective-permute-done.4.refs_5_
  12.3 0.0 collective-permute-done.5.refs_6_
  12.3 1.6 %collective-permute-done.6.refs_7_ = f32[72,128]{1,0:T(8,128)S(1)} collective-permute-done((f32[72,128]{1,0:T(8,128)S(1)}, f32[72,128]{1,0:T(8,128)S(1)}, u32[]{:S(2)}, u32[]{:S(2)}) %collective-permute-start.6) | collective-permute-done | bytes 36896 | tf_op jit(solution)/shard_map/ppermute | solution.py:727
  13.8 1.8 %shard_map.80 = (f32[8,72,128]{2,1,0:T(8,128)S(1)}, f32[8,72,128]{2,1,0:T(8,128)S(1)}, f32[32,4,128]{2,1,0:T(4,128)}) custom-call(f32[72,128]{1,0:T(8,128)S(1)} %get-tuple-element.39.refs_0_, f32[72,128]{1,0:T(8,128)S(1)} %collective-permute-done.refs_1_, f32[72,128]{1,0:T(8,128)S(1)} %collective-permute-done.1.refs_2_, ...), custom_call_target="tpu_custom_call" | custom-call | tf_op jit(solution)/shard_map/pallas_call | solution.py:32
  15.6 4.6 %all-to-all-start = ((f32[32,4,128]{2,1,0:T(4,128)}), f32[32,4,128]{2,1,0:T(4,128)S(1)}, u32[]{:S(2)}, u32[]{:S(2)}) async-start(f32[32,4,128]{2,1,0:T(4,128)} %get-tuple-element.56), calls=%async_computation | async-start | bytes 131072 | tf_op jit(solution)/shard_map/all_to_all | solution.py:716
  20.2 0.2 shard_map.81.refs_2_.refs_5_
  20.4 0.3 shard_map.82
  20.7 0.3 collective-permute-start.7
  21.1 2.5 %collective-permute-start.8 = (f32[3,72,128]{2,1,0:T(8,128)S(1)}, f32[3,72,128]{2,1,0:T(8,128)S(1)}, u32[]{:S(2)}, u32[]{:S(2)}) collective-permute-start(f32[3,72,128]{2,1,0:T(8,128)S(1)} %get-tuple-element.59), channel_id=1, source_target_pairs={{4,8},{12,16},{20,24},{28,0},{8,4},{16,12},{24,20},{0,28},{5,9},{1... | collective-permute-start | bytes 331784 | tf_op jit(solution)/shard_map/ppermute | solution.py:782
  23.6 0.7 %collective-permute-start.10 = (f32[72,128]{1,0:T(8,128)S(1)}, f32[72,128]{1,0:T(8,128)S(1)}, u32[]{:S(2)}, u32[]{:S(2)}) collective-permute-start(f32[72,128]{1,0:T(8,128)S(1)} %shard_map.81.refs_2_.refs_5_), channel_id=1, source_target_pairs={{1,2},{2,1},{5,6},{6,5},{9,10},{10,9},{13,14},{14,13},{17,18},{18,... | collective-permute-start | bytes 110600 | tf_op jit(solution)/shard_map/ppermute | solution.py:784
  24.2 4.3 %collective-permute-start.9 = (f32[72,128]{1,0:T(8,128)S(1)}, f32[72,128]{1,0:T(8,128)S(1)}, u32[]{:S(2)}, u32[]{:S(2)}) collective-permute-start(f32[72,128]{1,0:T(8,128)S(1)} %shard_map.81.refs_2_.refs_5_), channel_id=1, source_target_pairs={{0,1},{1,0},{2,3},{3,2},{4,5},{5,4},{6,7},{7,6},{8,9},{9,8},{10,11... | collective-permute-start | bytes 110600 | tf_op jit(solution)/shard_map/ppermute | solution.py:783
  28.5 0.0 all-to-all-done.refs_0_
  28.5 0.9 %shard_map.83 = (f32[112,128]{1,0:T(8,128)S(1)}, f32[1,128]{1,0:T(1,128)S(1)}) custom-call(f32[32,4,128]{2,1,0:T(4,128)S(1)} %all-to-all-done.refs_0_), custom_call_target="tpu_custom_call" | custom-call | tf_op jit(solution)/shard_map/pallas_call | solution.py:32
  29.4 0.0 collective-permute-done.10.refs_4_
  29.4 1.1 %collective-permute-done.9.refs_3_ = f32[72,128]{1,0:T(8,128)S(1)} collective-permute-done((f32[72,128]{1,0:T(8,128)S(1)}, f32[72,128]{1,0:T(8,128)S(1)}, u32[]{:S(2)}, u32[]{:S(2)}) %collective-permute-start.9) | collective-permute-done | bytes 36896 | tf_op jit(solution)/shard_map/ppermute | solution.py:783
  30.5 0.0 collective-permute-done.7.refs_1_
  30.5 0.0 collective-permute-done.8.refs_2_
  30.5 2.2 %shard_map.84 = (f32[8,72,128]{2,1,0:T(8,128)S(1)}, f32[32,8,128]{2,1,0:T(8,128)}) custom-call(f32[32,4,128]{2,1,0:T(4,128)S(1)} %all-to-all-done.refs_0_, f32[3,72,128]{2,1,0:T(8,128)S(1)} %collective-permute-done.7.refs_1_, f32[3,72,128]{2,1,0:T(8,128)S(1)} %collective-permute-done.8.refs_2_, f32[72,128]{1,0:T(8,128)S(1)} %collective-permute-done.9.refs_3_, ...), custom_call_target="tpu_custom_call" | custom-call | tf_op jit(solution)/shard_map/pallas_call | solution.py:32
  32.6 2.6 %all-to-all-start.1 = ((f32[32,8,128]{2,1,0:T(8,128)}), f32[32,8,128]{2,1,0:T(8,128)S(1)}, u32[]{:S(2)}, u32[]{:S(2)}) async-start(f32[32,8,128]{2,1,0:T(8,128)} %get-tuple-element.62), calls=%async_computation.1 | async-start | bytes 262144 | tf_op jit(solution)/shard_map/all_to_all | solution.py:716
  35.2 0.4 shard_map.86
  35.6 0.2 collective-permute-start.11
  35.8 1.7 %collective-permute-start.12 = (f32[2,72,128]{2,1,0:T(8,128)S(1)}, f32[2,72,128]{2,1,0:T(8,128)S(1)}, u32[]{:S(2)}, u32[]{:S(2)}) collective-permute-start(f32[2,72,128]{2,1,0:T(8,128)S(1)} %get-tuple-element.70), channel_id=1, source_target_pairs={{0,8},{4,12},{8,0},{12,4},{16,24},{20,28},{24,16},{28,20},{1,9},{5... | collective-permute-start | bytes 221192 | tf_op jit(solution)/shard_map/ppermute | solution.py:812
  37.5 0.1 collective-permute-start.13
  37.6 1.6 %collective-permute-start.14 = (f32[2,72,128]{2,1,0:T(8,128)S(1)}, f32[2,72,128]{2,1,0:T(8,128)S(1)}, u32[]{:S(2)}, u32[]{:S(2)}) collective-permute-start(f32[2,72,128]{2,1,0:T(8,128)S(1)} %get-tuple-element.72), channel_id=1, source_target_pairs={{0,16},{4,20},{8,24},{12,28},{16,0},{20,4},{24,8},{28,12},{1,17},{... | collective-permute-start | bytes 221192 | tf_op jit(solution)/shard_map/ppermute | solution.py:812
  39.2 0.1 collective-permute-start.15
  39.3 0.0 collective-permute-done.11.refs_2_
  39.3 2.6 %collective-permute-start.16 = (f32[2,72,128]{2,1,0:T(8,128)S(1)}, f32[2,72,128]{2,1,0:T(8,128)S(1)}, u32[]{:S(2)}, u32[]{:S(2)}) collective-permute-start(f32[2,72,128]{2,1,0:T(8,128)S(1)} %get-tuple-element.74), channel_id=1, source_target_pairs={{0,24},{4,28},{8,16},{12,20},{16,8},{20,12},{24,0},{28,4},{1,25},{... | collective-permute-start | bytes 221192 | tf_op jit(solution)/shard_map/ppermute | solution.py:812
  41.9 0.0 collective-permute-done.12.refs_3_
  41.9 0.7 %collective-permute-start.17 = (f32[2,72,128]{2,1,0:T(8,128)S(1)}, f32[2,72,128]{2,1,0:T(8,128)S(1)}, u32[]{:S(2)}, u32[]{:S(2)}) collective-permute-start(f32[2,72,128]{2,1,0:T(8,128)S(1)} %get-tuple-element.75), channel_id=1, source_target_pairs={{0,28},{4,24},{8,20},{12,16},{16,12},{20,8},{24,4},{28,0},{1,29},{... | collective-permute-start | bytes 221192 | tf_op jit(solution)/shard_map/ppermute | solution.py:812
  42.6 1.2 %all-to-all-done.1.refs_0_ = f32[32,8,128]{2,1,0:T(8,128)S(1)} async-done(((f32[32,8,128]{2,1,0:T(8,128)}), f32[32,8,128]{2,1,0:T(8,128)S(1)}, u32[]{:S(2)}, u32[]{:S(2)}) %all-to-all-start.1) | async-done | bytes 131104 | tf_op jit(solution)/shard_map/all_to_all | solution.py:716
  43.7 1.6 %shard_map.85 = (f32[560,128]{1,0:T(8,128)}, f32[16,128]{1,0:T(8,128)S(1)}) custom-call(f32[32,8,128]{2,1,0:T(8,128)S(1)} %all-to-all-done.1.refs_0_, f32[112,128]{1,0:T(8,128)S(1)} %get-tuple-element.63.refs_1_, f32[1,128]{1,0:T(1,128)S(1)} %get-tuple-element.61.refs_10_.refs_2_, f32[8,72,128]{2,1,0:T(8,128)S(1)} %get-tuple-element.57.smooth_ref.refs_0_.refs_6_.refs_3_, ...), custom_call_target="tpu_custom_call" | custom-call | tf_op jit(solution)/shard_map/pallas_call | solution.py:32
  45.4 0.0 collective-permute-done.13.refs_4_
  45.4 0.0 collective-permute-done.14.refs_5_
  45.4 1.1 %collective-permute-done.15.refs_6_ = f32[2,72,128]{2,1,0:T(8,128)S(1)} collective-permute-done((f32[2,72,128]{2,1,0:T(8,128)S(1)}, f32[2,72,128]{2,1,0:T(8,128)S(1)}, u32[]{:S(2)}, u32[]{:S(2)}) %collective-permute-start.15) | collective-permute-done | bytes 73760 | tf_op jit(solution)/shard_map/ppermute | solution.py:812
  46.4 0.0 collective-permute-done.16.refs_7_
  46.4 0.7 %collective-permute-done.17.refs_8_ = f32[2,72,128]{2,1,0:T(8,128)S(1)} collective-permute-done((f32[2,72,128]{2,1,0:T(8,128)S(1)}, f32[2,72,128]{2,1,0:T(8,128)S(1)}, u32[]{:S(2)}, u32[]{:S(2)}) %collective-permute-start.17) | collective-permute-done | bytes 73760 | tf_op jit(solution)/shard_map/ppermute | solution.py:812
  47.2 1.1 %shard_map.87 = f32[560,128]{1,0:T(8,128)} custom-call(f32[16,128]{1,0:T(8,128)S(1)} %get-tuple-element.66.refs_0_, f32[2,72,128]{2,1,0:T(8,128)S(1)} %get-tuple-element.68.refs_1_, f32[2,72,128]{2,1,0:T(8,128)S(1)} %collective-permute-done.11.refs_2_, f32[2,72,128]{2,1,0:T(8,128)S(1)} %collective-permute-done.12.refs_3_, ...), custom_call_target="tpu_custom_call" | custom-call | tf_op jit(solution)/shard_map/pallas_call | solution.py:32
  (1 shorter events, 0.0 us)
Async XLA Ops:
  0.6 1.0 %copy-start = (f32[70,8,128]{2,1,0:T(8,128)S(1)}, f32[70,8,128]{2,1,0:T(8,128)}, u32[]{:S(2)}) copy-start(f32[70,8,128]{2,1,0:T(8,128)} %param.9) | copy-start | bytes 860164
  1.6 9.2 %copy-start.1 = (f32[70,8,128]{2,1,0:T(8,128)S(1)}, f32[70,8,128]{2,1,0:T(8,128)}, u32[]{:S(2)}) copy-start(f32[70,8,128]{2,1,0:T(8,128)} %param.6) | copy-start | bytes 860164
  2.0 4.9 %collective-permute-start = (f32[72,128]{1,0:T(8,128)S(1)}, f32[72,128]{1,0:T(8,128)S(1)}, u32[]{:S(2)}, u32[]{:S(2)}) collective-permute-start(f32[72,128]{1,0:T(8,128)S(1)} %get-tuple-element.40), channel_id=1, source_target_pairs={{0,4},{4,0},{8,12},{12,8},{16,20},{20,16},{24,28},{28,24},{1,5},{5... | collective-permute-start | bytes 110600 | tf_op jit(solution)/shard_map/ppermute | solution.py:727
  2.5 7.0 %collective-permute-start.1 = (f32[72,128]{1,0:T(8,128)S(1)}, f32[72,128]{1,0:T(8,128)S(1)}, u32[]{:S(2)}, u32[]{:S(2)}) collective-permute-start(f32[72,128]{1,0:T(8,128)S(1)} %get-tuple-element.41), channel_id=1, source_target_pairs={{0,8},{4,12},{8,0},{12,4},{16,24},{20,28},{24,16},{28,20},{1,9},{5... | collective-permute-start | bytes 110600 | tf_op jit(solution)/shard_map/ppermute | solution.py:727
  5.0 7.2 %collective-permute-start.2 = (f32[72,128]{1,0:T(8,128)S(1)}, f32[72,128]{1,0:T(8,128)S(1)}, u32[]{:S(2)}, u32[]{:S(2)}) collective-permute-start(f32[72,128]{1,0:T(8,128)S(1)} %get-tuple-element.42), channel_id=1, source_target_pairs={{0,12},{4,8},{8,4},{12,0},{16,28},{20,24},{24,20},{28,16},{1,13},{... | collective-permute-start | bytes 110600 | tf_op jit(solution)/shard_map/ppermute | solution.py:727
  5.1 7.1 %collective-permute-start.3 = (f32[72,128]{1,0:T(8,128)S(1)}, f32[72,128]{1,0:T(8,128)S(1)}, u32[]{:S(2)}, u32[]{:S(2)}) collective-permute-start(f32[72,128]{1,0:T(8,128)S(1)} %get-tuple-element.43), channel_id=1, source_target_pairs={{0,16},{4,20},{8,24},{12,28},{16,0},{20,4},{24,8},{28,12},{1,17},{... | collective-permute-start | bytes 110600 | tf_op jit(solution)/shard_map/ppermute | solution.py:727
  6.9 5.4 %collective-permute-start.4 = (f32[72,128]{1,0:T(8,128)S(1)}, f32[72,128]{1,0:T(8,128)S(1)}, u32[]{:S(2)}, u32[]{:S(2)}) collective-permute-start(f32[72,128]{1,0:T(8,128)S(1)} %get-tuple-element.44), channel_id=1, source_target_pairs={{0,20},{4,16},{8,28},{12,24},{16,4},{20,0},{24,12},{28,8},{1,21},{... | collective-permute-start | bytes 110600 | tf_op jit(solution)/shard_map/ppermute | solution.py:727
  6.9 5.4 %collective-permute-start.5 = (f32[72,128]{1,0:T(8,128)S(1)}, f32[72,128]{1,0:T(8,128)S(1)}, u32[]{:S(2)}, u32[]{:S(2)}) collective-permute-start(f32[72,128]{1,0:T(8,128)S(1)} %get-tuple-element.45), channel_id=1, source_target_pairs={{0,24},{4,28},{8,16},{12,20},{16,8},{20,12},{24,0},{28,4},{1,25},{... | collective-permute-start | bytes 110600 | tf_op jit(solution)/shard_map/ppermute | solution.py:727
  9.5 4.3 %collective-permute-start.6 = (f32[72,128]{1,0:T(8,128)S(1)}, f32[72,128]{1,0:T(8,128)S(1)}, u32[]{:S(2)}, u32[]{:S(2)}) collective-permute-start(f32[72,128]{1,0:T(8,128)S(1)} %get-tuple-element.46), channel_id=1, source_target_pairs={{0,28},{4,24},{8,20},{12,16},{16,12},{20,8},{24,4},{28,0},{1,29},{... | collective-permute-start | bytes 110600 | tf_op jit(solution)/shard_map/ppermute | solution.py:727
  9.7 0.7 %copy-start.3 = (f32[69]{0:T(128)S(1)}, f32[69]{0:T(128)}, u32[]{:S(2)}) copy-start(f32[69]{0:T(128)} %param.8) | copy-start | bytes 832
  9.7 0.7 %copy-start.4 = (f32[70]{0:T(128)S(1)}, f32[70]{0:T(128)}, u32[]{:S(2)}) copy-start(f32[70]{0:T(128)} %param.10) | copy-start | bytes 844
  9.7 0.7 %copy-start.5 = (f32[70]{0:T(128)S(1)}, f32[70]{0:T(128)}, u32[]{:S(2)}) copy-start(f32[70]{0:T(128)} %param.11) | copy-start | bytes 844
  10.8 1.0 %copy-start.2 = (f32[70,8,128]{2,1,0:T(8,128)S(1)}, f32[70,8,128]{2,1,0:T(8,128)}, u32[]{:S(2)}) copy-start(f32[70,8,128]{2,1,0:T(8,128)} %param.7) | copy-start | bytes 860164
  15.6 12.9 %all-to-all-start = ((f32[32,4,128]{2,1,0:T(4,128)}), f32[32,4,128]{2,1,0:T(4,128)S(1)}, u32[]{:S(2)}, u32[]{:S(2)}) async-start(f32[32,4,128]{2,1,0:T(4,128)} %get-tuple-element.56), calls=%async_computation | async-start | bytes 131072 | tf_op jit(solution)/shard_map/all_to_all | solution.py:716
  20.7 9.7 %collective-permute-start.7 = (f32[3,72,128]{2,1,0:T(8,128)S(1)}, f32[3,72,128]{2,1,0:T(8,128)S(1)}, u32[]{:S(2)}, u32[]{:S(2)}) collective-permute-start(f32[3,72,128]{2,1,0:T(8,128)S(1)} %get-tuple-element.58), channel_id=1, source_target_pairs={{0,4},{4,0},{8,12},{12,8},{16,20},{20,16},{24,28},{28,24},{1,5},{5... | collective-permute-start | bytes 331784 | tf_op jit(solution)/shard_map/ppermute | solution.py:781
  21.1 9.4 %collective-permute-start.8 = (f32[3,72,128]{2,1,0:T(8,128)S(1)}, f32[3,72,128]{2,1,0:T(8,128)S(1)}, u32[]{:S(2)}, u32[]{:S(2)}) collective-permute-start(f32[3,72,128]{2,1,0:T(8,128)S(1)} %get-tuple-element.59), channel_id=1, source_target_pairs={{4,8},{12,16},{20,24},{28,0},{8,4},{16,12},{24,20},{0,28},{5,9},{1... | collective-permute-start | bytes 331784 | tf_op jit(solution)/shard_map/ppermute | solution.py:782
  23.6 5.8 %collective-permute-start.10 = (f32[72,128]{1,0:T(8,128)S(1)}, f32[72,128]{1,0:T(8,128)S(1)}, u32[]{:S(2)}, u32[]{:S(2)}) collective-permute-start(f32[72,128]{1,0:T(8,128)S(1)} %shard_map.81.refs_2_.refs_5_), channel_id=1, source_target_pairs={{1,2},{2,1},{5,6},{6,5},{9,10},{10,9},{13,14},{14,13},{17,18},{18,... | collective-permute-start | bytes 110600 | tf_op jit(solution)/shard_map/ppermute | solution.py:784
  24.2 6.2 %collective-permute-start.9 = (f32[72,128]{1,0:T(8,128)S(1)}, f32[72,128]{1,0:T(8,128)S(1)}, u32[]{:S(2)}, u32[]{:S(2)}) collective-permute-start(f32[72,128]{1,0:T(8,128)S(1)} %shard_map.81.refs_2_.refs_5_), channel_id=1, source_target_pairs={{0,1},{1,0},{2,3},{3,2},{4,5},{5,4},{6,7},{7,6},{8,9},{9,8},{10,11... | collective-permute-start | bytes 110600 | tf_op jit(solution)/shard_map/ppermute | solution.py:783
  32.6 11.1 %all-to-all-start.1 = ((f32[32,8,128]{2,1,0:T(8,128)}), f32[32,8,128]{2,1,0:T(8,128)S(1)}, u32[]{:S(2)}, u32[]{:S(2)}) async-start(f32[32,8,128]{2,1,0:T(8,128)} %get-tuple-element.62), calls=%async_computation.1 | async-start | bytes 262144 | tf_op jit(solution)/shard_map/all_to_all | solution.py:716
  35.6 3.7 %collective-permute-start.11 = (f32[2,72,128]{2,1,0:T(8,128)S(1)}, f32[2,72,128]{2,1,0:T(8,128)S(1)}, u32[]{:S(2)}, u32[]{:S(2)}) collective-permute-start(f32[2,72,128]{2,1,0:T(8,128)S(1)} %get-tuple-element.69), channel_id=1, source_target_pairs={{0,4},{4,0},{8,12},{12,8},{16,20},{20,16},{24,28},{28,24},{1,5},{5... | collective-permute-start | bytes 221192 | tf_op jit(solution)/shard_map/ppermute | solution.py:812
  35.8 6.1 %collective-permute-start.12 = (f32[2,72,128]{2,1,0:T(8,128)S(1)}, f32[2,72,128]{2,1,0:T(8,128)S(1)}, u32[]{:S(2)}, u32[]{:S(2)}) collective-permute-start(f32[2,72,128]{2,1,0:T(8,128)S(1)} %get-tuple-element.70), channel_id=1, source_target_pairs={{0,8},{4,12},{8,0},{12,4},{16,24},{20,28},{24,16},{28,20},{1,9},{5... | collective-permute-start | bytes 221192 | tf_op jit(solution)/shard_map/ppermute | solution.py:812
  37.5 7.9 %collective-permute-start.13 = (f32[2,72,128]{2,1,0:T(8,128)S(1)}, f32[2,72,128]{2,1,0:T(8,128)S(1)}, u32[]{:S(2)}, u32[]{:S(2)}) collective-permute-start(f32[2,72,128]{2,1,0:T(8,128)S(1)} %get-tuple-element.71), channel_id=1, source_target_pairs={{0,12},{4,8},{8,4},{12,0},{16,28},{20,24},{24,20},{28,16},{1,13},{... | collective-permute-start | bytes 221192 | tf_op jit(solution)/shard_map/ppermute | solution.py:812
  37.6 7.8 %collective-permute-start.14 = (f32[2,72,128]{2,1,0:T(8,128)S(1)}, f32[2,72,128]{2,1,0:T(8,128)S(1)}, u32[]{:S(2)}, u32[]{:S(2)}) collective-permute-start(f32[2,72,128]{2,1,0:T(8,128)S(1)} %get-tuple-element.72), channel_id=1, source_target_pairs={{0,16},{4,20},{8,24},{12,28},{16,0},{20,4},{24,8},{28,12},{1,17},{... | collective-permute-start | bytes 221192 | tf_op jit(solution)/shard_map/ppermute | solution.py:812
  39.2 7.3 %collective-permute-start.15 = (f32[2,72,128]{2,1,0:T(8,128)S(1)}, f32[2,72,128]{2,1,0:T(8,128)S(1)}, u32[]{:S(2)}, u32[]{:S(2)}) collective-permute-start(f32[2,72,128]{2,1,0:T(8,128)S(1)} %get-tuple-element.73), channel_id=1, source_target_pairs={{0,20},{4,16},{8,28},{12,24},{16,4},{20,0},{24,12},{28,8},{1,21},{... | collective-permute-start | bytes 221192 | tf_op jit(solution)/shard_map/ppermute | solution.py:812
  39.3 7.2 %collective-permute-start.16 = (f32[2,72,128]{2,1,0:T(8,128)S(1)}, f32[2,72,128]{2,1,0:T(8,128)S(1)}, u32[]{:S(2)}, u32[]{:S(2)}) collective-permute-start(f32[2,72,128]{2,1,0:T(8,128)S(1)} %get-tuple-element.74), channel_id=1, source_target_pairs={{0,24},{4,28},{8,16},{12,20},{16,8},{20,12},{24,0},{28,4},{1,25},{... | collective-permute-start | bytes 221192 | tf_op jit(solution)/shard_map/ppermute | solution.py:812
  41.9 5.3 %collective-permute-start.17 = (f32[2,72,128]{2,1,0:T(8,128)S(1)}, f32[2,72,128]{2,1,0:T(8,128)S(1)}, u32[]{:S(2)}, u32[]{:S(2)}) collective-permute-start(f32[2,72,128]{2,1,0:T(8,128)S(1)} %get-tuple-element.75), channel_id=1, source_target_pairs={{0,28},{4,24},{8,20},{12,16},{16,12},{20,8},{24,4},{28,0},{1,29},{... | collective-permute-start | bytes 221192 | tf_op jit(solution)/shard_map/ppermute | solution.py:812

commit v4 on v3

--- a/solution.py
+++ b/solution.py
@@ -28,14 +28,14 @@
     return jnp.sum(value, axis=(0, 1), keepdims=True)
 
 
-def call(kernel, outs, *args, scratch=(), copies=0):
+def call(kernel, outs, *args, scratch=(), copies=0, sends=False):
     return pl.pallas_call(
         kernel,
         out_shape=[jax.ShapeDtypeStruct(shape, F32) for shape in outs],
         in_specs=[HBM if copies else VMEM] * len(args),
-        out_specs=[VMEM] * len(outs),
-        scratch_shapes=[pltpu.VMEM(shape, F32) for shape in scratch]
-        + [pltpu.SemaphoreType.DMA((copies,))] * bool(copies),
+        out_specs=[HBM] * sends + [VMEM] * (len(outs) - sends),
+        scratch_shapes=[pltpu.VMEM(shape, F32) for shape in [*scratch, *outs[:sends]]]
+        + [pltpu.SemaphoreType.DMA((max(copies, 1),))] * bool(copies or sends),
         compiler_params=pltpu.CompilerParams(vmem_limit_bytes=32 * 1024 * 1024),
     )(*args)
 
@@ -59,27 +59,33 @@
     count, lanes = len(tiles), tiles[0].shape[1]
     width = lanes // count
     group = iota(tiles[0].shape, 1) // width
-    tiles = list(tiles)
-    step = count // 2
-    while step:
-        low = (group & step) == 0
-        for j in range(count):
-            if j & step == 0:
-                a, b = tiles[j], tiles[j + step]
-                tiles[j] = jnp.where(low, a, turn(b, step * width))
-                tiles[j + step] = jnp.where(low, turn(a, -step * width), b)
-        step //= 2
-    return tiles
-
-
-def pack_kernel(levels, x_ref, *out_refs):
-    *out_refs, packed_ref = out_refs
+    tiles = [turn(tile, i * width) for i, tile in enumerate(tiles)]
+    step = 1
+    while step < count:
+        here = (group & step) == 0
+        tiles = [jnp.where(here, tiles[u], tiles[(u + step) % count]) for u in range(count)]
+        step *= 2
+    return [turn(tiles[-s % count], -s * width) for s in range(count)]
+
+
+def pack_kernel(levels, x_ref, packed_ref, near_ref):
     points, padded, _ = packed_ref.shape
     for s, tile in enumerate(swap_groups(load_columns(x_ref, points, levels, padded))):
         packed_ref[s] = tile
+    other = 1 - (lax.axis_index("tile") & 1)
+    for j in range(points // 2):
+        near_ref[j] = packed_ref[2 * j + other]
+
+
+def far_steps(tiles):
+    return list(range(tiles - 2, 0, -2))
+
+
+def relay_kernel(near_ref, packed_ref, *out_refs):
     tile = lax.axis_index("tile")
-    for k, out_ref in enumerate(out_refs):
-        out_ref[...] = packed_ref[tile ^ k]
+    for step, out_ref in zip(far_steps(packed_ref.shape[0]), out_refs):
+        place = tile ^ step
+        out_ref[0], out_ref[1] = packed_ref[place], near_ref[place >> 1]
 
 
 def tables_kernel(levels, *refs):
@@ -212,14 +218,18 @@
 
 
 def smooth_kernel(levels, tiles, groups, swap, *refs):
-    *kelvin_refs, forced_ref, weight_ref, base_ref, matrices_ref, rows_ref, unit_ref = refs[: -3 - swap]
-    residual_ref, smooth_ref, message_ref = refs[-3 - swap : len(refs) - swap]
+    *refs, message_ref, message_sem = refs
+    count = len(refs) - 6 - 2 * swap
+    *kelvin_refs, forced_ref, weight_ref, base_ref, matrices_ref, rows_ref, unit_ref = refs[:count]
+    sent_ref, residual_ref, smooth_ref, rim_ref, inner_ref, outer_ref, *refs = refs[count:]
     points, padded, across = residual_ref.shape
     if swap:
-        scratch_ref = refs[-1]
+        state_ref, scratch_ref = refs
         tile = lax.axis_index("tile")
-        for k, part_ref in enumerate(kelvin_refs):
-            scratch_ref[tile ^ k] = part_ref[...]
+        packed_ref, near_ref, *far_refs = kelvin_refs
+        scratch_ref[tile], scratch_ref[tile ^ 1] = packed_ref[tile], near_ref[tile >> 1]
+        for step, far_ref in zip(far_steps(points), far_refs):
+            scratch_ref[tile ^ step], scratch_ref[tile ^ (step + 1)] = far_ref[0], far_ref[1]
         kelvin = swap_groups([scratch_ref[i] for i in range(points)])
     else:
         kelvin = [kelvin_refs[0][i] for i in range(points)]
@@ -261,44 +271,33 @@
     corners = (0, 2, across - 1, 1)
     for place, corner in zip(neighbours(tiles, groups)[5:], corners):
         message_ref[pl.ds(place, 1), 0, :] = rows[corner : corner + 1] + scalars
-
-
-def rim_kernel(smooth_ref, weight_ref, rim_ref):
-    points, padded, across = smooth_ref.shape
+    send = pltpu.make_async_copy(message_ref, sent_ref, message_sem.at[0])
+    send.start()
+
     stride = across // points
-    lane = iota((padded, across), 1)
     rim = jnp.zeros((padded, across), F32)
     for i in range(points):
         place = (lane - stride * i + 2) & (across - 1)
-        rim = jnp.where(place < 4, turn(smooth_ref[i], stride * i), rim)
-        rim = jnp.where((place == 5) | (place == 6), turn(weight_ref[i], stride * i + 4), rim)
+        rim = jnp.where(place < 4, turn(smooth[i], stride * i), rim)
+        rim = jnp.where((place == 5) | (place == 6), turn(weight[i], stride * i + 4), rim)
     rim_ref[...] = rim
-
-
-def side_kernel(swap, smooth_ref, weight_ref, _, inner_ref, outer_ref, *packed_ref):
-    points = smooth_ref.shape[0]
     even = lax.rem(lax.axis_index("tile"), 2) == 0
-    for j, place in enumerate((0, 1)):
-        west, east = smooth_ref[place], smooth_ref[points - 2 + place]
+    sides = zip((smooth[0], smooth[1], weight[0]), (smooth[-2], smooth[-1], weight[-1]))
+    for j, (west, east) in enumerate(sides):
         inner_ref[j] = jnp.where(even, east, west)
         outer_ref[j] = jnp.where(even, west, east)
-    west, east = weight_ref[0], weight_ref[points - 1]
-    inner_ref[2] = jnp.where(even, east, west)
-    outer_ref[2] = jnp.where(even, west, east)
     if swap:
-        for s, tile in enumerate(swap_groups([smooth_ref[i] for i in range(points)])):
-            packed_ref[0][s] = tile
-
-
-def send_kernel(smooth_ref, second_ref, *out_refs):
-    *out_refs, packed_ref = out_refs
-    points = second_ref.shape[0]
-    for s, tile in enumerate(swap_groups([second_ref[i] for i in range(points)])):
-        packed_ref[s] = tile
+        for s, tile in enumerate(swap_groups(smooth)):
+            state_ref[s] = tile
+    send.wait()
+
+
+def send_kernel(near_ref, smooth_ref, second_ref, *out_refs):
     tile = lax.axis_index("tile")
-    for k, out_ref in enumerate(out_refs):
-        out_ref[0] = smooth_ref[tile ^ k]
-        out_ref[1] = packed_ref[tile ^ k]
+    for step, out_ref in zip(far_steps(smooth_ref.shape[0]), out_refs):
+        place = tile ^ step
+        out_ref[0], out_ref[1] = smooth_ref[place], second_ref[place]
+        out_ref[2], out_ref[3] = near_ref[place >> 1, 0], near_ref[place >> 1, 1]
 
 
 def neighbours(tiles, groups):
@@ -482,9 +481,14 @@
     weight_ref,
     inverse_ref,
     coarse_ref,
-    second_ref,
-    message_ref,
+    *refs,
 ):
+    *refs, message_ref, message_sem = refs
+    swap = len(refs) > 2
+    if swap:
+        packed_smooth_ref, sent_ref, second_ref, packed_ref, near_ref = refs
+    else:
+        sent_ref, second_ref = refs
     points, padded, across = smooth_ref.shape
     blocks = tiles * groups
     stride = across // points
@@ -511,10 +515,18 @@
     lane = iota(shape, 1)
     first, final = lane == 0, lane == across - 1
 
-    def across_sum(tile, low, high):
-        low = jnp.where(first, jnp.where(at_south, tile, low), turn(tile, 1))
-        high = jnp.where(final, jnp.where(at_north, tile, high), turn(tile, -1))
-        return low + high
+    inside = lane & (stride - 1)
+    is_south, is_north = inside == stride - 1, inside == 0
+    outside = lane == jnp.where(at_south, 0, -1)
+    outside = outside | (lane == jnp.where(at_north, across - 1, -1))
+
+    def across_sum(tile, ends):
+        ends = jnp.where(outside, tile, ends)
+        return jnp.where(first, ends, turn(tile, 1)) + jnp.where(final, ends, turn(tile, -1))
+
+    def tile_ends(south, north):
+        both = jnp.where(is_north, turn(south, 1), turn(north, -1))
+        return [turn(both, -stride * i) for i in range(points)]
 
     weight = [weight_ref[i] for i in range(points)]
     from_west = [jnp.where(even_tile, outer_ref[j], inner_ref[j]) for j in range(3)]
@@ -522,48 +534,45 @@
     weight = from_west[2:] + weight + from_east[2:]
     field = from_west[:2] + [smooth_ref[i] for i in range(points)] + from_east[:2]
 
-    def spread_image(tile_weight, here, ends, low, high):
-        value = tile_weight * here
-        if ends:
-            value = value + add_all([here - there for there in ends])
-        return value + jnp.where(first, here - low, jnp.where(final, here - high, 0.0))
-
     rim, low, high = rim_ref[...], low_ref[...], high_ref[...]
     from_south = jnp.where(even_group, high, low)
     from_north = jnp.where(even_group, low, high)
-    lows = [c_sw] + [turn(from_south, 1 - stride * i) for i in range(points)] + [c_se]
-    highs = [c_nw] + [turn(from_north, -1 - stride * i) for i in range(points)] + [c_ne]
-    near = [(e_west, (own,), e_sw, e_nw)] + [(own, (), e_south, e_north)] * points
-    near += [(e_east, (own,), e_se, e_ne)]
-    near[1] = (own, (e_west,), e_south, e_north)
-    near[points] = (own, (e_east,), e_south, e_north)
+    ends = [jnp.where(first, c_sw, c_nw), *tile_ends(from_south, from_north), jnp.where(first, c_se, c_ne)]
+
+    def steps(here, low, high):
+        return jnp.where(first, here - low, jnp.where(final, here - high, 0.0))
+
+    here = [e_west] + [own] * points + [e_east]
+    jumps = [steps(e_west, e_sw, e_nw) + (e_west - own)]
+    jumps += [steps(own, e_south, e_north)] * points
+    jumps += [steps(e_east, e_se, e_ne) + (e_east - own)]
+    jumps[1] = jumps[1] + (own - e_west)
+    jumps[points] = jumps[points] + (own - e_east)
     image = [
         (field[i] + field[i + 2])
-        + across_sum(field[i + 1], lows[i], highs[i])
-        - (weight[i] * field[i + 1] + spread_image(weight[i], *near[i]))
+        + across_sum(field[i + 1], ends[i])
+        - (weight[i] * (field[i + 1] + here[i]) + jumps[i])
         for i in range(points + 2)
     ]
     edge = stride * (points - 1)
 
     def ring_image(tile, step, here, west, east, west_lane, east_lane, c_west, c_east):
         rim_weight = turn(tile, -4)
-        spread = rim_weight * here + (here - own)
-        spread = spread + jnp.where(lane == west_lane, here - west, jnp.where(lane == east_lane, here - east, 0.0))
+        spread = (here - own) + jnp.where(lane == west_lane, here - west, jnp.where(lane == east_lane, here - east, 0.0))
         return (
             jnp.where(lane == west_lane, c_west, turn(tile, stride))
             + jnp.where(lane == east_lane, c_east, turn(tile, -stride))
             + (turn(tile, step) + turn(rim, -step))
-            - (rim_weight * tile + spread)
+            - (rim_weight * (tile + here) + spread)
         )
 
     ring_south = ring_image(from_south, 1, e_south, e_sw, e_se, across - 1, edge - 1, c_sw, c_se)
     ring_north = ring_image(from_north, -1, e_north, e_nw, e_ne, 0, edge, c_nw, c_ne)
-    inside = lane & (stride - 1)
-    is_south, is_north = inside == stride - 1, inside == 0
     ring = jnp.where(is_south, ring_south, jnp.where(is_north, ring_north, 0.0))
     ring_field = jnp.where(is_south, from_south, from_north)
     second = dot(inverse_ref[:, :padded], image + [ring])
     ring = ring_field - second.pop()
+    ends = tile_ends(ring, ring)
     second = [field[i + 1] - tile for i, tile in enumerate(second)]
 
     names = ("image", "change", "residual")
@@ -579,7 +588,7 @@
         second_ref[i] = tile
         again = (
             (second[i] + second[i + 2])
-            + across_sum(tile, turn(ring, 1 - stride * i), turn(ring, -1 - stride * i))
+            + across_sum(tile, ends[i])
             - weight[i + 1] * tile
         )
         residual = residual_ref[i]
@@ -613,6 +622,16 @@
     row = scalars_row(out, across)
     message_ref[...] = jnp.zeros(message_ref.shape, F32)
     message_ref[:, 0, :] = jnp.broadcast_to(row, (blocks, across))
+    send = pltpu.make_async_copy(message_ref, sent_ref, message_sem.at[0])
+    send.start()
+    if swap:
+        for s, tile in enumerate(swap_groups(second[1 : points + 1])):
+            packed_ref[s] = tile
+        other = 1 - (lax.axis_index("tile") & 1)
+        for j in range(points // 2):
+            near_ref[j, 0] = packed_smooth_ref[2 * j + other]
+            near_ref[j, 1] = packed_ref[2 * j + other]
+    send.wait()
 
 
 def final_kernel(
@@ -683,13 +702,16 @@
 
 
 def state_kernel(levels, scalars_ref, *refs):
-    *part_refs, state_ref, scratch_ref = refs
+    smooth_ref, second_ref, near_ref, *part_refs, state_ref, scratch_ref = refs
     tile = lax.axis_index("tile")
     scale, kappa = scalars_ref[0:1, :], scalars_ref[1:2, :]
-    for k, part_ref in enumerate(part_refs):
-        shift = scalars_ref[2 + k : 3 + k, :]
-        scratch_ref[tile ^ k] = scale * part_ref[0] + (kappa * part_ref[1] + shift)
-    store_columns(state_ref, swap_groups([scratch_ref[s] for s in range(len(part_refs))]), levels)
+    pairs = {0: (smooth_ref[tile], second_ref[tile]), 1: (near_ref[tile >> 1, 0], near_ref[tile >> 1, 1])}
+    for step, part_ref in zip(far_steps(smooth_ref.shape[0]), part_refs):
+        pairs[step] = (part_ref[0], part_ref[1])
+        pairs[step + 1] = (part_ref[2], part_ref[3])
+    for k, (smooth, second) in pairs.items():
+        scratch_ref[tile ^ k] = scale * smooth + (kappa * second + scalars_ref[2 + k : 3 + k, :])
+    store_columns(state_ref, swap_groups([scratch_ref[s] for s in range(len(pairs))]), levels)
 
 
 def per_device(
@@ -708,6 +730,7 @@
     width = across // tiles
     swap = tiles == points
     flat = (levels * points, across)
+    field = (points, padded, across)
 
     def to_tiles(value):
         return lax.all_to_all(value, "tile", split_axis=0, concat_axis=0, tiled=True)
@@ -720,15 +743,18 @@
 
     kelvin = previous_kelvin_field
     if swap:
-        kelvin = list(call(
-            part(pack_kernel, levels), [(padded, across)] * tiles, kelvin.reshape(flat), scratch=[(points, padded, across)]
-        ))
-        for k in range(1, tiles):
-            kelvin[k] = lax.ppermute(kelvin[k], "tile", [(i, i ^ k) for i in range(tiles)])
+        near = (tiles // 2, padded, across)
+        packed, near = call(part(pack_kernel, levels), [field, near], kelvin.reshape(flat))
+        near = lax.ppermute(near, "tile", [(i, i ^ 1) for i in range(tiles)])
+        far = call(relay_kernel, [(2, padded, across)] * (tiles // 2 - 1), near, packed)
+        kelvin = [packed, near] + [
+            lax.ppermute(value, "tile", [(i, i ^ step) for i in range(tiles)])
+            for step, value in zip(far_steps(tiles), far)
+        ]
     else:
         kelvin = kelvin.reshape(levels, points, tiles, width).transpose(2, 1, 0, 3)
         kelvin = to_tiles(kelvin).transpose(1, 2, 0, 3).reshape(points, levels, across)
-        kelvin = [jnp.pad(kelvin, ((0, 0), (0, padded - levels), (0, 0)))]
+        kelvin = jnp.pad(kelvin, ((0, 0), (0, padded - levels), (0, 0)))
 
     vectors = [v[None, :] for v in (layer_link_factor, longwave_opacity, shortwave_opacity)]
     inverse, matrix, absorbed = call(
@@ -744,7 +770,6 @@
 
     forcing = forcing_vector.reshape(flat)
     weights = shift_weights.reshape(flat)
-    field = (points, padded, across)
     forced, weights, *prepared = call(
         part(prepare_kernel, levels),
         [field, field, field, (2 * padded, across), (16, across), (padded, across)],
@@ -757,17 +782,14 @@
     )
     prepared = [forced, weights, *prepared]
     message = (blocks, MESSAGE_ROWS, across)
-    residual, smooth, message = call(
+    tile, side = (padded, across), (3, padded, across)
+    message, residual, smooth, rim, inner, outer, *packed = call(
         part(smooth_kernel, levels, tiles, groups, swap),
-        [field, field, message],
-        *kelvin,
+        [message, field, field, tile, side, side] + [field] * swap,
+        *(kelvin if swap else [kelvin]),
         *prepared,
         scratch=[field] * swap,
-    )
-    tile, side = (padded, across), (3, padded, across)
-    (rim,) = call(rim_kernel, [tile], smooth, weights)
-    inner, outer, *packed = call(
-        part(side_kernel, swap), [side, side] + [field] * swap, smooth, weights, rim
+        sends=True,
     )
     received = gather(message)
 
@@ -787,9 +809,10 @@
         [(saved_rows(tiles, groups), lanes), (1, lanes)],
         received,
     )
-    second, message = call(
+    near = (tiles // 2, 2, padded, across)
+    message, second, *sent = call(
         part(second_kernel, levels, tiles, groups),
-        [field, (blocks, LAST_ROWS, across)],
+        [(blocks, LAST_ROWS, across), field] + [field, near] * swap,
         received,
         inner,
         outer,
@@ -801,15 +824,17 @@
         weights,
         inverse,
         coarse,
+        *packed,
+        sends=True,
     )
     received = gather(message)
     parts = []
     if swap:
-        parts = list(
-            call(send_kernel, [(2, padded, across)] * tiles, packed[0], second, scratch=[field])
-        )
-        for k in range(1, tiles):
-            parts[k] = lax.ppermute(parts[k], "tile", [(i, i ^ k) for i in range(tiles)])
+        near = lax.ppermute(sent[1], "tile", inner_pairs(tiles))
+        parts = [packed[0], sent[0], near]
+        far = call(send_kernel, [(4, padded, across)] * (tiles // 2 - 1), near, packed[0], sent[0])
+        for step, value in zip(far_steps(tiles), far):
+            parts.append(lax.ppermute(value, "tile", [(i, i ^ step) for i in range(tiles)]))
     solution_field, state = call(
         part(final_kernel, levels, tiles, groups, swap),
         [flat, (-(-(tiles + 2) // 8) * 8, across) if swap else field],

time: 48.6 us -> 46.1 us (0.949)
  waiting for transfers between devices: 5.65 us -> 11.4 us
  starting transfers between devices: 29.5 us -> 23.9 us
  local copies, waits for them, and re-layouts: 2.58 us -> 0.97 us
  Pallas kernels: 9.69 us -> 8.76 us
    ppermute x14 -> x8, starting transfers between devices: 14.6 us -> 8.66 us  [the longest x6 8.07 us: per_device(): lax.ppermute(value, 'tile', [(i, i ^ step) for i in range(tiles)])]
    all_to_all x2, waiting for transfers between devices: 1.18 us -> 4.79 us  [gather(): lax.all_to_all(value, ('tile', 'grp'), split_axis=0, concat_axis=0, tiled...]
    ppermute x14 -> x8, waiting for transfers between devices: 3.39 us -> 5.49 us  [the longest x6 4.88 us: per_device(): lax.ppermute(value, 'tile', [(i, i ^ step) for i in range(tiles)])]
    unnamed x12, local copies, waits for them, and re-layouts: 2.58 us -> 0.97 us
    pallas_call x11 -> x10, Pallas kernels: 9.69 us -> 8.76 us  [call(): pl.pallas_call(kernel, out_shape=[jax.ShapeDtypeStruct(shape, F32) for sh...]
  transfers between devices with their start and end apart: 20 -> 14, of which waited for: 5 -> 7; matrix products, arithmetic and copies ran while one was open for 0% -> 0% of each run, Pallas kernels for 9% -> 7%
where the time goes in v4:
time: 46.1 us; the launch traced here: 45.8 us
  starting transfers between devices  23.9 us (52%)
  waiting for transfers between devices  11.4 us (25%)
  Pallas kernels  8.76 us (19%)
  local copies, waits for them, and re-layouts  0.97 us (2%)
  between operations  0.76 us (2%)
    pallas_call x10, Pallas kernels, call(): pl.pallas_call(kernel, out_shape=[jax.ShapeDtypeStruct(shape, F32) for sh...  8.76 us
    ppermute x6, starting transfers between devices, per_device(): lax.ppermute(value, 'tile', [(i, i ^ step) for i in range(tiles)])  8.07 us
    all_to_all x2, starting transfers between devices, gather(): lax.all_to_all(value, ('tile', 'grp'), split_axis=0, concat_axis=0, tiled...  7.52 us
    ppermute x6, waiting for transfers between devices, per_device(): lax.ppermute(value, 'tile', [(i, i ^ step) for i in range(tiles)])  4.88 us
    all_to_all x2, waiting for transfers between devices, gather(): lax.all_to_all(value, ('tile', 'grp'), split_axis=0, concat_axis=0, tiled...  4.79 us
    ppermute x1, starting transfers between devices, per_device(): low = lax.ppermute(rim, 'grp', inner_pairs(groups))  4.27 us
    ppermute x1, starting transfers between devices, per_device(): outer = lax.ppermute(outer, 'tile', outer_pairs(tiles, True))  2.53 us
    ppermute x1, waiting for transfers between devices, per_device(): low = lax.ppermute(rim, 'grp', inner_pairs(groups))  1.07 us
  transfers between devices with their start and end apart: 14, of which 7 were waited for; matrix products, arithmetic and copies ran while one was open for 0% of the time, Pallas kernels for 7%

profile of v4, /device:TPU:0, one launch (start us, length us, event | category | flops | bytes accessed | tf_op | source)
XLA Modules:
  0.0 45.8 jit_solution(11588191318894611973)
XLA Ops:
  0.6 0.0 copy-start
  0.6 0.9 %copy-done = f32[70,8,128]{2,1,0:T(8,128)S(1)} copy-done((f32[70,8,128]{2,1,0:T(8,128)S(1)}, f32[70,8,128]{2,1,0:T(8,128)}, u32[]{:S(2)}) %copy-start) | copy-done | bytes 286744
  1.6 0.0 copy-start.3
  1.6 0.0 copy-start.4
  1.6 0.0 copy-start.5
  1.6 0.0 copy-start.2
  1.6 0.3 shard_map.77
  1.9 0.0 copy-start.1
  1.9 0.5 %collective-permute-start = (f32[4,72,128]{2,1,0:T(8,128)S(1)}, f32[4,72,128]{2,1,0:T(8,128)S(1)}, u32[]{:S(2)}, u32[]{:S(2)}) collective-permute-start(f32[4,72,128]{2,1,0:T(8,128)S(1)} %get-tuple-element.35), channel_id=1, source_target_pairs={{0,4},{4,0},{8,12},{12,8},{16,20},{20,16},{24,28},{28,24},{1,5},{5... | collective-permute-start | bytes 442376 | tf_op jit(solution)/shard_map/ppermute | solution.py:748
  2.4 0.0 copy-done.3
  2.4 0.0 copy-done.4
  2.4 0.0 copy-done.5
  2.4 0.4 shard_map.79
  2.8 0.6 %collective-permute-done.near_ref.refs_1_ = f32[4,72,128]{2,1,0:T(8,128)S(1)} collective-permute-done((f32[4,72,128]{2,1,0:T(8,128)S(1)}, f32[4,72,128]{2,1,0:T(8,128)S(1)}, u32[]{:S(2)}, u32[]{:S(2)}) %collective-permute-start) | collective-permute-done | bytes 147488 | tf_op jit(solution)/shard_map/ppermute | solution.py:748
  3.4 3.9 %collective-permute-start.1 = (f32[2,72,128]{2,1,0:T(8,128)S(1)}, f32[2,72,128]{2,1,0:T(8,128)S(1)}, u32[]{:S(2)}, u32[]{:S(2)}) collective-permute-start(f32[2,72,128]{2,1,0:T(8,128)S(1)} %get-tuple-element.36), channel_id=1, source_target_pairs={{0,24},{4,28},{8,16},{12,20},{16,8},{20,12},{24,0},{28,4},{1,25},{... | collective-permute-start | bytes 221192 | tf_op jit(solution)/shard_map/ppermute | solution.py:751
  7.3 0.5 %collective-permute-start.2 = (f32[2,72,128]{2,1,0:T(8,128)S(1)}, f32[2,72,128]{2,1,0:T(8,128)S(1)}, u32[]{:S(2)}, u32[]{:S(2)}) collective-permute-start(f32[2,72,128]{2,1,0:T(8,128)S(1)} %get-tuple-element.37), channel_id=1, source_target_pairs={{0,16},{4,20},{8,24},{12,28},{16,0},{20,4},{24,8},{28,12},{1,17},{... | collective-permute-start | bytes 221192 | tf_op jit(solution)/shard_map/ppermute | solution.py:751
  7.8 0.1 collective-permute-start.3
  8.0 0.0 copy-done.2
  8.0 0.0 copy-done.1
  8.0 0.5 %shard_map.80 = (f32[8,72,128]{2,1,0:T(8,128)S(1)}, f32[8,72,128]{2,1,0:T(8,128)S(1)}, f32[8,72,128]{2,1,0:T(8,128)S(1)}, f32[144,128]{1,0:T(8,128)S(1)}, f32[16,128]{1,0:T(8,128)S(1)}, /*index=5*/f32[72,128]{1,0:T(8,128)S(1)}) custom-call(f32[560,128]{1,0:T(8,128)S(1)} %bitcast.9, f32[560,128]{1,0:T(8,128)S(1)} %bitcast.10, ...), custom_call_target="tpu_custom_call" | custom-call | tf_op jit(solution)/shard_map/pallas_call | solution.py:32
  8.5 1.4 %collective-permute-done.1.refs_2_ = f32[2,72,128]{2,1,0:T(8,128)S(1)} collective-permute-done((f32[2,72,128]{2,1,0:T(8,128)S(1)}, f32[2,72,128]{2,1,0:T(8,128)S(1)}, u32[]{:S(2)}, u32[]{:S(2)}) %collective-permute-start.1) | collective-permute-done | bytes 73760 | tf_op jit(solution)/shard_map/ppermute | solution.py:751
  10.0 1.7 %collective-permute-done.2.refs_3_ = f32[2,72,128]{2,1,0:T(8,128)S(1)} collective-permute-done((f32[2,72,128]{2,1,0:T(8,128)S(1)}, f32[2,72,128]{2,1,0:T(8,128)S(1)}, u32[]{:S(2)}, u32[]{:S(2)}) %collective-permute-start.2) | collective-permute-done | bytes 73760 | tf_op jit(solution)/shard_map/ppermute | solution.py:751
  11.7 0.5 %collective-permute-done.3.refs_4_ = f32[2,72,128]{2,1,0:T(8,128)S(1)} collective-permute-done((f32[2,72,128]{2,1,0:T(8,128)S(1)}, f32[2,72,128]{2,1,0:T(8,128)S(1)}, u32[]{:S(2)}, u32[]{:S(2)}) %collective-permute-start.3) | collective-permute-done | bytes 73760 | tf_op jit(solution)/shard_map/ppermute | solution.py:751
  12.2 1.8 %shard_map.81 = (f32[32,4,128]{2,1,0:T(4,128)}, f32[8,72,128]{2,1,0:T(8,128)S(1)}, f32[8,72,128]{2,1,0:T(8,128)S(1)}, f32[72,128]{1,0:T(8,128)S(1)}, f32[3,72,12...) custom-call(f32[8,72,128]{2,1,0:T(8,128)S(1)} %get-tuple-element.34.packed_ref.refs_0_, ...), custom_call_target="tpu_custom_call" | custom-call | tf_op jit(solution)/shard_map/pallas_call | solution.py:32
  14.0 4.9 %all-to-all-start = ((f32[32,4,128]{2,1,0:T(4,128)}), f32[32,4,128]{2,1,0:T(4,128)S(1)}, u32[]{:S(2)}, u32[]{:S(2)}) async-start(f32[32,4,128]{2,1,0:T(4,128)} %get-tuple-element.48), calls=%async_computation | async-start | bytes 131072 | tf_op jit(solution)/shard_map/all_to_all | solution.py:739
  18.9 0.3 collective-permute-start.4
  19.2 2.5 %collective-permute-start.5 = (f32[3,72,128]{2,1,0:T(8,128)S(1)}, f32[3,72,128]{2,1,0:T(8,128)S(1)}, u32[]{:S(2)}, u32[]{:S(2)}) collective-permute-start(f32[3,72,128]{2,1,0:T(8,128)S(1)} %get-tuple-element.50), channel_id=1, source_target_pairs={{4,8},{12,16},{20,24},{28,0},{8,4},{16,12},{24,20},{0,28},{5,9},{1... | collective-permute-start | bytes 331784 | tf_op jit(solution)/shard_map/ppermute | solution.py:804
  21.8 0.7 %collective-permute-start.7 = (f32[72,128]{1,0:T(8,128)S(1)}, f32[72,128]{1,0:T(8,128)S(1)}, u32[]{:S(2)}, u32[]{:S(2)}) collective-permute-start(f32[72,128]{1,0:T(8,128)S(1)} %get-tuple-element.51.refs_5_), channel_id=1, source_target_pairs={{1,2},{2,1},{5,6},{6,5},{9,10},{10,9},{13,14},{14,13},{17,18},{18,... | collective-permute-start | bytes 110600 | tf_op jit(solution)/shard_map/ppermute | solution.py:806
  22.4 4.3 %collective-permute-start.6 = (f32[72,128]{1,0:T(8,128)S(1)}, f32[72,128]{1,0:T(8,128)S(1)}, u32[]{:S(2)}, u32[]{:S(2)}) collective-permute-start(f32[72,128]{1,0:T(8,128)S(1)} %get-tuple-element.51.refs_5_), channel_id=1, source_target_pairs={{0,1},{1,0},{2,3},{3,2},{4,5},{5,4},{6,7},{7,6},{8,9},{9,8},{10,11... | collective-permute-start | bytes 110600 | tf_op jit(solution)/shard_map/ppermute | solution.py:805
  26.7 0.0 all-to-all-done.refs_0_
  26.7 0.9 %shard_map.82 = (f32[112,128]{1,0:T(8,128)S(1)}, f32[1,128]{1,0:T(1,128)S(1)}) custom-call(f32[32,4,128]{2,1,0:T(4,128)S(1)} %all-to-all-done.refs_0_), custom_call_target="tpu_custom_call" | custom-call | tf_op jit(solution)/shard_map/pallas_call | solution.py:32
  27.6 0.0 collective-permute-done.7.refs_4_
  27.6 1.1 %collective-permute-done.6.refs_3_ = f32[72,128]{1,0:T(8,128)S(1)} collective-permute-done((f32[72,128]{1,0:T(8,128)S(1)}, f32[72,128]{1,0:T(8,128)S(1)}, u32[]{:S(2)}, u32[]{:S(2)}) %collective-permute-start.6) | collective-permute-done | bytes 36896 | tf_op jit(solution)/shard_map/ppermute | solution.py:805
  28.6 0.0 collective-permute-done.4.refs_1_
  28.6 0.0 collective-permute-done.5.refs_2_
  28.7 2.2 %shard_map.83 = (f32[32,8,128]{2,1,0:T(8,128)}, f32[8,72,128]{2,1,0:T(8,128)S(1)}, f32[8,72,128]{2,1,0:T(8,128)S(1)}, f32[4,2,72,128]{3,2,1,0:T(8,128)S(1)}) custom-call(f32[32,4,128]{2,1,0:T(4,128)S(1)} %all-to-all-done.refs_0_, f32[3,72,128]{2,1,0:T(8,128)S(1)} %collective-permute-done.4.refs_1_, f32[3,72,128]{2,1,0:T(8,128)S(1)} %collective-permute-done.5.refs_2_, ...), custom_call_target="tpu_custom_call" | custom-call | tf_op jit(solution)/shard_map/pallas_call | solution.py:32
  30.9 0.1 collective-permute-start.8
  31.0 2.6 %all-to-all-start.1 = ((f32[32,8,128]{2,1,0:T(8,128)}), f32[32,8,128]{2,1,0:T(8,128)S(1)}, u32[]{:S(2)}, u32[]{:S(2)}) async-start(f32[32,8,128]{2,1,0:T(8,128)} %get-tuple-element.56), calls=%async_computation.1 | async-start | bytes 262144 | tf_op jit(solution)/shard_map/all_to_all | solution.py:739
  33.6 0.0 collective-permute-done.8.near_ref.refs_3_
  33.6 2.6 %collective-permute-start.9 = (f32[4,72,128]{2,1,0:T(8,128)S(1)}, f32[4,72,128]{2,1,0:T(8,128)S(1)}, u32[]{:S(2)}, u32[]{:S(2)}) collective-permute-start(f32[4,72,128]{2,1,0:T(8,128)S(1)} %get-tuple-element.63), channel_id=1, source_target_pairs={{0,24},{4,28},{8,16},{12,20},{16,8},{20,12},{24,0},{28,4},{1,25},{... | collective-permute-start | bytes 442376 | tf_op jit(solution)/shard_map/ppermute | solution.py:837
  36.3 0.6 %collective-permute-start.10 = (f32[4,72,128]{2,1,0:T(8,128)S(1)}, f32[4,72,128]{2,1,0:T(8,128)S(1)}, u32[]{:S(2)}, u32[]{:S(2)}) collective-permute-start(f32[4,72,128]{2,1,0:T(8,128)S(1)} %get-tuple-element.64), channel_id=1, source_target_pairs={{0,16},{4,20},{8,24},{12,28},{16,0},{20,4},{24,8},{28,12},{1,17},{... | collective-permute-start | bytes 442376 | tf_op jit(solution)/shard_map/ppermute | solution.py:837
  36.8 0.4 collective-permute-start.11
  37.2 4.8 %all-to-all-done.1.refs_0_ = f32[32,8,128]{2,1,0:T(8,128)S(1)} async-done(((f32[32,8,128]{2,1,0:T(8,128)}), f32[32,8,128]{2,1,0:T(8,128)S(1)}, u32[]{:S(2)}, u32[]{:S(2)}) %all-to-all-start.1) | async-done | bytes 131104 | tf_op jit(solution)/shard_map/all_to_all | solution.py:739
  42.0 1.6 %shard_map.84 = (f32[560,128]{1,0:T(8,128)}, f32[16,128]{1,0:T(8,128)S(1)}) custom-call(f32[32,8,128]{2,1,0:T(8,128)S(1)} %all-to-all-done.1.refs_0_, f32[112,128]{1,0:T(8,128)S(1)} %get-tuple-element.57.refs_1_, f32[1,128]{1,0:T(1,128)S(1)} %get-tuple-element.54.refs_10_.refs_2_, f32[8,72,128]{2,1,0:T(8,128)S(1)} %get-tuple-element.52.refs_6_.refs_3_, ...), custom_call_target="tpu_custom_call" | custom-call | tf_op jit(solution)/shard_map/pallas_call | solution.py:32
  43.6 0.0 collective-permute-done.9.refs_4_
  43.6 1.2 %collective-permute-done.10.refs_5_ = f32[4,72,128]{2,1,0:T(8,128)S(1)} collective-permute-done((f32[4,72,128]{2,1,0:T(8,128)S(1)}, f32[4,72,128]{2,1,0:T(8,128)S(1)}, u32[]{:S(2)}, u32[]{:S(2)}) %collective-permute-start.10) | collective-permute-done | bytes 147488 | tf_op jit(solution)/shard_map/ppermute | solution.py:837
  44.8 0.0 collective-permute-done.11.refs_6_
  44.8 1.0 %shard_map.86 = f32[560,128]{1,0:T(8,128)} custom-call(f32[16,128]{1,0:T(8,128)S(1)} %get-tuple-element.60.refs_0_, f32[8,72,128]{2,1,0:T(8,128)S(1)} %get-tuple-element.55.refs_11_.smooth_ref.refs_1_, f32[8,72,128]{2,1,0:T(8,128)S(1)} %get-tuple-element.61.second_ref.refs_2_, f32[4,2,72,128]{3,2,1,0:T(8,128)S(1)} %collective-permute-done.8.near_ref.refs_3_, ...), custom_call_target="tpu_custom_call" | custom-call | tf_op jit(solution)/shard_map/pallas_call | solution.py:32
  (3 shorter events, 0.1 us)
Async XLA Ops:
  0.6 1.0 %copy-start = (f32[70,8,128]{2,1,0:T(8,128)S(1)}, f32[70,8,128]{2,1,0:T(8,128)}, u32[]{:S(2)}) copy-start(f32[70,8,128]{2,1,0:T(8,128)} %param.9) | copy-start | bytes 860164
  1.6 0.8 %copy-start.3 = (f32[69]{0:T(128)S(1)}, f32[69]{0:T(128)}, u32[]{:S(2)}) copy-start(f32[69]{0:T(128)} %param.8) | copy-start | bytes 832
  1.6 0.8 %copy-start.4 = (f32[70]{0:T(128)S(1)}, f32[70]{0:T(128)}, u32[]{:S(2)}) copy-start(f32[70]{0:T(128)} %param.10) | copy-start | bytes 844
  1.6 0.8 %copy-start.5 = (f32[70]{0:T(128)S(1)}, f32[70]{0:T(128)}, u32[]{:S(2)}) copy-start(f32[70]{0:T(128)} %param.11) | copy-start | bytes 844
  1.6 6.4 %copy-start.2 = (f32[70,8,128]{2,1,0:T(8,128)S(1)}, f32[70,8,128]{2,1,0:T(8,128)}, u32[]{:S(2)}) copy-start(f32[70,8,128]{2,1,0:T(8,128)} %param.7) | copy-start | bytes 860164
  1.9 6.1 %copy-start.1 = (f32[70,8,128]{2,1,0:T(8,128)S(1)}, f32[70,8,128]{2,1,0:T(8,128)}, u32[]{:S(2)}) copy-start(f32[70,8,128]{2,1,0:T(8,128)} %param.6) | copy-start | bytes 860164
  1.9 1.5 %collective-permute-start = (f32[4,72,128]{2,1,0:T(8,128)S(1)}, f32[4,72,128]{2,1,0:T(8,128)S(1)}, u32[]{:S(2)}, u32[]{:S(2)}) collective-permute-start(f32[4,72,128]{2,1,0:T(8,128)S(1)} %get-tuple-element.35), channel_id=1, source_target_pairs={{0,4},{4,0},{8,12},{12,8},{16,20},{20,16},{24,28},{28,24},{1,5},{5... | collective-permute-start | bytes 442376 | tf_op jit(solution)/shard_map/ppermute | solution.py:748
  3.4 6.5 %collective-permute-start.1 = (f32[2,72,128]{2,1,0:T(8,128)S(1)}, f32[2,72,128]{2,1,0:T(8,128)S(1)}, u32[]{:S(2)}, u32[]{:S(2)}) collective-permute-start(f32[2,72,128]{2,1,0:T(8,128)S(1)} %get-tuple-element.36), channel_id=1, source_target_pairs={{0,24},{4,28},{8,16},{12,20},{16,8},{20,12},{24,0},{28,4},{1,25},{... | collective-permute-start | bytes 221192 | tf_op jit(solution)/shard_map/ppermute | solution.py:751
  7.3 4.4 %collective-permute-start.2 = (f32[2,72,128]{2,1,0:T(8,128)S(1)}, f32[2,72,128]{2,1,0:T(8,128)S(1)}, u32[]{:S(2)}, u32[]{:S(2)}) collective-permute-start(f32[2,72,128]{2,1,0:T(8,128)S(1)} %get-tuple-element.37), channel_id=1, source_target_pairs={{0,16},{4,20},{8,24},{12,28},{16,0},{20,4},{24,8},{28,12},{1,17},{... | collective-permute-start | bytes 221192 | tf_op jit(solution)/shard_map/ppermute | solution.py:751
  7.8 4.4 %collective-permute-start.3 = (f32[2,72,128]{2,1,0:T(8,128)S(1)}, f32[2,72,128]{2,1,0:T(8,128)S(1)}, u32[]{:S(2)}, u32[]{:S(2)}) collective-permute-start(f32[2,72,128]{2,1,0:T(8,128)S(1)} %get-tuple-element.38), channel_id=1, source_target_pairs={{0,8},{4,12},{8,0},{12,4},{16,24},{20,28},{24,16},{28,20},{1,9},{5... | collective-permute-start | bytes 221192 | tf_op jit(solution)/shard_map/ppermute | solution.py:751
  14.0 12.7 %all-to-all-start = ((f32[32,4,128]{2,1,0:T(4,128)}), f32[32,4,128]{2,1,0:T(4,128)S(1)}, u32[]{:S(2)}, u32[]{:S(2)}) async-start(f32[32,4,128]{2,1,0:T(4,128)} %get-tuple-element.48), calls=%async_computation | async-start | bytes 131072 | tf_op jit(solution)/shard_map/all_to_all | solution.py:739
  18.9 9.7 %collective-permute-start.4 = (f32[3,72,128]{2,1,0:T(8,128)S(1)}, f32[3,72,128]{2,1,0:T(8,128)S(1)}, u32[]{:S(2)}, u32[]{:S(2)}) collective-permute-start(f32[3,72,128]{2,1,0:T(8,128)S(1)} %get-tuple-element.49), channel_id=1, source_target_pairs={{0,4},{4,0},{8,12},{12,8},{16,20},{20,16},{24,28},{28,24},{1,5},{5... | collective-permute-start | bytes 331784 | tf_op jit(solution)/shard_map/ppermute | solution.py:803
  19.2 9.4 %collective-permute-start.5 = (f32[3,72,128]{2,1,0:T(8,128)S(1)}, f32[3,72,128]{2,1,0:T(8,128)S(1)}, u32[]{:S(2)}, u32[]{:S(2)}) collective-permute-start(f32[3,72,128]{2,1,0:T(8,128)S(1)} %get-tuple-element.50), channel_id=1, source_target_pairs={{4,8},{12,16},{20,24},{28,0},{8,4},{16,12},{24,20},{0,28},{5,9},{1... | collective-permute-start | bytes 331784 | tf_op jit(solution)/shard_map/ppermute | solution.py:804
  21.8 5.8 %collective-permute-start.7 = (f32[72,128]{1,0:T(8,128)S(1)}, f32[72,128]{1,0:T(8,128)S(1)}, u32[]{:S(2)}, u32[]{:S(2)}) collective-permute-start(f32[72,128]{1,0:T(8,128)S(1)} %get-tuple-element.51.refs_5_), channel_id=1, source_target_pairs={{1,2},{2,1},{5,6},{6,5},{9,10},{10,9},{13,14},{14,13},{17,18},{18,... | collective-permute-start | bytes 110600 | tf_op jit(solution)/shard_map/ppermute | solution.py:806
  22.4 6.2 %collective-permute-start.6 = (f32[72,128]{1,0:T(8,128)S(1)}, f32[72,128]{1,0:T(8,128)S(1)}, u32[]{:S(2)}, u32[]{:S(2)}) collective-permute-start(f32[72,128]{1,0:T(8,128)S(1)} %get-tuple-element.51.refs_5_), channel_id=1, source_target_pairs={{0,1},{1,0},{2,3},{3,2},{4,5},{5,4},{6,7},{7,6},{8,9},{9,8},{10,11... | collective-permute-start | bytes 110600 | tf_op jit(solution)/shard_map/ppermute | solution.py:805
  30.9 2.7 %collective-permute-start.8 = (f32[4,2,72,128]{3,2,1,0:T(8,128)S(1)}, f32[4,2,72,128]{3,2,1,0:T(8,128)S(1)}, u32[]{:S(2)}, u32[]{:S(2)}) collective-permute-start(f32[4,2,72,128]{3,2,1,0:T(8,128)S(1)} %get-tuple-element.62), channel_id=1, source_target_pairs={{0,4},{4,0},{8,12},{12,8},{16,20},{20,16},{24,28},{28,24},{1,5},{5... | collective-permute-start | bytes 884744 | tf_op jit(solution)/shard_map/ppermute | solution.py:833
  31.0 11.0 %all-to-all-start.1 = ((f32[32,8,128]{2,1,0:T(8,128)}), f32[32,8,128]{2,1,0:T(8,128)S(1)}, u32[]{:S(2)}, u32[]{:S(2)}) async-start(f32[32,8,128]{2,1,0:T(8,128)} %get-tuple-element.56), calls=%async_computation.1 | async-start | bytes 262144 | tf_op jit(solution)/shard_map/all_to_all | solution.py:739
  33.6 10.0 %collective-permute-start.9 = (f32[4,72,128]{2,1,0:T(8,128)S(1)}, f32[4,72,128]{2,1,0:T(8,128)S(1)}, u32[]{:S(2)}, u32[]{:S(2)}) collective-permute-start(f32[4,72,128]{2,1,0:T(8,128)S(1)} %get-tuple-element.63), channel_id=1, source_target_pairs={{0,24},{4,28},{8,16},{12,20},{16,8},{20,12},{24,0},{28,4},{1,25},{... | collective-permute-start | bytes 442376 | tf_op jit(solution)/shard_map/ppermute | solution.py:837
  36.3 8.6 %collective-permute-start.10 = (f32[4,72,128]{2,1,0:T(8,128)S(1)}, f32[4,72,128]{2,1,0:T(8,128)S(1)}, u32[]{:S(2)}, u32[]{:S(2)}) collective-permute-start(f32[4,72,128]{2,1,0:T(8,128)S(1)} %get-tuple-element.64), channel_id=1, source_target_pairs={{0,16},{4,20},{8,24},{12,28},{16,0},{20,4},{24,8},{28,12},{1,17},{... | collective-permute-start | bytes 442376 | tf_op jit(solution)/shard_map/ppermute | solution.py:837
  36.8 8.0 %collective-permute-start.11 = (f32[4,72,128]{2,1,0:T(8,128)S(1)}, f32[4,72,128]{2,1,0:T(8,128)S(1)}, u32[]{:S(2)}, u32[]{:S(2)}) collective-permute-start(f32[4,72,128]{2,1,0:T(8,128)S(1)} %get-tuple-element.65), channel_id=1, source_target_pairs={{0,8},{4,12},{8,0},{12,4},{16,24},{20,28},{24,16},{28,20},{1,9},{5... | collective-permute-start | bytes 442376 | tf_op jit(solution)/shard_map/ppermute | solution.py:837

commit v5 on v4

--- a/solution.py
+++ b/solution.py
@@ -466,41 +466,36 @@
     coarse_ref[...] = coarse
 
 
-def second_kernel(
+def beyond(groups, lane, across, none=-1):
+    group = lax.axis_index("grp")
+    south = jnp.where(group == 0, 0, none)
+    north = jnp.where(group == groups - 1, across - 1, none)
+    return (lane == south) | (lane == north)
+
+
+def inside_kernel(
     levels,
     tiles,
     groups,
     received_ref,
+    coarse_ref,
     inner_ref,
     outer_ref,
-    low_ref,
-    high_ref,
-    rim_ref,
     smooth_ref,
-    residual_ref,
     weight_ref,
     inverse_ref,
-    coarse_ref,
-    *refs,
+    image_ref,
+    second_ref,
+    values_ref,
+    corners_ref,
 ):
-    *refs, message_ref, message_sem = refs
-    swap = len(refs) > 2
-    if swap:
-        packed_smooth_ref, sent_ref, second_ref, packed_ref, near_ref = refs
-    else:
-        sent_ref, second_ref = refs
     points, padded, across = smooth_ref.shape
-    blocks = tiles * groups
-    stride = across // points
-    group_index = lax.axis_index("grp")
-    even_tile = lax.rem(lax.axis_index("tile"), 2) == 0
-    even_group = lax.rem(group_index, 2) == 0
-    at_south, at_north = group_index == 0, group_index == groups - 1
-
     coarse = coarse_ref[...]
     places = neighbours(tiles, groups)
     lane = iota(coarse.shape, 1)
     picked = [jnp.sum(jnp.where(lane == place, coarse, 0.0), axis=1, keepdims=True) for place in places]
+    for j, value in enumerate(picked):
+        values_ref[j : j + 1, :] = jnp.broadcast_to(value, (1, across))
     shape = (padded, across)
     real = iota(shape, 0) < levels
     own, e_west, e_east, e_south, e_north, e_sw, e_se, e_nw, e_ne = [
@@ -512,32 +507,26 @@
     corners = jnp.concatenate(corner_rows + [jnp.zeros((across - 4, across), F32)], axis=0).T
     c_sw, c_se, c_nw, c_ne = [corners[:padded, j : j + 1] for j in range(4)]
 
+    for j, corner in enumerate((c_sw, c_se, c_nw, c_ne)):
+        corners_ref[j] = jnp.broadcast_to(corner, shape)
+
     lane = iota(shape, 1)
     first, final = lane == 0, lane == across - 1
 
-    inside = lane & (stride - 1)
-    is_south, is_north = inside == stride - 1, inside == 0
-    outside = lane == jnp.where(at_south, 0, -1)
-    outside = outside | (lane == jnp.where(at_north, across - 1, -1))
+    outside = beyond(groups, lane, across)
 
     def across_sum(tile, ends):
         ends = jnp.where(outside, tile, ends)
         return jnp.where(first, ends, turn(tile, 1)) + jnp.where(final, ends, turn(tile, -1))
 
-    def tile_ends(south, north):
-        both = jnp.where(is_north, turn(south, 1), turn(north, -1))
-        return [turn(both, -stride * i) for i in range(points)]
-
+    even_tile = lax.rem(lax.axis_index("tile"), 2) == 0
     weight = [weight_ref[i] for i in range(points)]
     from_west = [jnp.where(even_tile, outer_ref[j], inner_ref[j]) for j in range(3)]
     from_east = [jnp.where(even_tile, inner_ref[j], outer_ref[j]) for j in range(3)]
     weight = from_west[2:] + weight + from_east[2:]
     field = from_west[:2] + [smooth_ref[i] for i in range(points)] + from_east[:2]
 
-    rim, low, high = rim_ref[...], low_ref[...], high_ref[...]
-    from_south = jnp.where(even_group, high, low)
-    from_north = jnp.where(even_group, low, high)
-    ends = [jnp.where(first, c_sw, c_nw), *tile_ends(from_south, from_north), jnp.where(first, c_se, c_ne)]
+    ends = [jnp.where(first, c_sw, c_nw), *[jnp.zeros(shape, F32)] * points, jnp.where(first, c_se, c_ne)]
 
     def steps(here, low, high):
         return jnp.where(first, here - low, jnp.where(final, here - high, 0.0))
@@ -554,6 +543,57 @@
         - (weight[i] * (field[i + 1] + here[i]) + jumps[i])
         for i in range(points + 2)
     ]
+    smoothed = dot(inverse_ref[:, :padded], image)
+    for i in range(points + 2):
+        image_ref[i] = image[i]
+        second_ref[i] = field[i + 1] - smoothed[i]
+
+
+def second_kernel(
+    levels,
+    groups,
+    low_ref,
+    high_ref,
+    rim_ref,
+    residual_ref,
+    weight_ref,
+    inverse_ref,
+    image_ref,
+    second_ref_in,
+    values_ref,
+    corners_ref,
+    *refs,
+):
+    *refs, message_ref, message_sem = refs
+    swap = len(refs) > 2
+    if swap:
+        packed_smooth_ref, sent_ref, second_ref, packed_ref, near_ref = refs
+    else:
+        sent_ref, second_ref = refs
+    points, padded, across = residual_ref.shape
+    blocks = message_ref.shape[0]
+    stride = across // points
+    even_group = lax.rem(lax.axis_index("grp"), 2) == 0
+
+    shape = (padded, across)
+    real = iota(shape, 0) < levels
+    values = [values_ref[j : j + 1, :] for j in range(9)]
+    own, e_west, e_east, e_south, e_north, e_sw, e_se, e_nw, e_ne = [
+        jnp.where(real, value, 0.0) for value in values
+    ]
+    c_sw, c_se, c_nw, c_ne = [corners_ref[j] for j in range(4)]
+    weight = [weight_ref[i] for i in range(points)]
+    lane = iota(shape, 1)
+    first, final = lane == 0, lane == across - 1
+    outside = beyond(groups, lane, across)
+    inside = lane & (stride - 1)
+    is_south, is_north = inside == stride - 1, inside == 0
+    rim, low, high = rim_ref[...], low_ref[...], high_ref[...]
+    from_south = jnp.where(even_group, high, low)
+    from_north = jnp.where(even_group, low, high)
+    outer = beyond(groups, jnp.where(is_north, 0, jnp.where(is_south, across - 1, 1)), across)
+    both = jnp.where(is_north, turn(from_south, 1), turn(from_north, -1))
+    both = jnp.where((is_north | is_south) & jnp.logical_not(outer), both, 0.0)
     edge = stride * (points - 1)
 
     def ring_image(tile, step, here, west, east, west_lane, east_lane, c_west, c_east):
@@ -570,10 +610,16 @@
     ring_north = ring_image(from_north, -1, e_north, e_nw, e_ne, 0, edge, c_nw, c_ne)
     ring = jnp.where(is_south, ring_south, jnp.where(is_north, ring_north, 0.0))
     ring_field = jnp.where(is_south, from_south, from_north)
-    second = dot(inverse_ref[:, :padded], image + [ring])
-    ring = ring_field - second.pop()
-    ends = tile_ends(ring, ring)
-    second = [field[i + 1] - tile for i, tile in enumerate(second)]
+    ring, smoothed = dot(inverse_ref[:, :padded], [ring, both])
+    ring = ring_field - ring
+    second, image = [second_ref_in[0]], [None]
+    ends = first | final
+    for i in range(1, points + 1):
+        shift = -stride * (i - 1)
+        image.append(jnp.where(ends, image_ref[i] + turn(both, shift), image_ref[i]))
+        second.append(jnp.where(ends, second_ref_in[i] - turn(smoothed, shift), second_ref_in[i]))
+    second.append(second_ref_in[points + 1])
+    both = jnp.where(is_north, turn(ring, 1), turn(ring, -1))
 
     names = ("image", "change", "residual")
     pairs = {}
@@ -586,16 +632,17 @@
     for i in range(points):
         tile = second[i + 1]
         second_ref[i] = tile
+        ends = jnp.where(outside, tile, turn(both, -stride * i))
         again = (
             (second[i] + second[i + 2])
-            + across_sum(tile, ends[i])
-            - weight[i + 1] * tile
+            + (jnp.where(first, ends, turn(tile, 1)) + jnp.where(final, ends, turn(tile, -1)))
+            - weight[i] * tile
         )
         residual = residual_ref[i]
         result = residual - image[i + 1]
         change = result - again
         left.append(fold(again + (result - 4.0 * tile)))
-        heavy = weight[i + 1]
+        heavy = weight[i]
         collect("qq", result * result)
         collect("rq", residual * result)
         collect("qd", result * change)
@@ -804,26 +851,37 @@
     outer = lax.ppermute(outer, "tile", outer_pairs(tiles, True))
     low = lax.ppermute(rim, "grp", inner_pairs(groups))
     high = lax.ppermute(rim, "grp", outer_pairs(groups, False))
+    wide = (points + 2, padded, across)
     steps, coarse = call(
         part(coarse_kernel, levels, points, tiles, groups),
         [(saved_rows(tiles, groups), lanes), (1, lanes)],
         received,
     )
+    image, second, values, corners = call(
+        part(inside_kernel, levels, tiles, groups),
+        [wide, wide, (16, across), (4, padded, across)],
+        received,
+        coarse,
+        inner,
+        outer,
+        smooth,
+        weights,
+        inverse,
+    )
     near = (tiles // 2, 2, padded, across)
     message, second, *sent = call(
-        part(second_kernel, levels, tiles, groups),
+        part(second_kernel, levels, groups),
         [(blocks, LAST_ROWS, across), field] + [field, near] * swap,
-        received,
-        inner,
-        outer,
         low,
         high,
         rim,
-        smooth,
         residual,
         weights,
         inverse,
-        coarse,
+        image,
+        second,
+        values,
+        corners,
         *packed,
         sends=True,
     )

time: 46.1 us -> 45.6 us (0.989)
  waiting for transfers between devices: 11.4 us -> 10.6 us
    ppermute x1, waiting for transfers between devices: 1.07 us -> 0.32 us  [per_device(): low = lax.ppermute(rim, 'grp', inner_pairs(groups))]
    pallas_call x10 -> x11, Pallas kernels: 8.76 us -> 8.96 us  [call(): pl.pallas_call(kernel, out_shape=[jax.ShapeDtypeStruct(shape, F32) for sh...]
  transfers between devices with their start and end apart: 14 -> 14, of which waited for: 7 -> 7; matrix products, arithmetic and copies ran while one was open for 0% -> 0% of each run, Pallas kernels for 7% -> 9%
where the time goes in v5:
time: 45.6 us; the launch traced here: 45.3 us
  starting transfers between devices  23.9 us (52%)
  waiting for transfers between devices  10.6 us (23%)
  Pallas kernels  8.96 us (20%)
  local copies, waits for them, and re-layouts  0.97 us (2%)
  between operations  0.78 us (2%)
    pallas_call x11, Pallas kernels, call(): pl.pallas_call(kernel, out_shape=[jax.ShapeDtypeStruct(shape, F32) for sh...  8.96 us
    ppermute x6, starting transfers between devices, per_device(): lax.ppermute(value, 'tile', [(i, i ^ step) for i in range(tiles)])  8.07 us
    all_to_all x2, starting transfers between devices, gather(): lax.all_to_all(value, ('tile', 'grp'), split_axis=0, concat_axis=0, tiled...  7.52 us
    ppermute x6, waiting for transfers between devices, per_device(): lax.ppermute(value, 'tile', [(i, i ^ step) for i in range(tiles)])  4.9 us
    all_to_all x2, waiting for transfers between devices, gather(): lax.all_to_all(value, ('tile', 'grp'), split_axis=0, concat_axis=0, tiled...  4.79 us
    ppermute x1, starting transfers between devices, per_device(): low = lax.ppermute(rim, 'grp', inner_pairs(groups))  4.27 us
    ppermute x1, starting transfers between devices, per_device(): outer = lax.ppermute(outer, 'tile', outer_pairs(tiles, True))  2.53 us
    unnamed x12, local copies, waits for them, and re-layouts  0.97 us
  transfers between devices with their start and end apart: 14, of which 7 were waited for; matrix products, arithmetic and copies ran while one was open for 0% of the time, Pallas kernels for 9%

profile of v5, /device:TPU:0, one launch (start us, length us, event | category | flops | bytes accessed | tf_op | source)
XLA Modules:
  0.0 45.3 jit_solution(10113497504592435299)
XLA Ops:
  0.6 0.0 copy-start
  0.6 0.9 %copy-done = f32[70,8,128]{2,1,0:T(8,128)S(1)} copy-done((f32[70,8,128]{2,1,0:T(8,128)S(1)}, f32[70,8,128]{2,1,0:T(8,128)}, u32[]{:S(2)}) %copy-start) | copy-done | bytes 286744
  1.6 0.0 copy-start.3
  1.6 0.0 copy-start.4
  1.6 0.0 copy-start.5
  1.6 0.0 copy-start.2
  1.6 0.3 shard_map.77
  1.9 0.0 copy-start.1
  1.9 0.5 %collective-permute-start = (f32[4,72,128]{2,1,0:T(8,128)S(1)}, f32[4,72,128]{2,1,0:T(8,128)S(1)}, u32[]{:S(2)}, u32[]{:S(2)}) collective-permute-start(f32[4,72,128]{2,1,0:T(8,128)S(1)} %get-tuple-element.39), channel_id=1, source_target_pairs={{0,4},{4,0},{8,12},{12,8},{16,20},{20,16},{24,28},{28,24},{1,5},{5... | collective-permute-start | bytes 442376 | tf_op jit(solution)/shard_map/ppermute | solution.py:795
  2.4 0.0 copy-done.3
  2.4 0.0 copy-done.4
  2.4 0.0 copy-done.5
  2.4 0.4 shard_map.79
  2.8 0.6 %collective-permute-done.near_ref.refs_1_ = f32[4,72,128]{2,1,0:T(8,128)S(1)} collective-permute-done((f32[4,72,128]{2,1,0:T(8,128)S(1)}, f32[4,72,128]{2,1,0:T(8,128)S(1)}, u32[]{:S(2)}, u32[]{:S(2)}) %collective-permute-start) | collective-permute-done | bytes 147488 | tf_op jit(solution)/shard_map/ppermute | solution.py:795
  3.4 3.9 %collective-permute-start.1 = (f32[2,72,128]{2,1,0:T(8,128)S(1)}, f32[2,72,128]{2,1,0:T(8,128)S(1)}, u32[]{:S(2)}, u32[]{:S(2)}) collective-permute-start(f32[2,72,128]{2,1,0:T(8,128)S(1)} %get-tuple-element.40), channel_id=1, source_target_pairs={{0,24},{4,28},{8,16},{12,20},{16,8},{20,12},{24,0},{28,4},{1,25},{... | collective-permute-start | bytes 221192 | tf_op jit(solution)/shard_map/ppermute | solution.py:798
  7.3 0.5 %collective-permute-start.2 = (f32[2,72,128]{2,1,0:T(8,128)S(1)}, f32[2,72,128]{2,1,0:T(8,128)S(1)}, u32[]{:S(2)}, u32[]{:S(2)}) collective-permute-start(f32[2,72,128]{2,1,0:T(8,128)S(1)} %get-tuple-element.41), channel_id=1, source_target_pairs={{0,16},{4,20},{8,24},{12,28},{16,0},{20,4},{24,8},{28,12},{1,17},{... | collective-permute-start | bytes 221192 | tf_op jit(solution)/shard_map/ppermute | solution.py:798
  7.8 0.1 collective-permute-start.3
  8.0 0.0 copy-done.2
  8.0 0.0 copy-done.1
  8.0 0.5 %shard_map.80 = (f32[8,72,128]{2,1,0:T(8,128)S(1)}, f32[8,72,128]{2,1,0:T(8,128)S(1)}, f32[8,72,128]{2,1,0:T(8,128)S(1)}, f32[144,128]{1,0:T(8,128)S(1)}, f32[16,128]{1,0:T(8,128)S(1)}, /*index=5*/f32[72,128]{1,0:T(8,128)S(1)}) custom-call(f32[560,128]{1,0:T(8,128)S(1)} %bitcast.9, f32[560,128]{1,0:T(8,128)S(1)} %bitcast.10, ...), custom_call_target="tpu_custom_call" | custom-call | tf_op jit(solution)/shard_map/pallas_call | solution.py:32
  8.5 1.4 %collective-permute-done.1.refs_2_ = f32[2,72,128]{2,1,0:T(8,128)S(1)} collective-permute-done((f32[2,72,128]{2,1,0:T(8,128)S(1)}, f32[2,72,128]{2,1,0:T(8,128)S(1)}, u32[]{:S(2)}, u32[]{:S(2)}) %collective-permute-start.1) | collective-permute-done | bytes 73760 | tf_op jit(solution)/shard_map/ppermute | solution.py:798
  10.0 1.7 %collective-permute-done.2.refs_3_ = f32[2,72,128]{2,1,0:T(8,128)S(1)} collective-permute-done((f32[2,72,128]{2,1,0:T(8,128)S(1)}, f32[2,72,128]{2,1,0:T(8,128)S(1)}, u32[]{:S(2)}, u32[]{:S(2)}) %collective-permute-start.2) | collective-permute-done | bytes 73760 | tf_op jit(solution)/shard_map/ppermute | solution.py:798
  11.7 0.5 %collective-permute-done.3.refs_4_ = f32[2,72,128]{2,1,0:T(8,128)S(1)} collective-permute-done((f32[2,72,128]{2,1,0:T(8,128)S(1)}, f32[2,72,128]{2,1,0:T(8,128)S(1)}, u32[]{:S(2)}, u32[]{:S(2)}) %collective-permute-start.3) | collective-permute-done | bytes 73760 | tf_op jit(solution)/shard_map/ppermute | solution.py:798
  12.2 1.8 %shard_map.81 = (f32[32,4,128]{2,1,0:T(4,128)}, f32[8,72,128]{2,1,0:T(8,128)S(1)}, f32[8,72,128]{2,1,0:T(8,128)S(1)}, f32[72,128]{1,0:T(8,128)S(1)}, f32[3,72,12...) custom-call(f32[8,72,128]{2,1,0:T(8,128)S(1)} %get-tuple-element.38.packed_ref.refs_0_, ...), custom_call_target="tpu_custom_call" | custom-call | tf_op jit(solution)/shard_map/pallas_call | solution.py:32
  14.0 4.9 %all-to-all-start = ((f32[32,4,128]{2,1,0:T(4,128)}), f32[32,4,128]{2,1,0:T(4,128)S(1)}, u32[]{:S(2)}, u32[]{:S(2)}) async-start(f32[32,4,128]{2,1,0:T(4,128)} %get-tuple-element.54), calls=%async_computation | async-start | bytes 131072 | tf_op jit(solution)/shard_map/all_to_all | solution.py:786
  18.9 0.3 collective-permute-start.6
  19.2 2.5 %collective-permute-start.7 = (f32[3,72,128]{2,1,0:T(8,128)S(1)}, f32[3,72,128]{2,1,0:T(8,128)S(1)}, u32[]{:S(2)}, u32[]{:S(2)}) collective-permute-start(f32[3,72,128]{2,1,0:T(8,128)S(1)} %get-tuple-element.57), channel_id=1, source_target_pairs={{4,8},{12,16},{20,24},{28,0},{8,4},{16,12},{24,20},{0,28},{5,9},{1... | collective-permute-start | bytes 331784 | tf_op jit(solution)/shard_map/ppermute | solution.py:851
  21.8 0.7 %collective-permute-start.5 = (f32[72,128]{1,0:T(8,128)S(1)}, f32[72,128]{1,0:T(8,128)S(1)}, u32[]{:S(2)}, u32[]{:S(2)}) collective-permute-start(f32[72,128]{1,0:T(8,128)S(1)} %get-tuple-element.52.refs_2_), channel_id=1, source_target_pairs={{1,2},{2,1},{5,6},{6,5},{9,10},{10,9},{13,14},{14,13},{17,18},{18,... | collective-permute-start | bytes 110600 | tf_op jit(solution)/shard_map/ppermute | solution.py:853
  22.4 4.3 %collective-permute-start.4 = (f32[72,128]{1,0:T(8,128)S(1)}, f32[72,128]{1,0:T(8,128)S(1)}, u32[]{:S(2)}, u32[]{:S(2)}) collective-permute-start(f32[72,128]{1,0:T(8,128)S(1)} %get-tuple-element.52.refs_2_), channel_id=1, source_target_pairs={{0,1},{1,0},{2,3},{3,2},{4,5},{5,4},{6,7},{7,6},{8,9},{9,8},{10,11... | collective-permute-start | bytes 110600 | tf_op jit(solution)/shard_map/ppermute | solution.py:852
  26.7 0.0 all-to-all-done.refs_0_
  26.7 0.9 %shard_map.82 = (f32[112,128]{1,0:T(8,128)S(1)}, f32[1,128]{1,0:T(1,128)S(1)}) custom-call(f32[32,4,128]{2,1,0:T(4,128)S(1)} %all-to-all-done.refs_0_), custom_call_target="tpu_custom_call" | custom-call | tf_op jit(solution)/shard_map/pallas_call | solution.py:32
  27.6 0.0 collective-permute-done.6.refs_2_
  27.6 0.0 collective-permute-done.7.refs_3_
  27.6 0.7 %shard_map.83 = (f32[10,72,128]{2,1,0:T(8,128)S(1)}, f32[10,72,128]{2,1,0:T(8,128)S(1)}, f32[16,128]{1,0:T(8,128)S(1)}, f32[4,72,128]{2,1,0:T(8,128)S(1)}) custom-call(f32[32,4,128]{2,1,0:T(4,128)S(1)} %all-to-all-done.refs_0_, f32[1,128]{1,0:T(1,128)S(1)} %get-tuple-element.55.refs_1_.refs_2_, f32[3,72,128]{2,1,0:T(8,128)S(1)} %collective-permute-done.6.refs_2_, ...), custom_call_target="tpu_custom_call" | custom-call | tf_op jit(solution)/shard_map/pallas_call | solution.py:32
  28.3 0.0 collective-permute-done.5.refs_1_
  28.3 0.3 collective-permute-done.4.refs_0_
  28.6 1.7 %shard_map.84 = (f32[32,8,128]{2,1,0:T(8,128)}, f32[8,72,128]{2,1,0:T(8,128)S(1)}, f32[8,72,128]{2,1,0:T(8,128)S(1)}, f32[4,2,72,128]{3,2,1,0:T(8,128)S(1)}) custom-call(f32[72,128]{1,0:T(8,128)S(1)} %collective-permute-done.4.refs_0_, f32[72,128]{1,0:T(8,128)S(1)} %collective-permute-done.5.refs_1_, f32[72,128]{1,0:T(8,128)S(1)} %get-tuple-element.52.refs_2_, ...), custom_call_target="tpu_custom_call" | custom-call | tf_op jit(solution)/shard_map/pallas_call | solution.py:32
  30.3 0.1 collective-permute-start.8
  30.4 2.6 %all-to-all-start.1 = ((f32[32,8,128]{2,1,0:T(8,128)}), f32[32,8,128]{2,1,0:T(8,128)S(1)}, u32[]{:S(2)}, u32[]{:S(2)}) async-start(f32[32,8,128]{2,1,0:T(8,128)} %get-tuple-element.64), calls=%async_computation.1 | async-start | bytes 262144 | tf_op jit(solution)/shard_map/all_to_all | solution.py:786
  33.0 0.0 collective-permute-done.8.near_ref.refs_3_
  33.1 2.7 %collective-permute-start.9 = (f32[4,72,128]{2,1,0:T(8,128)S(1)}, f32[4,72,128]{2,1,0:T(8,128)S(1)}, u32[]{:S(2)}, u32[]{:S(2)}) collective-permute-start(f32[4,72,128]{2,1,0:T(8,128)S(1)} %get-tuple-element.71), channel_id=1, source_target_pairs={{0,24},{4,28},{8,16},{12,20},{16,8},{20,12},{24,0},{28,4},{1,25},{... | collective-permute-start | bytes 442376 | tf_op jit(solution)/shard_map/ppermute | solution.py:895
  35.7 0.6 %collective-permute-start.10 = (f32[4,72,128]{2,1,0:T(8,128)S(1)}, f32[4,72,128]{2,1,0:T(8,128)S(1)}, u32[]{:S(2)}, u32[]{:S(2)}) collective-permute-start(f32[4,72,128]{2,1,0:T(8,128)S(1)} %get-tuple-element.72), channel_id=1, source_target_pairs={{0,16},{4,20},{8,24},{12,28},{16,0},{20,4},{24,8},{28,12},{1,17},{... | collective-permute-start | bytes 442376 | tf_op jit(solution)/shard_map/ppermute | solution.py:895
  36.3 0.3 collective-permute-start.11
  36.6 4.8 %all-to-all-done.1.refs_0_ = f32[32,8,128]{2,1,0:T(8,128)S(1)} async-done(((f32[32,8,128]{2,1,0:T(8,128)}), f32[32,8,128]{2,1,0:T(8,128)S(1)}, u32[]{:S(2)}, u32[]{:S(2)}) %all-to-all-start.1) | async-done | bytes 131104 | tf_op jit(solution)/shard_map/all_to_all | solution.py:786
  41.4 1.6 %shard_map.85 = (f32[560,128]{1,0:T(8,128)}, f32[16,128]{1,0:T(8,128)S(1)}) custom-call(f32[32,8,128]{2,1,0:T(8,128)S(1)} %all-to-all-done.1.refs_0_, f32[112,128]{1,0:T(8,128)S(1)} %get-tuple-element.65.refs_1_, f32[1,128]{1,0:T(1,128)S(1)} %get-tuple-element.55.refs_1_.refs_2_, f32[8,72,128]{2,1,0:T(8,128)S(1)} %get-tuple-element.58.refs_4_.refs_3_, ...), custom_call_target="tpu_custom_call" | custom-call | tf_op jit(solution)/shard_map/pallas_call | solution.py:32
  43.0 0.0 collective-permute-done.9.refs_4_
  43.0 1.3 %collective-permute-done.10.refs_5_ = f32[4,72,128]{2,1,0:T(8,128)S(1)} collective-permute-done((f32[4,72,128]{2,1,0:T(8,128)S(1)}, f32[4,72,128]{2,1,0:T(8,128)S(1)}, u32[]{:S(2)}, u32[]{:S(2)}) %collective-permute-start.10) | collective-permute-done | bytes 147488 | tf_op jit(solution)/shard_map/ppermute | solution.py:895
  44.3 0.0 collective-permute-done.11.refs_6_
  44.3 1.0 %shard_map.87 = f32[560,128]{1,0:T(8,128)} custom-call(f32[16,128]{1,0:T(8,128)S(1)} %get-tuple-element.68.refs_0_, f32[8,72,128]{2,1,0:T(8,128)S(1)} %get-tuple-element.63.refs_10_.smooth_ref.refs_1_, f32[8,72,128]{2,1,0:T(8,128)S(1)} %get-tuple-element.69.second_ref.refs_2_, f32[4,2,72,128]{3,2,1,0:T(8,128)S(1)} %collective-permute-done.8.near_ref.refs_3_, ...), custom_call_target="tpu_custom_call" | custom-call | tf_op jit(solution)/shard_map/pallas_call | solution.py:32
  (3 shorter events, 0.1 us)
Async XLA Ops:
  0.6 1.0 %copy-start = (f32[70,8,128]{2,1,0:T(8,128)S(1)}, f32[70,8,128]{2,1,0:T(8,128)}, u32[]{:S(2)}) copy-start(f32[70,8,128]{2,1,0:T(8,128)} %param.9) | copy-start | bytes 860164
  1.6 0.8 %copy-start.3 = (f32[69]{0:T(128)S(1)}, f32[69]{0:T(128)}, u32[]{:S(2)}) copy-start(f32[69]{0:T(128)} %param.8) | copy-start | bytes 832
  1.6 0.8 %copy-start.4 = (f32[70]{0:T(128)S(1)}, f32[70]{0:T(128)}, u32[]{:S(2)}) copy-start(f32[70]{0:T(128)} %param.10) | copy-start | bytes 844
  1.6 0.8 %copy-start.5 = (f32[70]{0:T(128)S(1)}, f32[70]{0:T(128)}, u32[]{:S(2)}) copy-start(f32[70]{0:T(128)} %param.11) | copy-start | bytes 844
  1.6 6.4 %copy-start.2 = (f32[70,8,128]{2,1,0:T(8,128)S(1)}, f32[70,8,128]{2,1,0:T(8,128)}, u32[]{:S(2)}) copy-start(f32[70,8,128]{2,1,0:T(8,128)} %param.7) | copy-start | bytes 860164
  1.9 6.1 %copy-start.1 = (f32[70,8,128]{2,1,0:T(8,128)S(1)}, f32[70,8,128]{2,1,0:T(8,128)}, u32[]{:S(2)}) copy-start(f32[70,8,128]{2,1,0:T(8,128)} %param.6) | copy-start | bytes 860164
  1.9 1.5 %collective-permute-start = (f32[4,72,128]{2,1,0:T(8,128)S(1)}, f32[4,72,128]{2,1,0:T(8,128)S(1)}, u32[]{:S(2)}, u32[]{:S(2)}) collective-permute-start(f32[4,72,128]{2,1,0:T(8,128)S(1)} %get-tuple-element.39), channel_id=1, source_target_pairs={{0,4},{4,0},{8,12},{12,8},{16,20},{20,16},{24,28},{28,24},{1,5},{5... | collective-permute-start | bytes 442376 | tf_op jit(solution)/shard_map/ppermute | solution.py:795
  3.4 6.5 %collective-permute-start.1 = (f32[2,72,128]{2,1,0:T(8,128)S(1)}, f32[2,72,128]{2,1,0:T(8,128)S(1)}, u32[]{:S(2)}, u32[]{:S(2)}) collective-permute-start(f32[2,72,128]{2,1,0:T(8,128)S(1)} %get-tuple-element.40), channel_id=1, source_target_pairs={{0,24},{4,28},{8,16},{12,20},{16,8},{20,12},{24,0},{28,4},{1,25},{... | collective-permute-start | bytes 221192 | tf_op jit(solution)/shard_map/ppermute | solution.py:798
  7.3 4.4 %collective-permute-start.2 = (f32[2,72,128]{2,1,0:T(8,128)S(1)}, f32[2,72,128]{2,1,0:T(8,128)S(1)}, u32[]{:S(2)}, u32[]{:S(2)}) collective-permute-start(f32[2,72,128]{2,1,0:T(8,128)S(1)} %get-tuple-element.41), channel_id=1, source_target_pairs={{0,16},{4,20},{8,24},{12,28},{16,0},{20,4},{24,8},{28,12},{1,17},{... | collective-permute-start | bytes 221192 | tf_op jit(solution)/shard_map/ppermute | solution.py:798
  7.8 4.4 %collective-permute-start.3 = (f32[2,72,128]{2,1,0:T(8,128)S(1)}, f32[2,72,128]{2,1,0:T(8,128)S(1)}, u32[]{:S(2)}, u32[]{:S(2)}) collective-permute-start(f32[2,72,128]{2,1,0:T(8,128)S(1)} %get-tuple-element.42), channel_id=1, source_target_pairs={{0,8},{4,12},{8,0},{12,4},{16,24},{20,28},{24,16},{28,20},{1,9},{5... | collective-permute-start | bytes 221192 | tf_op jit(solution)/shard_map/ppermute | solution.py:798
  14.0 12.7 %all-to-all-start = ((f32[32,4,128]{2,1,0:T(4,128)}), f32[32,4,128]{2,1,0:T(4,128)S(1)}, u32[]{:S(2)}, u32[]{:S(2)}) async-start(f32[32,4,128]{2,1,0:T(4,128)} %get-tuple-element.54), calls=%async_computation | async-start | bytes 131072 | tf_op jit(solution)/shard_map/all_to_all | solution.py:786
  18.9 8.6 %collective-permute-start.6 = (f32[3,72,128]{2,1,0:T(8,128)S(1)}, f32[3,72,128]{2,1,0:T(8,128)S(1)}, u32[]{:S(2)}, u32[]{:S(2)}) collective-permute-start(f32[3,72,128]{2,1,0:T(8,128)S(1)} %get-tuple-element.56), channel_id=1, source_target_pairs={{0,4},{4,0},{8,12},{12,8},{16,20},{20,16},{24,28},{28,24},{1,5},{5... | collective-permute-start | bytes 331784 | tf_op jit(solution)/shard_map/ppermute | solution.py:850
  19.2 8.3 %collective-permute-start.7 = (f32[3,72,128]{2,1,0:T(8,128)S(1)}, f32[3,72,128]{2,1,0:T(8,128)S(1)}, u32[]{:S(2)}, u32[]{:S(2)}) collective-permute-start(f32[3,72,128]{2,1,0:T(8,128)S(1)} %get-tuple-element.57), channel_id=1, source_target_pairs={{4,8},{12,16},{20,24},{28,0},{8,4},{16,12},{24,20},{0,28},{5,9},{1... | collective-permute-start | bytes 331784 | tf_op jit(solution)/shard_map/ppermute | solution.py:851
  21.8 6.5 %collective-permute-start.5 = (f32[72,128]{1,0:T(8,128)S(1)}, f32[72,128]{1,0:T(8,128)S(1)}, u32[]{:S(2)}, u32[]{:S(2)}) collective-permute-start(f32[72,128]{1,0:T(8,128)S(1)} %get-tuple-element.52.refs_2_), channel_id=1, source_target_pairs={{1,2},{2,1},{5,6},{6,5},{9,10},{10,9},{13,14},{14,13},{17,18},{18,... | collective-permute-start | bytes 110600 | tf_op jit(solution)/shard_map/ppermute | solution.py:853
  22.4 6.2 %collective-permute-start.4 = (f32[72,128]{1,0:T(8,128)S(1)}, f32[72,128]{1,0:T(8,128)S(1)}, u32[]{:S(2)}, u32[]{:S(2)}) collective-permute-start(f32[72,128]{1,0:T(8,128)S(1)} %get-tuple-element.52.refs_2_), channel_id=1, source_target_pairs={{0,1},{1,0},{2,3},{3,2},{4,5},{5,4},{6,7},{7,6},{8,9},{9,8},{10,11... | collective-permute-start | bytes 110600 | tf_op jit(solution)/shard_map/ppermute | solution.py:852
  30.3 2.7 %collective-permute-start.8 = (f32[4,2,72,128]{3,2,1,0:T(8,128)S(1)}, f32[4,2,72,128]{3,2,1,0:T(8,128)S(1)}, u32[]{:S(2)}, u32[]{:S(2)}) collective-permute-start(f32[4,2,72,128]{3,2,1,0:T(8,128)S(1)} %get-tuple-element.70), channel_id=1, source_target_pairs={{0,4},{4,0},{8,12},{12,8},{16,20},{20,16},{24,28},{28,24},{1,5},{5... | collective-permute-start | bytes 884744 | tf_op jit(solution)/shard_map/ppermute | solution.py:891
  30.4 11.0 %all-to-all-start.1 = ((f32[32,8,128]{2,1,0:T(8,128)}), f32[32,8,128]{2,1,0:T(8,128)S(1)}, u32[]{:S(2)}, u32[]{:S(2)}) async-start(f32[32,8,128]{2,1,0:T(8,128)} %get-tuple-element.64), calls=%async_computation.1 | async-start | bytes 262144 | tf_op jit(solution)/shard_map/all_to_all | solution.py:786
  33.1 10.0 %collective-permute-start.9 = (f32[4,72,128]{2,1,0:T(8,128)S(1)}, f32[4,72,128]{2,1,0:T(8,128)S(1)}, u32[]{:S(2)}, u32[]{:S(2)}) collective-permute-start(f32[4,72,128]{2,1,0:T(8,128)S(1)} %get-tuple-element.71), channel_id=1, source_target_pairs={{0,24},{4,28},{8,16},{12,20},{16,8},{20,12},{24,0},{28,4},{1,25},{... | collective-permute-start | bytes 442376 | tf_op jit(solution)/shard_map/ppermute | solution.py:895
  35.7 8.6 %collective-permute-start.10 = (f32[4,72,128]{2,1,0:T(8,128)S(1)}, f32[4,72,128]{2,1,0:T(8,128)S(1)}, u32[]{:S(2)}, u32[]{:S(2)}) collective-permute-start(f32[4,72,128]{2,1,0:T(8,128)S(1)} %get-tuple-element.72), channel_id=1, source_target_pairs={{0,16},{4,20},{8,24},{12,28},{16,0},{20,4},{24,8},{28,12},{1,17},{... | collective-permute-start | bytes 442376 | tf_op jit(solution)/shard_map/ppermute | solution.py:895
  36.3 8.0 %collective-permute-start.11 = (f32[4,72,128]{2,1,0:T(8,128)S(1)}, f32[4,72,128]{2,1,0:T(8,128)S(1)}, u32[]{:S(2)}, u32[]{:S(2)}) collective-permute-start(f32[4,72,128]{2,1,0:T(8,128)S(1)} %get-tuple-element.73), channel_id=1, source_target_pairs={{0,8},{4,12},{8,0},{12,4},{16,24},{20,28},{24,16},{28,20},{1,9},{5... | collective-permute-start | bytes 442376 | tf_op jit(solution)/shard_map/ppermute | solution.py:895

commit v6 on v5

--- a/solution.py
+++ b/solution.py
@@ -200,7 +200,9 @@
     points, padded, across = forced_ref.shape
     inverse = inverse_ref[:, :padded]
     sun = absorbed_ref[...] * cosine_ref[...]
-    forced = [tile + sun for tile in load_columns(forcing_ref, points, levels, padded)]
+    forcing = load_columns(forcing_ref, points, levels, padded)
+    rows_ref[16:24] = add_all([fold(tile) for tile in forcing])
+    forced = [tile + sun for tile in forcing]
     for i, tile in enumerate(dot(inverse, forced)):
         forced_ref[i] = forced[i]
         base_ref[i] = tile
@@ -208,7 +210,9 @@
     for i, tile in enumerate(weight):
         weight_out_ref[i] = tile
     matrices_ref[0:padded] = matrix_ref[...]
-    matrices_ref[padded:] = dot(inverse, [matrix_ref[...]])[0]
+    matrices_ref[padded : 2 * padded] = dot(inverse, [matrix_ref[...]])[0]
+    heated = jnp.sum(fold(matrix_ref[...]), axis=0, keepdims=True)
+    matrices_ref[2 * padded :] = jnp.broadcast_to(heated, (8, across))
     unit_ref[...] = jnp.broadcast_to(
         jnp.sum(inverse_ref[...], axis=1, keepdims=True), unit_ref.shape
     )
@@ -234,16 +238,12 @@
     else:
         kelvin = [kelvin_refs[0][i] for i in range(points)]
     squares = [tile * tile for tile in kelvin]
-    both = dot(matrices_ref[:, :padded], [tile * tile for tile in squares])
-    real = iota((padded, across), 0) < levels
+    emission = [tile * tile for tile in squares]
+    both = dot(matrices_ref[padded:, :padded], emission)
     solar, unit = rows_ref[8:9, :], unit_ref[...]
-    residual, smooth = [], []
+    means = [(tile[padded : padded + 1] + solar) * (1.0 / levels) for tile in both]
+    smooth = [base_ref[i] + (both[i][:padded] - unit * means[i]) for i in range(points)]
     for i in range(points):
-        heat = both[i][:padded]
-        mean = (jnp.sum(fold(heat), axis=0, keepdims=True) + solar) * (1.0 / levels)
-        residual.append(forced_ref[i] + jnp.where(real, heat - mean, 0.0))
-        smooth.append(base_ref[i] + (both[i][padded:] - unit * mean))
-        residual_ref[i] = residual[i]
         smooth_ref[i] = smooth[i]
     weight = [weight_ref[i] for i in range(points)]
     folded = [fold(tile) for tile in smooth]
@@ -253,7 +253,7 @@
     lane = iota(every.shape, 1)
     scalars = scalars_row(
         [
-            add_all([fold(tile) for tile in residual]) - loss,
+            rows_ref[16:24, :] - loss,
             folded[0],
             folded[-1],
             jnp.where(lane == 0, every, 0.0),
@@ -274,6 +274,10 @@
     send = pltpu.make_async_copy(message_ref, sent_ref, message_sem.at[0])
     send.start()
 
+    heat = dot(matrices_ref[:padded, :padded], emission)
+    real = iota((padded, across), 0) < levels
+    for i in range(points):
+        residual_ref[i] = forced_ref[i] + jnp.where(real, heat[i] - means[i], 0.0)
     stride = across // points
     rim = jnp.zeros((padded, across), F32)
     for i in range(points):
@@ -819,7 +823,7 @@
     weights = shift_weights.reshape(flat)
     forced, weights, *prepared = call(
         part(prepare_kernel, levels),
-        [field, field, field, (2 * padded, across), (16, across), (padded, across)],
+        [field, field, field, (2 * padded + 8, across), (24, across), (padded, across)],
         forcing,
         weights,
         inverse,

time: 45.6 us -> 45.4 us (level)
  no operation moved by 1% of the time
where the time goes in v6:
time: 45.4 us; the launch traced here: 45.1 us
  starting transfers between devices  23.9 us (53%)
  waiting for transfers between devices  10.6 us (23%)
  Pallas kernels  8.73 us (19%)
  local copies, waits for them, and re-layouts  0.97 us (2%)
  between operations  0.78 us (2%)
    pallas_call x11, Pallas kernels, call(): pl.pallas_call(kernel, out_shape=[jax.ShapeDtypeStruct(shape, F32) for sh...  8.73 us
    ppermute x6, starting transfers between devices, per_device(): lax.ppermute(value, 'tile', [(i, i ^ step) for i in range(tiles)])  8.07 us
    all_to_all x2, starting transfers between devices, gather(): lax.all_to_all(value, ('tile', 'grp'), split_axis=0, concat_axis=0, tiled...  7.52 us
    ppermute x6, waiting for transfers between devices, per_device(): lax.ppermute(value, 'tile', [(i, i ^ step) for i in range(tiles)])  4.92 us
    all_to_all x2, waiting for transfers between devices, gather(): lax.all_to_all(value, ('tile', 'grp'), split_axis=0, concat_axis=0, tiled...  4.79 us
    ppermute x1, starting transfers between devices, per_device(): low = lax.ppermute(rim, 'grp', inner_pairs(groups))  4.27 us
    ppermute x1, starting transfers between devices, per_device(): outer = lax.ppermute(outer, 'tile', outer_pairs(tiles, True))  2.53 us
    unnamed x12, local copies, waits for them, and re-layouts  0.97 us
  transfers between devices with their start and end apart: 14, of which 7 were waited for; matrix products, arithmetic and copies ran while one was open for 0% of the time, Pallas kernels for 9%

profile of v6, /device:TPU:0, one launch (start us, length us, event | category | flops | bytes accessed | tf_op | source)
XLA Modules:
  0.0 45.1 jit_solution(15266919957609174650)
XLA Ops:
  0.6 0.0 copy-start
  0.6 0.9 %copy-done = f32[70,8,128]{2,1,0:T(8,128)S(1)} copy-done((f32[70,8,128]{2,1,0:T(8,128)S(1)}, f32[70,8,128]{2,1,0:T(8,128)}, u32[]{:S(2)}) %copy-start) | copy-done | bytes 286744
  1.6 0.0 copy-start.3
  1.6 0.0 copy-start.4
  1.6 0.0 copy-start.5
  1.6 0.0 copy-start.2
  1.6 0.3 shard_map.77
  1.9 0.0 copy-start.1
  1.9 0.5 %collective-permute-start = (f32[4,72,128]{2,1,0:T(8,128)S(1)}, f32[4,72,128]{2,1,0:T(8,128)S(1)}, u32[]{:S(2)}, u32[]{:S(2)}) collective-permute-start(f32[4,72,128]{2,1,0:T(8,128)S(1)} %get-tuple-element.39), channel_id=1, source_target_pairs={{0,4},{4,0},{8,12},{12,8},{16,20},{20,16},{24,28},{28,24},{1,5},{5... | collective-permute-start | bytes 442376 | tf_op jit(solution)/shard_map/ppermute | solution.py:799
  2.4 0.0 copy-done.3
  2.4 0.0 copy-done.4
  2.4 0.0 copy-done.5
  2.4 0.4 shard_map.79
  2.8 0.6 %collective-permute-done.near_ref.refs_1_ = f32[4,72,128]{2,1,0:T(8,128)S(1)} collective-permute-done((f32[4,72,128]{2,1,0:T(8,128)S(1)}, f32[4,72,128]{2,1,0:T(8,128)S(1)}, u32[]{:S(2)}, u32[]{:S(2)}) %collective-permute-start) | collective-permute-done | bytes 147488 | tf_op jit(solution)/shard_map/ppermute | solution.py:799
  3.4 3.9 %collective-permute-start.1 = (f32[2,72,128]{2,1,0:T(8,128)S(1)}, f32[2,72,128]{2,1,0:T(8,128)S(1)}, u32[]{:S(2)}, u32[]{:S(2)}) collective-permute-start(f32[2,72,128]{2,1,0:T(8,128)S(1)} %get-tuple-element.40), channel_id=1, source_target_pairs={{0,24},{4,28},{8,16},{12,20},{16,8},{20,12},{24,0},{28,4},{1,25},{... | collective-permute-start | bytes 221192 | tf_op jit(solution)/shard_map/ppermute | solution.py:802
  7.3 0.5 %collective-permute-start.2 = (f32[2,72,128]{2,1,0:T(8,128)S(1)}, f32[2,72,128]{2,1,0:T(8,128)S(1)}, u32[]{:S(2)}, u32[]{:S(2)}) collective-permute-start(f32[2,72,128]{2,1,0:T(8,128)S(1)} %get-tuple-element.41), channel_id=1, source_target_pairs={{0,16},{4,20},{8,24},{12,28},{16,0},{20,4},{24,8},{28,12},{1,17},{... | collective-permute-start | bytes 221192 | tf_op jit(solution)/shard_map/ppermute | solution.py:802
  7.8 0.1 collective-permute-start.3
  8.0 0.0 copy-done.2
  8.0 0.0 copy-done.1
  8.0 0.5 %shard_map.80 = (f32[8,72,128]{2,1,0:T(8,128)S(1)}, f32[8,72,128]{2,1,0:T(8,128)S(1)}, f32[8,72,128]{2,1,0:T(8,128)S(1)}, f32[152,128]{1,0:T(8,128)S(1)}, f32[24,128]{1,0:T(8,128)S(1)}, /*index=5*/f32[72,128]{1,0:T(8,128)S(1)}) custom-call(f32[560,128]{1,0:T(8,128)S(1)} %bitcast.9, f32[560,128]{1,0:T(8,128)S(1)} %bitcast.10, ...), custom_call_target="tpu_custom_call" | custom-call | tf_op jit(solution)/shard_map/pallas_call | solution.py:32
  8.5 1.4 %collective-permute-done.1.refs_2_ = f32[2,72,128]{2,1,0:T(8,128)S(1)} collective-permute-done((f32[2,72,128]{2,1,0:T(8,128)S(1)}, f32[2,72,128]{2,1,0:T(8,128)S(1)}, u32[]{:S(2)}, u32[]{:S(2)}) %collective-permute-start.1) | collective-permute-done | bytes 73760 | tf_op jit(solution)/shard_map/ppermute | solution.py:802
  10.0 1.7 %collective-permute-done.2.refs_3_ = f32[2,72,128]{2,1,0:T(8,128)S(1)} collective-permute-done((f32[2,72,128]{2,1,0:T(8,128)S(1)}, f32[2,72,128]{2,1,0:T(8,128)S(1)}, u32[]{:S(2)}, u32[]{:S(2)}) %collective-permute-start.2) | collective-permute-done | bytes 73760 | tf_op jit(solution)/shard_map/ppermute | solution.py:802
  11.7 0.5 %collective-permute-done.3.refs_4_ = f32[2,72,128]{2,1,0:T(8,128)S(1)} collective-permute-done((f32[2,72,128]{2,1,0:T(8,128)S(1)}, f32[2,72,128]{2,1,0:T(8,128)S(1)}, u32[]{:S(2)}, u32[]{:S(2)}) %collective-permute-start.3) | collective-permute-done | bytes 73760 | tf_op jit(solution)/shard_map/ppermute | solution.py:802
  12.2 1.6 %shard_map.81 = (f32[32,4,128]{2,1,0:T(4,128)}, f32[8,72,128]{2,1,0:T(8,128)S(1)}, f32[8,72,128]{2,1,0:T(8,128)S(1)}, f32[72,128]{1,0:T(8,128)S(1)}, f32[3,72,12...) custom-call(f32[8,72,128]{2,1,0:T(8,128)S(1)} %get-tuple-element.38.packed_ref.refs_0_, ...), custom_call_target="tpu_custom_call" | custom-call | tf_op jit(solution)/shard_map/pallas_call | solution.py:32
  13.8 4.9 %all-to-all-start = ((f32[32,4,128]{2,1,0:T(4,128)}), f32[32,4,128]{2,1,0:T(4,128)S(1)}, u32[]{:S(2)}, u32[]{:S(2)}) async-start(f32[32,4,128]{2,1,0:T(4,128)} %get-tuple-element.54), calls=%async_computation | async-start | bytes 131072 | tf_op jit(solution)/shard_map/all_to_all | solution.py:790
  18.7 0.3 collective-permute-start.6
  19.0 2.5 %collective-permute-start.7 = (f32[3,72,128]{2,1,0:T(8,128)S(1)}, f32[3,72,128]{2,1,0:T(8,128)S(1)}, u32[]{:S(2)}, u32[]{:S(2)}) collective-permute-start(f32[3,72,128]{2,1,0:T(8,128)S(1)} %get-tuple-element.57), channel_id=1, source_target_pairs={{4,8},{12,16},{20,24},{28,0},{8,4},{16,12},{24,20},{0,28},{5,9},{1... | collective-permute-start | bytes 331784 | tf_op jit(solution)/shard_map/ppermute | solution.py:855
  21.6 0.7 %collective-permute-start.5 = (f32[72,128]{1,0:T(8,128)S(1)}, f32[72,128]{1,0:T(8,128)S(1)}, u32[]{:S(2)}, u32[]{:S(2)}) collective-permute-start(f32[72,128]{1,0:T(8,128)S(1)} %get-tuple-element.52.refs_2_), channel_id=1, source_target_pairs={{1,2},{2,1},{5,6},{6,5},{9,10},{10,9},{13,14},{14,13},{17,18},{18,... | collective-permute-start | bytes 110600 | tf_op jit(solution)/shard_map/ppermute | solution.py:857
  22.2 4.3 %collective-permute-start.4 = (f32[72,128]{1,0:T(8,128)S(1)}, f32[72,128]{1,0:T(8,128)S(1)}, u32[]{:S(2)}, u32[]{:S(2)}) collective-permute-start(f32[72,128]{1,0:T(8,128)S(1)} %get-tuple-element.52.refs_2_), channel_id=1, source_target_pairs={{0,1},{1,0},{2,3},{3,2},{4,5},{5,4},{6,7},{7,6},{8,9},{9,8},{10,11... | collective-permute-start | bytes 110600 | tf_op jit(solution)/shard_map/ppermute | solution.py:856
  26.5 0.0 all-to-all-done.refs_0_
  26.5 0.9 %shard_map.82 = (f32[112,128]{1,0:T(8,128)S(1)}, f32[1,128]{1,0:T(1,128)S(1)}) custom-call(f32[32,4,128]{2,1,0:T(4,128)S(1)} %all-to-all-done.refs_0_), custom_call_target="tpu_custom_call" | custom-call | tf_op jit(solution)/shard_map/pallas_call | solution.py:32
  27.4 0.0 collective-permute-done.6.refs_2_
  27.4 0.0 collective-permute-done.7.refs_3_
  27.4 0.7 %shard_map.83 = (f32[10,72,128]{2,1,0:T(8,128)S(1)}, f32[10,72,128]{2,1,0:T(8,128)S(1)}, f32[16,128]{1,0:T(8,128)S(1)}, f32[4,72,128]{2,1,0:T(8,128)S(1)}) custom-call(f32[32,4,128]{2,1,0:T(4,128)S(1)} %all-to-all-done.refs_0_, f32[1,128]{1,0:T(1,128)S(1)} %get-tuple-element.55.refs_1_.refs_2_, f32[3,72,128]{2,1,0:T(8,128)S(1)} %collective-permute-done.6.refs_2_, ...), custom_call_target="tpu_custom_call" | custom-call | tf_op jit(solution)/shard_map/pallas_call | solution.py:32
  28.1 0.0 collective-permute-done.5.refs_1_
  28.1 0.3 collective-permute-done.4.refs_0_
  28.4 1.7 %shard_map.84 = (f32[32,8,128]{2,1,0:T(8,128)}, f32[8,72,128]{2,1,0:T(8,128)S(1)}, f32[8,72,128]{2,1,0:T(8,128)S(1)}, f32[4,2,72,128]{3,2,1,0:T(8,128)S(1)}) custom-call(f32[72,128]{1,0:T(8,128)S(1)} %collective-permute-done.4.refs_0_, f32[72,128]{1,0:T(8,128)S(1)} %collective-permute-done.5.refs_1_, f32[72,128]{1,0:T(8,128)S(1)} %get-tuple-element.52.refs_2_, ...), custom_call_target="tpu_custom_call" | custom-call | tf_op jit(solution)/shard_map/pallas_call | solution.py:32
  30.1 0.1 collective-permute-start.8
  30.2 2.6 %all-to-all-start.1 = ((f32[32,8,128]{2,1,0:T(8,128)}), f32[32,8,128]{2,1,0:T(8,128)S(1)}, u32[]{:S(2)}, u32[]{:S(2)}) async-start(f32[32,8,128]{2,1,0:T(8,128)} %get-tuple-element.64), calls=%async_computation.1 | async-start | bytes 262144 | tf_op jit(solution)/shard_map/all_to_all | solution.py:790
  32.8 0.0 collective-permute-done.8.near_ref.refs_3_
  32.9 2.7 %collective-permute-start.9 = (f32[4,72,128]{2,1,0:T(8,128)S(1)}, f32[4,72,128]{2,1,0:T(8,128)S(1)}, u32[]{:S(2)}, u32[]{:S(2)}) collective-permute-start(f32[4,72,128]{2,1,0:T(8,128)S(1)} %get-tuple-element.71), channel_id=1, source_target_pairs={{0,24},{4,28},{8,16},{12,20},{16,8},{20,12},{24,0},{28,4},{1,25},{... | collective-permute-start | bytes 442376 | tf_op jit(solution)/shard_map/ppermute | solution.py:899
  35.5 0.6 %collective-permute-start.10 = (f32[4,72,128]{2,1,0:T(8,128)S(1)}, f32[4,72,128]{2,1,0:T(8,128)S(1)}, u32[]{:S(2)}, u32[]{:S(2)}) collective-permute-start(f32[4,72,128]{2,1,0:T(8,128)S(1)} %get-tuple-element.72), channel_id=1, source_target_pairs={{0,16},{4,20},{8,24},{12,28},{16,0},{20,4},{24,8},{28,12},{1,17},{... | collective-permute-start | bytes 442376 | tf_op jit(solution)/shard_map/ppermute | solution.py:899
  36.1 0.3 collective-permute-start.11
  36.4 4.8 %all-to-all-done.1.refs_0_ = f32[32,8,128]{2,1,0:T(8,128)S(1)} async-done(((f32[32,8,128]{2,1,0:T(8,128)}), f32[32,8,128]{2,1,0:T(8,128)S(1)}, u32[]{:S(2)}, u32[]{:S(2)}) %all-to-all-start.1) | async-done | bytes 131104 | tf_op jit(solution)/shard_map/all_to_all | solution.py:790
  41.2 1.6 %shard_map.85 = (f32[560,128]{1,0:T(8,128)}, f32[16,128]{1,0:T(8,128)S(1)}) custom-call(f32[32,8,128]{2,1,0:T(8,128)S(1)} %all-to-all-done.1.refs_0_, f32[112,128]{1,0:T(8,128)S(1)} %get-tuple-element.65.refs_1_, f32[1,128]{1,0:T(1,128)S(1)} %get-tuple-element.55.refs_1_.refs_2_, f32[8,72,128]{2,1,0:T(8,128)S(1)} %get-tuple-element.58.refs_4_.refs_3_, ...), custom_call_target="tpu_custom_call" | custom-call | tf_op jit(solution)/shard_map/pallas_call | solution.py:32
  42.8 0.0 collective-permute-done.9.refs_4_
  42.8 1.3 %collective-permute-done.10.refs_5_ = f32[4,72,128]{2,1,0:T(8,128)S(1)} collective-permute-done((f32[4,72,128]{2,1,0:T(8,128)S(1)}, f32[4,72,128]{2,1,0:T(8,128)S(1)}, u32[]{:S(2)}, u32[]{:S(2)}) %collective-permute-start.10) | collective-permute-done | bytes 147488 | tf_op jit(solution)/shard_map/ppermute | solution.py:899
  44.1 0.0 collective-permute-done.11.refs_6_
  44.1 1.0 %shard_map.87 = f32[560,128]{1,0:T(8,128)} custom-call(f32[16,128]{1,0:T(8,128)S(1)} %get-tuple-element.68.refs_0_, f32[8,72,128]{2,1,0:T(8,128)S(1)} %get-tuple-element.63.refs_10_.smooth_ref.refs_1_, f32[8,72,128]{2,1,0:T(8,128)S(1)} %get-tuple-element.69.second_ref.refs_2_, f32[4,2,72,128]{3,2,1,0:T(8,128)S(1)} %collective-permute-done.8.near_ref.refs_3_, ...), custom_call_target="tpu_custom_call" | custom-call | tf_op jit(solution)/shard_map/pallas_call | solution.py:32
  (3 shorter events, 0.1 us)
Async XLA Ops:
  0.6 1.0 %copy-start = (f32[70,8,128]{2,1,0:T(8,128)S(1)}, f32[70,8,128]{2,1,0:T(8,128)}, u32[]{:S(2)}) copy-start(f32[70,8,128]{2,1,0:T(8,128)} %param.9) | copy-start | bytes 860164
  1.6 0.8 %copy-start.3 = (f32[69]{0:T(128)S(1)}, f32[69]{0:T(128)}, u32[]{:S(2)}) copy-start(f32[69]{0:T(128)} %param.8) | copy-start | bytes 832
  1.6 0.8 %copy-start.4 = (f32[70]{0:T(128)S(1)}, f32[70]{0:T(128)}, u32[]{:S(2)}) copy-start(f32[70]{0:T(128)} %param.10) | copy-start | bytes 844
  1.6 0.8 %copy-start.5 = (f32[70]{0:T(128)S(1)}, f32[70]{0:T(128)}, u32[]{:S(2)}) copy-start(f32[70]{0:T(128)} %param.11) | copy-start | bytes 844
  1.6 6.4 %copy-start.2 = (f32[70,8,128]{2,1,0:T(8,128)S(1)}, f32[70,8,128]{2,1,0:T(8,128)}, u32[]{:S(2)}) copy-start(f32[70,8,128]{2,1,0:T(8,128)} %param.7) | copy-start | bytes 860164
  1.9 6.1 %copy-start.1 = (f32[70,8,128]{2,1,0:T(8,128)S(1)}, f32[70,8,128]{2,1,0:T(8,128)}, u32[]{:S(2)}) copy-start(f32[70,8,128]{2,1,0:T(8,128)} %param.6) | copy-start | bytes 860164
  1.9 1.5 %collective-permute-start = (f32[4,72,128]{2,1,0:T(8,128)S(1)}, f32[4,72,128]{2,1,0:T(8,128)S(1)}, u32[]{:S(2)}, u32[]{:S(2)}) collective-permute-start(f32[4,72,128]{2,1,0:T(8,128)S(1)} %get-tuple-element.39), channel_id=1, source_target_pairs={{0,4},{4,0},{8,12},{12,8},{16,20},{20,16},{24,28},{28,24},{1,5},{5... | collective-permute-start | bytes 442376 | tf_op jit(solution)/shard_map/ppermute | solution.py:799
  3.4 6.5 %collective-permute-start.1 = (f32[2,72,128]{2,1,0:T(8,128)S(1)}, f32[2,72,128]{2,1,0:T(8,128)S(1)}, u32[]{:S(2)}, u32[]{:S(2)}) collective-permute-start(f32[2,72,128]{2,1,0:T(8,128)S(1)} %get-tuple-element.40), channel_id=1, source_target_pairs={{0,24},{4,28},{8,16},{12,20},{16,8},{20,12},{24,0},{28,4},{1,25},{... | collective-permute-start | bytes 221192 | tf_op jit(solution)/shard_map/ppermute | solution.py:802
  7.3 4.4 %collective-permute-start.2 = (f32[2,72,128]{2,1,0:T(8,128)S(1)}, f32[2,72,128]{2,1,0:T(8,128)S(1)}, u32[]{:S(2)}, u32[]{:S(2)}) collective-permute-start(f32[2,72,128]{2,1,0:T(8,128)S(1)} %get-tuple-element.41), channel_id=1, source_target_pairs={{0,16},{4,20},{8,24},{12,28},{16,0},{20,4},{24,8},{28,12},{1,17},{... | collective-permute-start | bytes 221192 | tf_op jit(solution)/shard_map/ppermute | solution.py:802
  7.8 4.4 %collective-permute-start.3 = (f32[2,72,128]{2,1,0:T(8,128)S(1)}, f32[2,72,128]{2,1,0:T(8,128)S(1)}, u32[]{:S(2)}, u32[]{:S(2)}) collective-permute-start(f32[2,72,128]{2,1,0:T(8,128)S(1)} %get-tuple-element.42), channel_id=1, source_target_pairs={{0,8},{4,12},{8,0},{12,4},{16,24},{20,28},{24,16},{28,20},{1,9},{5... | collective-permute-start | bytes 221192 | tf_op jit(solution)/shard_map/ppermute | solution.py:802
  13.8 12.7 %all-to-all-start = ((f32[32,4,128]{2,1,0:T(4,128)}), f32[32,4,128]{2,1,0:T(4,128)S(1)}, u32[]{:S(2)}, u32[]{:S(2)}) async-start(f32[32,4,128]{2,1,0:T(4,128)} %get-tuple-element.54), calls=%async_computation | async-start | bytes 131072 | tf_op jit(solution)/shard_map/all_to_all | solution.py:790
  18.7 8.6 %collective-permute-start.6 = (f32[3,72,128]{2,1,0:T(8,128)S(1)}, f32[3,72,128]{2,1,0:T(8,128)S(1)}, u32[]{:S(2)}, u32[]{:S(2)}) collective-permute-start(f32[3,72,128]{2,1,0:T(8,128)S(1)} %get-tuple-element.56), channel_id=1, source_target_pairs={{0,4},{4,0},{8,12},{12,8},{16,20},{20,16},{24,28},{28,24},{1,5},{5... | collective-permute-start | bytes 331784 | tf_op jit(solution)/shard_map/ppermute | solution.py:854
  19.0 8.3 %collective-permute-start.7 = (f32[3,72,128]{2,1,0:T(8,128)S(1)}, f32[3,72,128]{2,1,0:T(8,128)S(1)}, u32[]{:S(2)}, u32[]{:S(2)}) collective-permute-start(f32[3,72,128]{2,1,0:T(8,128)S(1)} %get-tuple-element.57), channel_id=1, source_target_pairs={{4,8},{12,16},{20,24},{28,0},{8,4},{16,12},{24,20},{0,28},{5,9},{1... | collective-permute-start | bytes 331784 | tf_op jit(solution)/shard_map/ppermute | solution.py:855
  21.6 6.5 %collective-permute-start.5 = (f32[72,128]{1,0:T(8,128)S(1)}, f32[72,128]{1,0:T(8,128)S(1)}, u32[]{:S(2)}, u32[]{:S(2)}) collective-permute-start(f32[72,128]{1,0:T(8,128)S(1)} %get-tuple-element.52.refs_2_), channel_id=1, source_target_pairs={{1,2},{2,1},{5,6},{6,5},{9,10},{10,9},{13,14},{14,13},{17,18},{18,... | collective-permute-start | bytes 110600 | tf_op jit(solution)/shard_map/ppermute | solution.py:857
  22.2 6.2 %collective-permute-start.4 = (f32[72,128]{1,0:T(8,128)S(1)}, f32[72,128]{1,0:T(8,128)S(1)}, u32[]{:S(2)}, u32[]{:S(2)}) collective-permute-start(f32[72,128]{1,0:T(8,128)S(1)} %get-tuple-element.52.refs_2_), channel_id=1, source_target_pairs={{0,1},{1,0},{2,3},{3,2},{4,5},{5,4},{6,7},{7,6},{8,9},{9,8},{10,11... | collective-permute-start | bytes 110600 | tf_op jit(solution)/shard_map/ppermute | solution.py:856
  30.1 2.7 %collective-permute-start.8 = (f32[4,2,72,128]{3,2,1,0:T(8,128)S(1)}, f32[4,2,72,128]{3,2,1,0:T(8,128)S(1)}, u32[]{:S(2)}, u32[]{:S(2)}) collective-permute-start(f32[4,2,72,128]{3,2,1,0:T(8,128)S(1)} %get-tuple-element.70), channel_id=1, source_target_pairs={{0,4},{4,0},{8,12},{12,8},{16,20},{20,16},{24,28},{28,24},{1,5},{5... | collective-permute-start | bytes 884744 | tf_op jit(solution)/shard_map/ppermute | solution.py:895
  30.2 11.0 %all-to-all-start.1 = ((f32[32,8,128]{2,1,0:T(8,128)}), f32[32,8,128]{2,1,0:T(8,128)S(1)}, u32[]{:S(2)}, u32[]{:S(2)}) async-start(f32[32,8,128]{2,1,0:T(8,128)} %get-tuple-element.64), calls=%async_computation.1 | async-start | bytes 262144 | tf_op jit(solution)/shard_map/all_to_all | solution.py:790
  32.9 10.0 %collective-permute-start.9 = (f32[4,72,128]{2,1,0:T(8,128)S(1)}, f32[4,72,128]{2,1,0:T(8,128)S(1)}, u32[]{:S(2)}, u32[]{:S(2)}) collective-permute-start(f32[4,72,128]{2,1,0:T(8,128)S(1)} %get-tuple-element.71), channel_id=1, source_target_pairs={{0,24},{4,28},{8,16},{12,20},{16,8},{20,12},{24,0},{28,4},{1,25},{... | collective-permute-start | bytes 442376 | tf_op jit(solution)/shard_map/ppermute | solution.py:899
  35.5 8.6 %collective-permute-start.10 = (f32[4,72,128]{2,1,0:T(8,128)S(1)}, f32[4,72,128]{2,1,0:T(8,128)S(1)}, u32[]{:S(2)}, u32[]{:S(2)}) collective-permute-start(f32[4,72,128]{2,1,0:T(8,128)S(1)} %get-tuple-element.72), channel_id=1, source_target_pairs={{0,16},{4,20},{8,24},{12,28},{16,0},{20,4},{24,8},{28,12},{1,17},{... | collective-permute-start | bytes 442376 | tf_op jit(solution)/shard_map/ppermute | solution.py:899
  36.1 8.0 %collective-permute-start.11 = (f32[4,72,128]{2,1,0:T(8,128)S(1)}, f32[4,72,128]{2,1,0:T(8,128)S(1)}, u32[]{:S(2)}, u32[]{:S(2)}) collective-permute-start(f32[4,72,128]{2,1,0:T(8,128)S(1)} %get-tuple-element.73), channel_id=1, source_target_pairs={{0,8},{4,12},{8,0},{12,4},{16,24},{20,28},{24,16},{28,20},{1,9},{5... | collective-permute-start | bytes 442376 | tf_op jit(solution)/shard_map/ppermute | solution.py:899

commit v7 on v6

--- a/solution.py
+++ b/solution.py
@@ -42,17 +42,22 @@
 
 def load_columns(ref, points, levels, padded):
     tiles = []
+    whole = levels // 8 * 8
     for i in range(points):
-        tile = ref[pl.ds(i, levels, stride=points), :]
+        parts = [ref[pl.ds(i, whole, stride=points), :]]
         if padded > levels:
-            tile = jnp.concatenate([tile, jnp.zeros((padded - levels, tile.shape[1]), F32)], axis=0)
-        tiles.append(tile)
+            last = ref[pl.ds((levels - 8) * points + i, 8, stride=points), :]
+            parts += [last[8 - (levels - whole) :], jnp.zeros((padded - levels, last.shape[1]), F32)]
+        tiles.append(jnp.concatenate(parts, axis=0))
     return tiles
 
 
 def store_columns(ref, tiles, levels):
+    points, whole = len(tiles), levels // 8 * 8
     for i, tile in enumerate(tiles):
-        ref[pl.ds(i, levels, stride=len(tiles)), :] = tile[:levels]
+        ref[pl.ds(i, whole, stride=points), :] = tile[:whole]
+        if whole < levels:
+            ref[pl.ds((levels - 8) * points + i, 8, stride=points), :] = tile[levels - 8 : levels]
 
 
 def swap_groups(tiles):
@@ -910,7 +915,7 @@
         (state,) = call(part(state_kernel, levels), [flat], state, *parts, scratch=[field])
     if not swap:
         state = state[:, :levels].reshape(points, levels, tiles, width).transpose(2, 1, 0, 3)
-        state = to_tiles(state).transpose(2, 1, 0, 3)
+        state = to_tiles(state).transpose(1, 2, 0, 3)
     shape = (levels, points, across)
     return solution_field.reshape(shape), state.reshape(shape)
 

time: 45.4 us -> 45.4 us (level)
  no operation moved by 1% of the time
where the time goes in v7:
time: 45.4 us; the launch traced here: 45.1 us
  starting transfers between devices  23.9 us (53%)
  waiting for transfers between devices  10.7 us (24%)
  Pallas kernels  8.73 us (19%)
  local copies, waits for them, and re-layouts  0.97 us (2%)
  between operations  0.78 us (2%)
    pallas_call x11, Pallas kernels, call(): pl.pallas_call(kernel, out_shape=[jax.ShapeDtypeStruct(shape, F32) for sh...  8.73 us
    ppermute x6, starting transfers between devices, per_device(): lax.ppermute(value, 'tile', [(i, i ^ step) for i in range(tiles)])  8.07 us
    all_to_all x2, starting transfers between devices, gather(): lax.all_to_all(value, ('tile', 'grp'), split_axis=0, concat_axis=0, tiled...  7.51 us
    ppermute x6, waiting for transfers between devices, per_device(): lax.ppermute(value, 'tile', [(i, i ^ step) for i in range(tiles)])  4.93 us
    all_to_all x2, waiting for transfers between devices, gather(): lax.all_to_all(value, ('tile', 'grp'), split_axis=0, concat_axis=0, tiled...  4.79 us
    ppermute x1, starting transfers between devices, per_device(): low = lax.ppermute(rim, 'grp', inner_pairs(groups))  4.27 us
    ppermute x1, starting transfers between devices, per_device(): outer = lax.ppermute(outer, 'tile', outer_pairs(tiles, True))  2.53 us
    unnamed x12, local copies, waits for them, and re-layouts  0.97 us
  transfers between devices with their start and end apart: 14, of which 7 were waited for; matrix products, arithmetic and copies ran while one was open for 0% of the time, Pallas kernels for 9%

profile of v7, /device:TPU:0, one launch (start us, length us, event | category | flops | bytes accessed | tf_op | source)
XLA Modules:
  0.0 45.1 jit_solution(1843867372298063951)
XLA Ops:
  0.6 0.0 copy-start
  0.6 0.9 %copy-done = f32[70,8,128]{2,1,0:T(8,128)S(1)} copy-done((f32[70,8,128]{2,1,0:T(8,128)S(1)}, f32[70,8,128]{2,1,0:T(8,128)}, u32[]{:S(2)}) %copy-start) | copy-done | bytes 286744
  1.6 0.0 copy-start.3
  1.6 0.0 copy-start.4
  1.6 0.0 copy-start.5
  1.6 0.0 copy-start.2
  1.6 0.3 shard_map.77
  1.9 0.0 copy-start.1
  1.9 0.5 %collective-permute-start = (f32[4,72,128]{2,1,0:T(8,128)S(1)}, f32[4,72,128]{2,1,0:T(8,128)S(1)}, u32[]{:S(2)}, u32[]{:S(2)}) collective-permute-start(f32[4,72,128]{2,1,0:T(8,128)S(1)} %get-tuple-element.39), channel_id=1, source_target_pairs={{0,4},{4,0},{8,12},{12,8},{16,20},{20,16},{24,28},{28,24},{1,5},{5... | collective-permute-start | bytes 442376 | tf_op jit(solution)/shard_map/ppermute | solution.py:804
  2.4 0.0 copy-done.3
  2.4 0.0 copy-done.4
  2.4 0.0 copy-done.5
  2.4 0.4 shard_map.79
  2.8 0.6 %collective-permute-done.near_ref.refs_1_ = f32[4,72,128]{2,1,0:T(8,128)S(1)} collective-permute-done((f32[4,72,128]{2,1,0:T(8,128)S(1)}, f32[4,72,128]{2,1,0:T(8,128)S(1)}, u32[]{:S(2)}, u32[]{:S(2)}) %collective-permute-start) | collective-permute-done | bytes 147488 | tf_op jit(solution)/shard_map/ppermute | solution.py:804
  3.4 3.9 %collective-permute-start.1 = (f32[2,72,128]{2,1,0:T(8,128)S(1)}, f32[2,72,128]{2,1,0:T(8,128)S(1)}, u32[]{:S(2)}, u32[]{:S(2)}) collective-permute-start(f32[2,72,128]{2,1,0:T(8,128)S(1)} %get-tuple-element.40), channel_id=1, source_target_pairs={{0,24},{4,28},{8,16},{12,20},{16,8},{20,12},{24,0},{28,4},{1,25},{... | collective-permute-start | bytes 221192 | tf_op jit(solution)/shard_map/ppermute | solution.py:807
  7.3 0.5 %collective-permute-start.2 = (f32[2,72,128]{2,1,0:T(8,128)S(1)}, f32[2,72,128]{2,1,0:T(8,128)S(1)}, u32[]{:S(2)}, u32[]{:S(2)}) collective-permute-start(f32[2,72,128]{2,1,0:T(8,128)S(1)} %get-tuple-element.41), channel_id=1, source_target_pairs={{0,16},{4,20},{8,24},{12,28},{16,0},{20,4},{24,8},{28,12},{1,17},{... | collective-permute-start | bytes 221192 | tf_op jit(solution)/shard_map/ppermute | solution.py:807
  7.8 0.1 collective-permute-start.3
  8.0 0.0 copy-done.2
  8.0 0.0 copy-done.1
  8.0 0.5 %shard_map.80 = (f32[8,72,128]{2,1,0:T(8,128)S(1)}, f32[8,72,128]{2,1,0:T(8,128)S(1)}, f32[8,72,128]{2,1,0:T(8,128)S(1)}, f32[152,128]{1,0:T(8,128)S(1)}, f32[24,128]{1,0:T(8,128)S(1)}, /*index=5*/f32[72,128]{1,0:T(8,128)S(1)}) custom-call(f32[560,128]{1,0:T(8,128)S(1)} %bitcast.9, f32[560,128]{1,0:T(8,128)S(1)} %bitcast.10, ...), custom_call_target="tpu_custom_call" | custom-call | tf_op jit(solution)/shard_map/pallas_call | solution.py:32
  8.5 1.4 %collective-permute-done.1.refs_2_ = f32[2,72,128]{2,1,0:T(8,128)S(1)} collective-permute-done((f32[2,72,128]{2,1,0:T(8,128)S(1)}, f32[2,72,128]{2,1,0:T(8,128)S(1)}, u32[]{:S(2)}, u32[]{:S(2)}) %collective-permute-start.1) | collective-permute-done | bytes 73760 | tf_op jit(solution)/shard_map/ppermute | solution.py:807
  10.0 1.7 %collective-permute-done.2.refs_3_ = f32[2,72,128]{2,1,0:T(8,128)S(1)} collective-permute-done((f32[2,72,128]{2,1,0:T(8,128)S(1)}, f32[2,72,128]{2,1,0:T(8,128)S(1)}, u32[]{:S(2)}, u32[]{:S(2)}) %collective-permute-start.2) | collective-permute-done | bytes 73760 | tf_op jit(solution)/shard_map/ppermute | solution.py:807
  11.7 0.5 %collective-permute-done.3.refs_4_ = f32[2,72,128]{2,1,0:T(8,128)S(1)} collective-permute-done((f32[2,72,128]{2,1,0:T(8,128)S(1)}, f32[2,72,128]{2,1,0:T(8,128)S(1)}, u32[]{:S(2)}, u32[]{:S(2)}) %collective-permute-start.3) | collective-permute-done | bytes 73760 | tf_op jit(solution)/shard_map/ppermute | solution.py:807
  12.2 1.6 %shard_map.81 = (f32[32,4,128]{2,1,0:T(4,128)}, f32[8,72,128]{2,1,0:T(8,128)S(1)}, f32[8,72,128]{2,1,0:T(8,128)S(1)}, f32[72,128]{1,0:T(8,128)S(1)}, f32[3,72,12...) custom-call(f32[8,72,128]{2,1,0:T(8,128)S(1)} %get-tuple-element.38.packed_ref.refs_0_, ...), custom_call_target="tpu_custom_call" | custom-call | tf_op jit(solution)/shard_map/pallas_call | solution.py:32
  13.8 4.9 %all-to-all-start = ((f32[32,4,128]{2,1,0:T(4,128)}), f32[32,4,128]{2,1,0:T(4,128)S(1)}, u32[]{:S(2)}, u32[]{:S(2)}) async-start(f32[32,4,128]{2,1,0:T(4,128)} %get-tuple-element.54), calls=%async_computation | async-start | bytes 131072 | tf_op jit(solution)/shard_map/all_to_all | solution.py:795
  18.7 0.3 collective-permute-start.6
  19.0 2.5 %collective-permute-start.7 = (f32[3,72,128]{2,1,0:T(8,128)S(1)}, f32[3,72,128]{2,1,0:T(8,128)S(1)}, u32[]{:S(2)}, u32[]{:S(2)}) collective-permute-start(f32[3,72,128]{2,1,0:T(8,128)S(1)} %get-tuple-element.57), channel_id=1, source_target_pairs={{4,8},{12,16},{20,24},{28,0},{8,4},{16,12},{24,20},{0,28},{5,9},{1... | collective-permute-start | bytes 331784 | tf_op jit(solution)/shard_map/ppermute | solution.py:860
  21.6 0.7 %collective-permute-start.5 = (f32[72,128]{1,0:T(8,128)S(1)}, f32[72,128]{1,0:T(8,128)S(1)}, u32[]{:S(2)}, u32[]{:S(2)}) collective-permute-start(f32[72,128]{1,0:T(8,128)S(1)} %get-tuple-element.52.refs_2_), channel_id=1, source_target_pairs={{1,2},{2,1},{5,6},{6,5},{9,10},{10,9},{13,14},{14,13},{17,18},{18,... | collective-permute-start | bytes 110600 | tf_op jit(solution)/shard_map/ppermute | solution.py:862
  22.2 4.3 %collective-permute-start.4 = (f32[72,128]{1,0:T(8,128)S(1)}, f32[72,128]{1,0:T(8,128)S(1)}, u32[]{:S(2)}, u32[]{:S(2)}) collective-permute-start(f32[72,128]{1,0:T(8,128)S(1)} %get-tuple-element.52.refs_2_), channel_id=1, source_target_pairs={{0,1},{1,0},{2,3},{3,2},{4,5},{5,4},{6,7},{7,6},{8,9},{9,8},{10,11... | collective-permute-start | bytes 110600 | tf_op jit(solution)/shard_map/ppermute | solution.py:861
  26.5 0.0 all-to-all-done.refs_0_
  26.5 0.9 %shard_map.82 = (f32[112,128]{1,0:T(8,128)S(1)}, f32[1,128]{1,0:T(1,128)S(1)}) custom-call(f32[32,4,128]{2,1,0:T(4,128)S(1)} %all-to-all-done.refs_0_), custom_call_target="tpu_custom_call" | custom-call | tf_op jit(solution)/shard_map/pallas_call | solution.py:32
  27.4 0.0 collective-permute-done.6.refs_2_
  27.4 0.0 collective-permute-done.7.refs_3_
  27.4 0.7 %shard_map.83 = (f32[10,72,128]{2,1,0:T(8,128)S(1)}, f32[10,72,128]{2,1,0:T(8,128)S(1)}, f32[16,128]{1,0:T(8,128)S(1)}, f32[4,72,128]{2,1,0:T(8,128)S(1)}) custom-call(f32[32,4,128]{2,1,0:T(4,128)S(1)} %all-to-all-done.refs_0_, f32[1,128]{1,0:T(1,128)S(1)} %get-tuple-element.55.refs_1_.refs_2_, f32[3,72,128]{2,1,0:T(8,128)S(1)} %collective-permute-done.6.refs_2_, ...), custom_call_target="tpu_custom_call" | custom-call | tf_op jit(solution)/shard_map/pallas_call | solution.py:32
  28.1 0.0 collective-permute-done.5.refs_1_
  28.1 0.3 collective-permute-done.4.refs_0_
  28.4 1.7 %shard_map.84 = (f32[32,8,128]{2,1,0:T(8,128)}, f32[8,72,128]{2,1,0:T(8,128)S(1)}, f32[8,72,128]{2,1,0:T(8,128)S(1)}, f32[4,2,72,128]{3,2,1,0:T(8,128)S(1)}) custom-call(f32[72,128]{1,0:T(8,128)S(1)} %collective-permute-done.4.refs_0_, f32[72,128]{1,0:T(8,128)S(1)} %collective-permute-done.5.refs_1_, f32[72,128]{1,0:T(8,128)S(1)} %get-tuple-element.52.refs_2_, ...), custom_call_target="tpu_custom_call" | custom-call | tf_op jit(solution)/shard_map/pallas_call | solution.py:32
  30.1 0.1 collective-permute-start.8
  30.2 2.6 %all-to-all-start.1 = ((f32[32,8,128]{2,1,0:T(8,128)}), f32[32,8,128]{2,1,0:T(8,128)S(1)}, u32[]{:S(2)}, u32[]{:S(2)}) async-start(f32[32,8,128]{2,1,0:T(8,128)} %get-tuple-element.64), calls=%async_computation.1 | async-start | bytes 262144 | tf_op jit(solution)/shard_map/all_to_all | solution.py:795
  32.8 0.0 collective-permute-done.8.near_ref.refs_3_
  32.9 2.7 %collective-permute-start.9 = (f32[4,72,128]{2,1,0:T(8,128)S(1)}, f32[4,72,128]{2,1,0:T(8,128)S(1)}, u32[]{:S(2)}, u32[]{:S(2)}) collective-permute-start(f32[4,72,128]{2,1,0:T(8,128)S(1)} %get-tuple-element.71), channel_id=1, source_target_pairs={{0,24},{4,28},{8,16},{12,20},{16,8},{20,12},{24,0},{28,4},{1,25},{... | collective-permute-start | bytes 442376 | tf_op jit(solution)/shard_map/ppermute | solution.py:904
  35.5 0.6 %collective-permute-start.10 = (f32[4,72,128]{2,1,0:T(8,128)S(1)}, f32[4,72,128]{2,1,0:T(8,128)S(1)}, u32[]{:S(2)}, u32[]{:S(2)}) collective-permute-start(f32[4,72,128]{2,1,0:T(8,128)S(1)} %get-tuple-element.72), channel_id=1, source_target_pairs={{0,16},{4,20},{8,24},{12,28},{16,0},{20,4},{24,8},{28,12},{1,17},{... | collective-permute-start | bytes 442376 | tf_op jit(solution)/shard_map/ppermute | solution.py:904
  36.1 0.3 collective-permute-start.11
  36.4 4.8 %all-to-all-done.1.refs_0_ = f32[32,8,128]{2,1,0:T(8,128)S(1)} async-done(((f32[32,8,128]{2,1,0:T(8,128)}), f32[32,8,128]{2,1,0:T(8,128)S(1)}, u32[]{:S(2)}, u32[]{:S(2)}) %all-to-all-start.1) | async-done | bytes 131104 | tf_op jit(solution)/shard_map/all_to_all | solution.py:795
  41.2 1.6 %shard_map.85 = (f32[560,128]{1,0:T(8,128)}, f32[16,128]{1,0:T(8,128)S(1)}) custom-call(f32[32,8,128]{2,1,0:T(8,128)S(1)} %all-to-all-done.1.refs_0_, f32[112,128]{1,0:T(8,128)S(1)} %get-tuple-element.65.refs_1_, f32[1,128]{1,0:T(1,128)S(1)} %get-tuple-element.55.refs_1_.refs_2_, f32[8,72,128]{2,1,0:T(8,128)S(1)} %get-tuple-element.58.refs_4_.refs_3_, ...), custom_call_target="tpu_custom_call" | custom-call | tf_op jit(solution)/shard_map/pallas_call | solution.py:32
  42.8 0.0 collective-permute-done.9.refs_4_
  42.8 1.3 %collective-permute-done.10.refs_5_ = f32[4,72,128]{2,1,0:T(8,128)S(1)} collective-permute-done((f32[4,72,128]{2,1,0:T(8,128)S(1)}, f32[4,72,128]{2,1,0:T(8,128)S(1)}, u32[]{:S(2)}, u32[]{:S(2)}) %collective-permute-start.10) | collective-permute-done | bytes 147488 | tf_op jit(solution)/shard_map/ppermute | solution.py:904
  44.1 0.0 collective-permute-done.11.refs_6_
  44.1 1.0 %shard_map.87 = f32[560,128]{1,0:T(8,128)} custom-call(f32[16,128]{1,0:T(8,128)S(1)} %get-tuple-element.68.refs_0_, f32[8,72,128]{2,1,0:T(8,128)S(1)} %get-tuple-element.63.refs_10_.smooth_ref.refs_1_, f32[8,72,128]{2,1,0:T(8,128)S(1)} %get-tuple-element.69.second_ref.refs_2_, f32[4,2,72,128]{3,2,1,0:T(8,128)S(1)} %collective-permute-done.8.near_ref.refs_3_, ...), custom_call_target="tpu_custom_call" | custom-call | tf_op jit(solution)/shard_map/pallas_call | solution.py:32
  (3 shorter events, 0.1 us)
Async XLA Ops:
  0.6 1.0 %copy-start = (f32[70,8,128]{2,1,0:T(8,128)S(1)}, f32[70,8,128]{2,1,0:T(8,128)}, u32[]{:S(2)}) copy-start(f32[70,8,128]{2,1,0:T(8,128)} %param.9) | copy-start | bytes 860164
  1.6 0.8 %copy-start.3 = (f32[69]{0:T(128)S(1)}, f32[69]{0:T(128)}, u32[]{:S(2)}) copy-start(f32[69]{0:T(128)} %param.8) | copy-start | bytes 832
  1.6 0.8 %copy-start.4 = (f32[70]{0:T(128)S(1)}, f32[70]{0:T(128)}, u32[]{:S(2)}) copy-start(f32[70]{0:T(128)} %param.10) | copy-start | bytes 844
  1.6 0.8 %copy-start.5 = (f32[70]{0:T(128)S(1)}, f32[70]{0:T(128)}, u32[]{:S(2)}) copy-start(f32[70]{0:T(128)} %param.11) | copy-start | bytes 844
  1.6 6.4 %copy-start.2 = (f32[70,8,128]{2,1,0:T(8,128)S(1)}, f32[70,8,128]{2,1,0:T(8,128)}, u32[]{:S(2)}) copy-start(f32[70,8,128]{2,1,0:T(8,128)} %param.7) | copy-start | bytes 860164
  1.9 6.1 %copy-start.1 = (f32[70,8,128]{2,1,0:T(8,128)S(1)}, f32[70,8,128]{2,1,0:T(8,128)}, u32[]{:S(2)}) copy-start(f32[70,8,128]{2,1,0:T(8,128)} %param.6) | copy-start | bytes 860164
  1.9 1.5 %collective-permute-start = (f32[4,72,128]{2,1,0:T(8,128)S(1)}, f32[4,72,128]{2,1,0:T(8,128)S(1)}, u32[]{:S(2)}, u32[]{:S(2)}) collective-permute-start(f32[4,72,128]{2,1,0:T(8,128)S(1)} %get-tuple-element.39), channel_id=1, source_target_pairs={{0,4},{4,0},{8,12},{12,8},{16,20},{20,16},{24,28},{28,24},{1,5},{5... | collective-permute-start | bytes 442376 | tf_op jit(solution)/shard_map/ppermute | solution.py:804
  3.4 6.5 %collective-permute-start.1 = (f32[2,72,128]{2,1,0:T(8,128)S(1)}, f32[2,72,128]{2,1,0:T(8,128)S(1)}, u32[]{:S(2)}, u32[]{:S(2)}) collective-permute-start(f32[2,72,128]{2,1,0:T(8,128)S(1)} %get-tuple-element.40), channel_id=1, source_target_pairs={{0,24},{4,28},{8,16},{12,20},{16,8},{20,12},{24,0},{28,4},{1,25},{... | collective-permute-start | bytes 221192 | tf_op jit(solution)/shard_map/ppermute | solution.py:807
  7.3 4.4 %collective-permute-start.2 = (f32[2,72,128]{2,1,0:T(8,128)S(1)}, f32[2,72,128]{2,1,0:T(8,128)S(1)}, u32[]{:S(2)}, u32[]{:S(2)}) collective-permute-start(f32[2,72,128]{2,1,0:T(8,128)S(1)} %get-tuple-element.41), channel_id=1, source_target_pairs={{0,16},{4,20},{8,24},{12,28},{16,0},{20,4},{24,8},{28,12},{1,17},{... | collective-permute-start | bytes 221192 | tf_op jit(solution)/shard_map/ppermute | solution.py:807
  7.8 4.4 %collective-permute-start.3 = (f32[2,72,128]{2,1,0:T(8,128)S(1)}, f32[2,72,128]{2,1,0:T(8,128)S(1)}, u32[]{:S(2)}, u32[]{:S(2)}) collective-permute-start(f32[2,72,128]{2,1,0:T(8,128)S(1)} %get-tuple-element.42), channel_id=1, source_target_pairs={{0,8},{4,12},{8,0},{12,4},{16,24},{20,28},{24,16},{28,20},{1,9},{5... | collective-permute-start | bytes 221192 | tf_op jit(solution)/shard_map/ppermute | solution.py:807
  13.8 12.7 %all-to-all-start = ((f32[32,4,128]{2,1,0:T(4,128)}), f32[32,4,128]{2,1,0:T(4,128)S(1)}, u32[]{:S(2)}, u32[]{:S(2)}) async-start(f32[32,4,128]{2,1,0:T(4,128)} %get-tuple-element.54), calls=%async_computation | async-start | bytes 131072 | tf_op jit(solution)/shard_map/all_to_all | solution.py:795
  18.7 8.6 %collective-permute-start.6 = (f32[3,72,128]{2,1,0:T(8,128)S(1)}, f32[3,72,128]{2,1,0:T(8,128)S(1)}, u32[]{:S(2)}, u32[]{:S(2)}) collective-permute-start(f32[3,72,128]{2,1,0:T(8,128)S(1)} %get-tuple-element.56), channel_id=1, source_target_pairs={{0,4},{4,0},{8,12},{12,8},{16,20},{20,16},{24,28},{28,24},{1,5},{5... | collective-permute-start | bytes 331784 | tf_op jit(solution)/shard_map/ppermute | solution.py:859
  19.0 8.3 %collective-permute-start.7 = (f32[3,72,128]{2,1,0:T(8,128)S(1)}, f32[3,72,128]{2,1,0:T(8,128)S(1)}, u32[]{:S(2)}, u32[]{:S(2)}) collective-permute-start(f32[3,72,128]{2,1,0:T(8,128)S(1)} %get-tuple-element.57), channel_id=1, source_target_pairs={{4,8},{12,16},{20,24},{28,0},{8,4},{16,12},{24,20},{0,28},{5,9},{1... | collective-permute-start | bytes 331784 | tf_op jit(solution)/shard_map/ppermute | solution.py:860
  21.6 6.5 %collective-permute-start.5 = (f32[72,128]{1,0:T(8,128)S(1)}, f32[72,128]{1,0:T(8,128)S(1)}, u32[]{:S(2)}, u32[]{:S(2)}) collective-permute-start(f32[72,128]{1,0:T(8,128)S(1)} %get-tuple-element.52.refs_2_), channel_id=1, source_target_pairs={{1,2},{2,1},{5,6},{6,5},{9,10},{10,9},{13,14},{14,13},{17,18},{18,... | collective-permute-start | bytes 110600 | tf_op jit(solution)/shard_map/ppermute | solution.py:862
  22.2 6.2 %collective-permute-start.4 = (f32[72,128]{1,0:T(8,128)S(1)}, f32[72,128]{1,0:T(8,128)S(1)}, u32[]{:S(2)}, u32[]{:S(2)}) collective-permute-start(f32[72,128]{1,0:T(8,128)S(1)} %get-tuple-element.52.refs_2_), channel_id=1, source_target_pairs={{0,1},{1,0},{2,3},{3,2},{4,5},{5,4},{6,7},{7,6},{8,9},{9,8},{10,11... | collective-permute-start | bytes 110600 | tf_op jit(solution)/shard_map/ppermute | solution.py:861
  30.1 2.7 %collective-permute-start.8 = (f32[4,2,72,128]{3,2,1,0:T(8,128)S(1)}, f32[4,2,72,128]{3,2,1,0:T(8,128)S(1)}, u32[]{:S(2)}, u32[]{:S(2)}) collective-permute-start(f32[4,2,72,128]{3,2,1,0:T(8,128)S(1)} %get-tuple-element.70), channel_id=1, source_target_pairs={{0,4},{4,0},{8,12},{12,8},{16,20},{20,16},{24,28},{28,24},{1,5},{5... | collective-permute-start | bytes 884744 | tf_op jit(solution)/shard_map/ppermute | solution.py:900
  30.2 11.0 %all-to-all-start.1 = ((f32[32,8,128]{2,1,0:T(8,128)}), f32[32,8,128]{2,1,0:T(8,128)S(1)}, u32[]{:S(2)}, u32[]{:S(2)}) async-start(f32[32,8,128]{2,1,0:T(8,128)} %get-tuple-element.64), calls=%async_computation.1 | async-start | bytes 262144 | tf_op jit(solution)/shard_map/all_to_all | solution.py:795
  32.9 10.0 %collective-permute-start.9 = (f32[4,72,128]{2,1,0:T(8,128)S(1)}, f32[4,72,128]{2,1,0:T(8,128)S(1)}, u32[]{:S(2)}, u32[]{:S(2)}) collective-permute-start(f32[4,72,128]{2,1,0:T(8,128)S(1)} %get-tuple-element.71), channel_id=1, source_target_pairs={{0,24},{4,28},{8,16},{12,20},{16,8},{20,12},{24,0},{28,4},{1,25},{... | collective-permute-start | bytes 442376 | tf_op jit(solution)/shard_map/ppermute | solution.py:904
  35.5 8.6 %collective-permute-start.10 = (f32[4,72,128]{2,1,0:T(8,128)S(1)}, f32[4,72,128]{2,1,0:T(8,128)S(1)}, u32[]{:S(2)}, u32[]{:S(2)}) collective-permute-start(f32[4,72,128]{2,1,0:T(8,128)S(1)} %get-tuple-element.72), channel_id=1, source_target_pairs={{0,16},{4,20},{8,24},{12,28},{16,0},{20,4},{24,8},{28,12},{1,17},{... | collective-permute-start | bytes 442376 | tf_op jit(solution)/shard_map/ppermute | solution.py:904
  36.1 8.0 %collective-permute-start.11 = (f32[4,72,128]{2,1,0:T(8,128)S(1)}, f32[4,72,128]{2,1,0:T(8,128)S(1)}, u32[]{:S(2)}, u32[]{:S(2)}) collective-permute-start(f32[4,72,128]{2,1,0:T(8,128)S(1)} %get-tuple-element.73), channel_id=1, source_target_pairs={{0,8},{4,12},{8,0},{12,4},{16,24},{20,28},{24,16},{28,20},{1,9},{5... | collective-permute-start | bytes 442376 | tf_op jit(solution)/shard_map/ppermute | solution.py:904

commit v8 on v7

--- a/solution.py
+++ b/solution.py
@@ -156,14 +156,10 @@
 
 
 def scalars_row(values, lanes):
-    count = len(values)
-    padded = -(-count // 8) * 8
-    rows = [jnp.sum(value, axis=0, keepdims=True) for value in values]
-    rows += [jnp.zeros_like(rows[0])] * (padded - count)
-    sums = jnp.sum(jnp.concatenate(rows, axis=0), axis=1, keepdims=True)
-    shape = (padded, lanes)
-    spread = jnp.where(iota(shape, 0) == iota(shape, 1), sums, 0.0)
-    return jnp.sum(spread, axis=0, keepdims=True)
+    sums = jnp.sum(jnp.concatenate(values, axis=0), axis=1, keepdims=True)
+    lane = iota((8, lanes), 1)
+    parts = [jnp.where(lane == j, sums[8 * j : 8 * j + 8], 0.0) for j in range(len(values))]
+    return jnp.sum(add_all(parts), axis=0, keepdims=True)
 
 
 def fold(tile):
@@ -178,6 +174,15 @@
     while len(parts) > 1:
         parts = [a + b for a, b in zip(parts[::2], parts[1::2])] + parts[len(parts) // 2 * 2 :]
     return parts[0]
+
+
+def rim_sums(fields, weights):
+    weighted = add_all([fold(a * b) for a, b in zip(fields, weights)])
+    every = add_all([fold(tile) for tile in fields])
+    lane, across = iota(every.shape, 1), every.shape[1]
+    south = jnp.where(lane == 0, every, 0.0)
+    north = jnp.where(lane == across - 1, every, 0.0)
+    return [weighted, fold(fields[0]), fold(fields[-1]), south, north]
 
 
 def dot(matrix, tiles):
@@ -201,6 +206,7 @@
     matrices_ref,
     rows_ref,
     unit_ref,
+    sums_ref,
 ):
     points, padded, across = forced_ref.shape
     inverse = inverse_ref[:, :padded]
@@ -222,6 +228,8 @@
         jnp.sum(inverse_ref[...], axis=1, keepdims=True), unit_ref.shape
     )
     rows_ref[0:8] = add_all([fold(tile) for tile in weight])
+    for j, value in enumerate(rim_sums(weight, weight)):
+        sums_ref[8 * j : 8 * j + 8] = value
     solar = jnp.sum(fold(sun), axis=0, keepdims=True)
     rows_ref[8:16] = jnp.broadcast_to(solar, (8, across))
 
@@ -491,12 +499,14 @@
     inner_ref,
     outer_ref,
     smooth_ref,
+    residual_ref,
     weight_ref,
     inverse_ref,
     image_ref,
     second_ref,
     values_ref,
     corners_ref,
+    sums_ref,
 ):
     points, padded, across = smooth_ref.shape
     coarse = coarse_ref[...]
@@ -552,6 +562,9 @@
         - (weight[i] * (field[i + 1] + here[i]) + jumps[i])
         for i in range(points + 2)
     ]
+    residual = [residual_ref[i] for i in range(points)]
+    for j, value in enumerate(rim_sums(residual, weight[1 : points + 1])):
+        sums_ref[8 * j : 8 * j + 8] = value
     smoothed = dot(inverse_ref[:, :padded], image)
     for i in range(points + 2):
         image_ref[i] = image[i]
@@ -571,6 +584,8 @@
     second_ref_in,
     values_ref,
     corners_ref,
+    residual_sums_ref,
+    weight_sums_ref,
     *refs,
 ):
     *refs, message_ref, message_sem = refs
@@ -630,7 +645,7 @@
     second.append(second_ref_in[points + 1])
     both = jnp.where(is_north, turn(ring, 1), turn(ring, -1))
 
-    names = ("image", "change", "residual")
+    names = ("image", "change")
     pairs = {}
     sides = {name: [] for name in names}
     left = []
@@ -657,23 +672,23 @@
         collect("qd", result * change)
         collect("dd", change * change)
         collect("rd", residual * change)
-        collect("ww", heavy * heavy)
-        sides.setdefault("weight", []).append(fold(heavy))
-        for name, value in zip(names, (result, change, residual)):
+        for name, value in zip(names, (result, change)):
             sides[name].append(fold(value))
             collect("w" + name, heavy * value)
     pairs = {key: add_all(value) for key, value in pairs.items()}
     lane = iota(pairs["qq"].shape, 1)
     out = [pairs[key] for key in ("qq", "rq", "qd", "dd", "rd")]
-    for name in names + ("weight",):
+    for name in names:
         every = add_all(sides[name])
         out += [
-            pairs["ww"] if name == "weight" else pairs["w" + name],
+            pairs["w" + name],
             sides[name][0],
             sides[name][-1],
             jnp.where(lane == 0, every, 0.0),
             jnp.where(lane == across - 1, every, 0.0),
         ]
+    for sums_ref in (residual_sums_ref, weight_sums_ref):
+        out += [sums_ref[8 * j : 8 * j + 8] for j in range(5)]
     out.append(add_all(left))
     row = scalars_row(out, across)
     message_ref[...] = jnp.zeros(message_ref.shape, F32)
@@ -826,9 +841,9 @@
 
     forcing = forcing_vector.reshape(flat)
     weights = shift_weights.reshape(flat)
-    forced, weights, *prepared = call(
+    forced, weights, *prepared, weight_sums = call(
         part(prepare_kernel, levels),
-        [field, field, field, (2 * padded + 8, across), (24, across), (padded, across)],
+        [field, field, field, (2 * padded + 8, across), (24, across), (padded, across), (40, across)],
         forcing,
         weights,
         inverse,
@@ -866,14 +881,15 @@
         [(saved_rows(tiles, groups), lanes), (1, lanes)],
         received,
     )
-    image, second, values, corners = call(
+    image, second, values, corners, residual_sums = call(
         part(inside_kernel, levels, tiles, groups),
-        [wide, wide, (16, across), (4, padded, across)],
+        [wide, wide, (16, across), (4, padded, across), (40, across)],
         received,
         coarse,
         inner,
         outer,
         smooth,
+        residual,
         weights,
         inverse,
     )
@@ -891,6 +907,8 @@
         second,
         values,
         corners,
+        residual_sums,
+        weight_sums,
         *packed,
         sends=True,
     )

time: 45.4 us -> 45.3 us (level)
  no operation moved by 1% of the time
where the time goes in v8:
time: 45.3 us; the launch traced here: 45 us
  starting transfers between devices  23.9 us (53%)
  waiting for transfers between devices  10.6 us (23%)
  Pallas kernels  8.65 us (19%)
  local copies, waits for them, and re-layouts  0.97 us (2%)
  between operations  0.78 us (2%)
    pallas_call x11, Pallas kernels, call(): pl.pallas_call(kernel, out_shape=[jax.ShapeDtypeStruct(shape, F32) for sh...  8.65 us
    ppermute x6, starting transfers between devices, per_device(): lax.ppermute(value, 'tile', [(i, i ^ step) for i in range(tiles)])  8.07 us
    all_to_all x2, starting transfers between devices, gather(): lax.all_to_all(value, ('tile', 'grp'), split_axis=0, concat_axis=0, tiled...  7.51 us
    ppermute x6, waiting for transfers between devices, per_device(): lax.ppermute(value, 'tile', [(i, i ^ step) for i in range(tiles)])  4.94 us
    all_to_all x2, waiting for transfers between devices, gather(): lax.all_to_all(value, ('tile', 'grp'), split_axis=0, concat_axis=0, tiled...  4.79 us
    ppermute x1, starting transfers between devices, per_device(): low = lax.ppermute(rim, 'grp', inner_pairs(groups))  4.27 us
    ppermute x1, starting transfers between devices, per_device(): outer = lax.ppermute(outer, 'tile', outer_pairs(tiles, True))  2.53 us
    unnamed x12, local copies, waits for them, and re-layouts  0.97 us
  transfers between devices with their start and end apart: 14, of which 7 were waited for; matrix products, arithmetic and copies ran while one was open for 0% of the time, Pallas kernels for 9%

profile of v8, /device:TPU:0, one launch (start us, length us, event | category | flops | bytes accessed | tf_op | source)
XLA Modules:
  0.0 45.0 jit_solution(12977823594378970253)
XLA Ops:
  0.6 0.0 copy-start
  0.6 0.9 %copy-done = f32[70,8,128]{2,1,0:T(8,128)S(1)} copy-done((f32[70,8,128]{2,1,0:T(8,128)S(1)}, f32[70,8,128]{2,1,0:T(8,128)}, u32[]{:S(2)}) %copy-start) | copy-done | bytes 286744
  1.6 0.0 copy-start.3
  1.6 0.0 copy-start.4
  1.6 0.0 copy-start.5
  1.6 0.0 copy-start.2
  1.6 0.3 shard_map.77
  1.9 0.0 copy-start.1
  1.9 0.5 %collective-permute-start = (f32[4,72,128]{2,1,0:T(8,128)S(1)}, f32[4,72,128]{2,1,0:T(8,128)S(1)}, u32[]{:S(2)}, u32[]{:S(2)}) collective-permute-start(f32[4,72,128]{2,1,0:T(8,128)S(1)} %get-tuple-element.41), channel_id=1, source_target_pairs={{0,4},{4,0},{8,12},{12,8},{16,20},{20,16},{24,28},{28,24},{1,5},{5... | collective-permute-start | bytes 442376 | tf_op jit(solution)/shard_map/ppermute | solution.py:819
  2.4 0.0 copy-done.3
  2.4 0.0 copy-done.4
  2.4 0.0 copy-done.5
  2.4 0.4 shard_map.79
  2.8 0.6 %collective-permute-done.near_ref.refs_1_ = f32[4,72,128]{2,1,0:T(8,128)S(1)} collective-permute-done((f32[4,72,128]{2,1,0:T(8,128)S(1)}, f32[4,72,128]{2,1,0:T(8,128)S(1)}, u32[]{:S(2)}, u32[]{:S(2)}) %collective-permute-start) | collective-permute-done | bytes 147488 | tf_op jit(solution)/shard_map/ppermute | solution.py:819
  3.4 3.9 %collective-permute-start.1 = (f32[2,72,128]{2,1,0:T(8,128)S(1)}, f32[2,72,128]{2,1,0:T(8,128)S(1)}, u32[]{:S(2)}, u32[]{:S(2)}) collective-permute-start(f32[2,72,128]{2,1,0:T(8,128)S(1)} %get-tuple-element.42), channel_id=1, source_target_pairs={{0,24},{4,28},{8,16},{12,20},{16,8},{20,12},{24,0},{28,4},{1,25},{... | collective-permute-start | bytes 221192 | tf_op jit(solution)/shard_map/ppermute | solution.py:822
  7.3 0.5 %collective-permute-start.2 = (f32[2,72,128]{2,1,0:T(8,128)S(1)}, f32[2,72,128]{2,1,0:T(8,128)S(1)}, u32[]{:S(2)}, u32[]{:S(2)}) collective-permute-start(f32[2,72,128]{2,1,0:T(8,128)S(1)} %get-tuple-element.43), channel_id=1, source_target_pairs={{0,16},{4,20},{8,24},{12,28},{16,0},{20,4},{24,8},{28,12},{1,17},{... | collective-permute-start | bytes 221192 | tf_op jit(solution)/shard_map/ppermute | solution.py:822
  7.8 0.1 collective-permute-start.3
  8.0 0.0 copy-done.2
  8.0 0.0 copy-done.1
  8.0 0.5 %shard_map.80 = (f32[8,72,128]{2,1,0:T(8,128)S(1)}, f32[8,72,128]{2,1,0:T(8,128)S(1)}, f32[8,72,128]{2,1,0:T(8,128)S(1)}, f32[152,128]{1,0:T(8,128)S(1)}, f32[24...) custom-call(f32[560,128]{1,0:T(8,128)S(1)} %bitcast.9, f32[560,128]{1,0:T(8,128)S(1)} %bitcast.10, ...), custom_call_target="tpu_custom_call" | custom-call | tf_op jit(solution)/shard_map/pallas_call | solution.py:32
  8.5 1.4 %collective-permute-done.1.refs_2_ = f32[2,72,128]{2,1,0:T(8,128)S(1)} collective-permute-done((f32[2,72,128]{2,1,0:T(8,128)S(1)}, f32[2,72,128]{2,1,0:T(8,128)S(1)}, u32[]{:S(2)}, u32[]{:S(2)}) %collective-permute-start.1) | collective-permute-done | bytes 73760 | tf_op jit(solution)/shard_map/ppermute | solution.py:822
  10.0 1.7 %collective-permute-done.2.refs_3_ = f32[2,72,128]{2,1,0:T(8,128)S(1)} collective-permute-done((f32[2,72,128]{2,1,0:T(8,128)S(1)}, f32[2,72,128]{2,1,0:T(8,128)S(1)}, u32[]{:S(2)}, u32[]{:S(2)}) %collective-permute-start.2) | collective-permute-done | bytes 73760 | tf_op jit(solution)/shard_map/ppermute | solution.py:822
  11.7 0.5 %collective-permute-done.3.refs_4_ = f32[2,72,128]{2,1,0:T(8,128)S(1)} collective-permute-done((f32[2,72,128]{2,1,0:T(8,128)S(1)}, f32[2,72,128]{2,1,0:T(8,128)S(1)}, u32[]{:S(2)}, u32[]{:S(2)}) %collective-permute-start.3) | collective-permute-done | bytes 73760 | tf_op jit(solution)/shard_map/ppermute | solution.py:822
  12.2 1.6 %shard_map.81 = (f32[32,4,128]{2,1,0:T(4,128)}, f32[8,72,128]{2,1,0:T(8,128)S(1)}, f32[8,72,128]{2,1,0:T(8,128)S(1)}, f32[72,128]{1,0:T(8,128)S(1)}, f32[3,72,12...) custom-call(f32[8,72,128]{2,1,0:T(8,128)S(1)} %get-tuple-element.40.packed_ref.refs_0_, ...), custom_call_target="tpu_custom_call" | custom-call | tf_op jit(solution)/shard_map/pallas_call | solution.py:32
  13.8 4.9 %all-to-all-start = ((f32[32,4,128]{2,1,0:T(4,128)}), f32[32,4,128]{2,1,0:T(4,128)S(1)}, u32[]{:S(2)}, u32[]{:S(2)}) async-start(f32[32,4,128]{2,1,0:T(4,128)} %get-tuple-element.56), calls=%async_computation | async-start | bytes 131072 | tf_op jit(solution)/shard_map/all_to_all | solution.py:810
  18.7 0.3 collective-permute-start.6
  19.0 2.5 %collective-permute-start.7 = (f32[3,72,128]{2,1,0:T(8,128)S(1)}, f32[3,72,128]{2,1,0:T(8,128)S(1)}, u32[]{:S(2)}, u32[]{:S(2)}) collective-permute-start(f32[3,72,128]{2,1,0:T(8,128)S(1)} %get-tuple-element.59), channel_id=1, source_target_pairs={{4,8},{12,16},{20,24},{28,0},{8,4},{16,12},{24,20},{0,28},{5,9},{1... | collective-permute-start | bytes 331784 | tf_op jit(solution)/shard_map/ppermute | solution.py:875
  21.6 0.7 %collective-permute-start.5 = (f32[72,128]{1,0:T(8,128)S(1)}, f32[72,128]{1,0:T(8,128)S(1)}, u32[]{:S(2)}, u32[]{:S(2)}) collective-permute-start(f32[72,128]{1,0:T(8,128)S(1)} %get-tuple-element.54.refs_2_), channel_id=1, source_target_pairs={{1,2},{2,1},{5,6},{6,5},{9,10},{10,9},{13,14},{14,13},{17,18},{18,... | collective-permute-start | bytes 110600 | tf_op jit(solution)/shard_map/ppermute | solution.py:877
  22.2 4.3 %collective-permute-start.4 = (f32[72,128]{1,0:T(8,128)S(1)}, f32[72,128]{1,0:T(8,128)S(1)}, u32[]{:S(2)}, u32[]{:S(2)}) collective-permute-start(f32[72,128]{1,0:T(8,128)S(1)} %get-tuple-element.54.refs_2_), channel_id=1, source_target_pairs={{0,1},{1,0},{2,3},{3,2},{4,5},{5,4},{6,7},{7,6},{8,9},{9,8},{10,11... | collective-permute-start | bytes 110600 | tf_op jit(solution)/shard_map/ppermute | solution.py:876
  26.5 0.0 all-to-all-done.refs_0_
  26.5 0.9 %shard_map.82 = (f32[112,128]{1,0:T(8,128)S(1)}, f32[1,128]{1,0:T(1,128)S(1)}) custom-call(f32[32,4,128]{2,1,0:T(4,128)S(1)} %all-to-all-done.refs_0_), custom_call_target="tpu_custom_call" | custom-call | tf_op jit(solution)/shard_map/pallas_call | solution.py:32
  27.4 0.0 collective-permute-done.6.refs_2_
  27.4 0.0 collective-permute-done.7.refs_3_
  27.4 0.7 %shard_map.83 = (f32[10,72,128]{2,1,0:T(8,128)S(1)}, f32[10,72,128]{2,1,0:T(8,128)S(1)}, f32[16,128]{1,0:T(8,128)S(1)}, f32[4,72,128]{2,1,0:T(8,128)S(1)}, f32[40,128]{1,0:T(8,128)S(1)}) custom-call(f32[32,4,128]{2,1,0:T(4,128)S(1)} %all-to-all-done.refs_0_, f32[1,128]{1,0:T(1,128)S(1)} %get-tuple-element.57.refs_1_.refs_2_, ...), custom_call_target="tpu_custom_call" | custom-call | tf_op jit(solution)/shard_map/pallas_call | solution.py:32
  28.1 0.0 collective-permute-done.5.refs_1_
  28.1 0.3 collective-permute-done.4.refs_0_
  28.4 1.6 %shard_map.84 = (f32[32,8,128]{2,1,0:T(8,128)}, f32[8,72,128]{2,1,0:T(8,128)S(1)}, f32[8,72,128]{2,1,0:T(8,128)S(1)}, f32[4,2,72,128]{3,2,1,0:T(8,128)S(1)}) custom-call(f32[72,128]{1,0:T(8,128)S(1)} %collective-permute-done.4.refs_0_, f32[72,128]{1,0:T(8,128)S(1)} %collective-permute-done.5.refs_1_, f32[72,128]{1,0:T(8,128)S(1)} %get-tuple-element.54.refs_2_, ...), custom_call_target="tpu_custom_call" | custom-call | tf_op jit(solution)/shard_map/pallas_call | solution.py:32
  30.0 0.1 collective-permute-start.8
  30.1 2.6 %all-to-all-start.1 = ((f32[32,8,128]{2,1,0:T(8,128)}), f32[32,8,128]{2,1,0:T(8,128)S(1)}, u32[]{:S(2)}, u32[]{:S(2)}) async-start(f32[32,8,128]{2,1,0:T(8,128)} %get-tuple-element.68), calls=%async_computation.1 | async-start | bytes 262144 | tf_op jit(solution)/shard_map/all_to_all | solution.py:810
  32.7 0.0 collective-permute-done.8.near_ref.refs_3_
  32.8 2.7 %collective-permute-start.9 = (f32[4,72,128]{2,1,0:T(8,128)S(1)}, f32[4,72,128]{2,1,0:T(8,128)S(1)}, u32[]{:S(2)}, u32[]{:S(2)}) collective-permute-start(f32[4,72,128]{2,1,0:T(8,128)S(1)} %get-tuple-element.75), channel_id=1, source_target_pairs={{0,24},{4,28},{8,16},{12,20},{16,8},{20,12},{24,0},{28,4},{1,25},{... | collective-permute-start | bytes 442376 | tf_op jit(solution)/shard_map/ppermute | solution.py:922
  35.4 0.6 %collective-permute-start.10 = (f32[4,72,128]{2,1,0:T(8,128)S(1)}, f32[4,72,128]{2,1,0:T(8,128)S(1)}, u32[]{:S(2)}, u32[]{:S(2)}) collective-permute-start(f32[4,72,128]{2,1,0:T(8,128)S(1)} %get-tuple-element.76), channel_id=1, source_target_pairs={{0,16},{4,20},{8,24},{12,28},{16,0},{20,4},{24,8},{28,12},{1,17},{... | collective-permute-start | bytes 442376 | tf_op jit(solution)/shard_map/ppermute | solution.py:922
  36.0 0.3 collective-permute-start.11
  36.3 4.8 %all-to-all-done.1.refs_0_ = f32[32,8,128]{2,1,0:T(8,128)S(1)} async-done(((f32[32,8,128]{2,1,0:T(8,128)}), f32[32,8,128]{2,1,0:T(8,128)S(1)}, u32[]{:S(2)}, u32[]{:S(2)}) %all-to-all-start.1) | async-done | bytes 131104 | tf_op jit(solution)/shard_map/all_to_all | solution.py:810
  41.1 1.6 %shard_map.85 = (f32[560,128]{1,0:T(8,128)}, f32[16,128]{1,0:T(8,128)S(1)}) custom-call(f32[32,8,128]{2,1,0:T(8,128)S(1)} %all-to-all-done.1.refs_0_, f32[112,128]{1,0:T(8,128)S(1)} %get-tuple-element.69.refs_1_, f32[1,128]{1,0:T(1,128)S(1)} %get-tuple-element.57.refs_1_.refs_2_, f32[8,72,128]{2,1,0:T(8,128)S(1)} %get-tuple-element.60.refs_4_.refs_3_, ...), custom_call_target="tpu_custom_call" | custom-call | tf_op jit(solution)/shard_map/pallas_call | solution.py:32
  42.7 0.0 collective-permute-done.9.refs_4_
  42.7 1.3 %collective-permute-done.10.refs_5_ = f32[4,72,128]{2,1,0:T(8,128)S(1)} collective-permute-done((f32[4,72,128]{2,1,0:T(8,128)S(1)}, f32[4,72,128]{2,1,0:T(8,128)S(1)}, u32[]{:S(2)}, u32[]{:S(2)}) %collective-permute-start.10) | collective-permute-done | bytes 147488 | tf_op jit(solution)/shard_map/ppermute | solution.py:922
  44.0 0.0 collective-permute-done.11.refs_6_
  44.0 1.0 %shard_map.87 = f32[560,128]{1,0:T(8,128)} custom-call(f32[16,128]{1,0:T(8,128)S(1)} %get-tuple-element.72.refs_0_, f32[8,72,128]{2,1,0:T(8,128)S(1)} %get-tuple-element.67.refs_12_.smooth_ref.refs_1_, f32[8,72,128]{2,1,0:T(8,128)S(1)} %get-tuple-element.73.second_ref.refs_2_, f32[4,2,72,128]{3,2,1,0:T(8,128)S(1)} %collective-permute-done.8.near_ref.refs_3_, ...), custom_call_target="tpu_custom_call" | custom-call | tf_op jit(solution)/shard_map/pallas_call | solution.py:32
  (3 shorter events, 0.1 us)
Async XLA Ops:
  0.6 1.0 %copy-start = (f32[70,8,128]{2,1,0:T(8,128)S(1)}, f32[70,8,128]{2,1,0:T(8,128)}, u32[]{:S(2)}) copy-start(f32[70,8,128]{2,1,0:T(8,128)} %param.9) | copy-start | bytes 860164
  1.6 0.8 %copy-start.3 = (f32[69]{0:T(128)S(1)}, f32[69]{0:T(128)}, u32[]{:S(2)}) copy-start(f32[69]{0:T(128)} %param.8) | copy-start | bytes 832
  1.6 0.8 %copy-start.4 = (f32[70]{0:T(128)S(1)}, f32[70]{0:T(128)}, u32[]{:S(2)}) copy-start(f32[70]{0:T(128)} %param.10) | copy-start | bytes 844
  1.6 0.8 %copy-start.5 = (f32[70]{0:T(128)S(1)}, f32[70]{0:T(128)}, u32[]{:S(2)}) copy-start(f32[70]{0:T(128)} %param.11) | copy-start | bytes 844
  1.6 6.4 %copy-start.2 = (f32[70,8,128]{2,1,0:T(8,128)S(1)}, f32[70,8,128]{2,1,0:T(8,128)}, u32[]{:S(2)}) copy-start(f32[70,8,128]{2,1,0:T(8,128)} %param.7) | copy-start | bytes 860164
  1.9 6.1 %copy-start.1 = (f32[70,8,128]{2,1,0:T(8,128)S(1)}, f32[70,8,128]{2,1,0:T(8,128)}, u32[]{:S(2)}) copy-start(f32[70,8,128]{2,1,0:T(8,128)} %param.6) | copy-start | bytes 860164
  1.9 1.5 %collective-permute-start = (f32[4,72,128]{2,1,0:T(8,128)S(1)}, f32[4,72,128]{2,1,0:T(8,128)S(1)}, u32[]{:S(2)}, u32[]{:S(2)}) collective-permute-start(f32[4,72,128]{2,1,0:T(8,128)S(1)} %get-tuple-element.41), channel_id=1, source_target_pairs={{0,4},{4,0},{8,12},{12,8},{16,20},{20,16},{24,28},{28,24},{1,5},{5... | collective-permute-start | bytes 442376 | tf_op jit(solution)/shard_map/ppermute | solution.py:819
  3.4 6.5 %collective-permute-start.1 = (f32[2,72,128]{2,1,0:T(8,128)S(1)}, f32[2,72,128]{2,1,0:T(8,128)S(1)}, u32[]{:S(2)}, u32[]{:S(2)}) collective-permute-start(f32[2,72,128]{2,1,0:T(8,128)S(1)} %get-tuple-element.42), channel_id=1, source_target_pairs={{0,24},{4,28},{8,16},{12,20},{16,8},{20,12},{24,0},{28,4},{1,25},{... | collective-permute-start | bytes 221192 | tf_op jit(solution)/shard_map/ppermute | solution.py:822
  7.3 4.4 %collective-permute-start.2 = (f32[2,72,128]{2,1,0:T(8,128)S(1)}, f32[2,72,128]{2,1,0:T(8,128)S(1)}, u32[]{:S(2)}, u32[]{:S(2)}) collective-permute-start(f32[2,72,128]{2,1,0:T(8,128)S(1)} %get-tuple-element.43), channel_id=1, source_target_pairs={{0,16},{4,20},{8,24},{12,28},{16,0},{20,4},{24,8},{28,12},{1,17},{... | collective-permute-start | bytes 221192 | tf_op jit(solution)/shard_map/ppermute | solution.py:822
  7.8 4.4 %collective-permute-start.3 = (f32[2,72,128]{2,1,0:T(8,128)S(1)}, f32[2,72,128]{2,1,0:T(8,128)S(1)}, u32[]{:S(2)}, u32[]{:S(2)}) collective-permute-start(f32[2,72,128]{2,1,0:T(8,128)S(1)} %get-tuple-element.44), channel_id=1, source_target_pairs={{0,8},{4,12},{8,0},{12,4},{16,24},{20,28},{24,16},{28,20},{1,9},{5... | collective-permute-start | bytes 221192 | tf_op jit(solution)/shard_map/ppermute | solution.py:822
  13.8 12.7 %all-to-all-start = ((f32[32,4,128]{2,1,0:T(4,128)}), f32[32,4,128]{2,1,0:T(4,128)S(1)}, u32[]{:S(2)}, u32[]{:S(2)}) async-start(f32[32,4,128]{2,1,0:T(4,128)} %get-tuple-element.56), calls=%async_computation | async-start | bytes 131072 | tf_op jit(solution)/shard_map/all_to_all | solution.py:810
  18.7 8.6 %collective-permute-start.6 = (f32[3,72,128]{2,1,0:T(8,128)S(1)}, f32[3,72,128]{2,1,0:T(8,128)S(1)}, u32[]{:S(2)}, u32[]{:S(2)}) collective-permute-start(f32[3,72,128]{2,1,0:T(8,128)S(1)} %get-tuple-element.58), channel_id=1, source_target_pairs={{0,4},{4,0},{8,12},{12,8},{16,20},{20,16},{24,28},{28,24},{1,5},{5... | collective-permute-start | bytes 331784 | tf_op jit(solution)/shard_map/ppermute | solution.py:874
  19.0 8.3 %collective-permute-start.7 = (f32[3,72,128]{2,1,0:T(8,128)S(1)}, f32[3,72,128]{2,1,0:T(8,128)S(1)}, u32[]{:S(2)}, u32[]{:S(2)}) collective-permute-start(f32[3,72,128]{2,1,0:T(8,128)S(1)} %get-tuple-element.59), channel_id=1, source_target_pairs={{4,8},{12,16},{20,24},{28,0},{8,4},{16,12},{24,20},{0,28},{5,9},{1... | collective-permute-start | bytes 331784 | tf_op jit(solution)/shard_map/ppermute | solution.py:875
  21.6 6.6 %collective-permute-start.5 = (f32[72,128]{1,0:T(8,128)S(1)}, f32[72,128]{1,0:T(8,128)S(1)}, u32[]{:S(2)}, u32[]{:S(2)}) collective-permute-start(f32[72,128]{1,0:T(8,128)S(1)} %get-tuple-element.54.refs_2_), channel_id=1, source_target_pairs={{1,2},{2,1},{5,6},{6,5},{9,10},{10,9},{13,14},{14,13},{17,18},{18,... | collective-permute-start | bytes 110600 | tf_op jit(solution)/shard_map/ppermute | solution.py:877
  22.2 6.2 %collective-permute-start.4 = (f32[72,128]{1,0:T(8,128)S(1)}, f32[72,128]{1,0:T(8,128)S(1)}, u32[]{:S(2)}, u32[]{:S(2)}) collective-permute-start(f32[72,128]{1,0:T(8,128)S(1)} %get-tuple-element.54.refs_2_), channel_id=1, source_target_pairs={{0,1},{1,0},{2,3},{3,2},{4,5},{5,4},{6,7},{7,6},{8,9},{9,8},{10,11... | collective-permute-start | bytes 110600 | tf_op jit(solution)/shard_map/ppermute | solution.py:876
  30.0 2.7 %collective-permute-start.8 = (f32[4,2,72,128]{3,2,1,0:T(8,128)S(1)}, f32[4,2,72,128]{3,2,1,0:T(8,128)S(1)}, u32[]{:S(2)}, u32[]{:S(2)}) collective-permute-start(f32[4,2,72,128]{3,2,1,0:T(8,128)S(1)} %get-tuple-element.74), channel_id=1, source_target_pairs={{0,4},{4,0},{8,12},{12,8},{16,20},{20,16},{24,28},{28,24},{1,5},{5... | collective-permute-start | bytes 884744 | tf_op jit(solution)/shard_map/ppermute | solution.py:918
  30.1 11.0 %all-to-all-start.1 = ((f32[32,8,128]{2,1,0:T(8,128)}), f32[32,8,128]{2,1,0:T(8,128)S(1)}, u32[]{:S(2)}, u32[]{:S(2)}) async-start(f32[32,8,128]{2,1,0:T(8,128)} %get-tuple-element.68), calls=%async_computation.1 | async-start | bytes 262144 | tf_op jit(solution)/shard_map/all_to_all | solution.py:810
  32.8 10.0 %collective-permute-start.9 = (f32[4,72,128]{2,1,0:T(8,128)S(1)}, f32[4,72,128]{2,1,0:T(8,128)S(1)}, u32[]{:S(2)}, u32[]{:S(2)}) collective-permute-start(f32[4,72,128]{2,1,0:T(8,128)S(1)} %get-tuple-element.75), channel_id=1, source_target_pairs={{0,24},{4,28},{8,16},{12,20},{16,8},{20,12},{24,0},{28,4},{1,25},{... | collective-permute-start | bytes 442376 | tf_op jit(solution)/shard_map/ppermute | solution.py:922
  35.4 8.6 %collective-permute-start.10 = (f32[4,72,128]{2,1,0:T(8,128)S(1)}, f32[4,72,128]{2,1,0:T(8,128)S(1)}, u32[]{:S(2)}, u32[]{:S(2)}) collective-permute-start(f32[4,72,128]{2,1,0:T(8,128)S(1)} %get-tuple-element.76), channel_id=1, source_target_pairs={{0,16},{4,20},{8,24},{12,28},{16,0},{20,4},{24,8},{28,12},{1,17},{... | collective-permute-start | bytes 442376 | tf_op jit(solution)/shard_map/ppermute | solution.py:922
  36.0 8.0 %collective-permute-start.11 = (f32[4,72,128]{2,1,0:T(8,128)S(1)}, f32[4,72,128]{2,1,0:T(8,128)S(1)}, u32[]{:S(2)}, u32[]{:S(2)}) collective-permute-start(f32[4,72,128]{2,1,0:T(8,128)S(1)} %get-tuple-element.77), channel_id=1, source_target_pairs={{0,8},{4,12},{8,0},{12,4},{16,24},{20,28},{24,16},{28,20},{1,9},{5... | collective-permute-start | bytes 442376 | tf_op jit(solution)/shard_map/ppermute | solution.py:922

commit v9 on v7

--- a/solution.py
+++ b/solution.py
@@ -271,8 +271,7 @@
     corner = jnp.where((lane == 0) | (lane == across - 1), smooth[0], turn(smooth[-1], 2))
     rows = jnp.concatenate([corner, jnp.zeros((across - padded, across), F32)], axis=0).T
     scalars = turn(scalars, padded)
-    message_ref[...] = jnp.zeros(message_ref.shape, F32)
-    message_ref[:, 0, :] = jnp.broadcast_to(scalars, (message_ref.shape[0], across))
+    message_ref[...] = jnp.broadcast_to(scalars[None], message_ref.shape)
     corners = (0, 2, across - 1, 1)
     for place, corner in zip(neighbours(tiles, groups)[5:], corners):
         message_ref[pl.ds(place, 1), 0, :] = rows[corner : corner + 1] + scalars
@@ -676,8 +675,7 @@
         ]
     out.append(add_all(left))
     row = scalars_row(out, across)
-    message_ref[...] = jnp.zeros(message_ref.shape, F32)
-    message_ref[:, 0, :] = jnp.broadcast_to(row, (blocks, across))
+    message_ref[...] = jnp.broadcast_to(row[None], message_ref.shape)
     send = pltpu.make_async_copy(message_ref, sent_ref, message_sem.at[0])
     send.start()
     if swap:

time: 45.4 us -> 45.4 us (level)
  no operation moved by 1% of the time
where the time goes in v9:
time: 45.4 us; the launch traced here: 45.1 us
  starting transfers between devices  23.9 us (53%)
  waiting for transfers between devices  10.7 us (24%)
  Pallas kernels  8.74 us (19%)
  local copies, waits for them, and re-layouts  0.97 us (2%)
  between operations  0.78 us (2%)
    pallas_call x11, Pallas kernels, call(): pl.pallas_call(kernel, out_shape=[jax.ShapeDtypeStruct(shape, F32) for sh...  8.74 us
    ppermute x6, starting transfers between devices, per_device(): lax.ppermute(value, 'tile', [(i, i ^ step) for i in range(tiles)])  8.07 us
    all_to_all x2, starting transfers between devices, gather(): lax.all_to_all(value, ('tile', 'grp'), split_axis=0, concat_axis=0, tiled...  7.51 us
    ppermute x6, waiting for transfers between devices, per_device(): lax.ppermute(value, 'tile', [(i, i ^ step) for i in range(tiles)])  4.93 us
    all_to_all x2, waiting for transfers between devices, gather(): lax.all_to_all(value, ('tile', 'grp'), split_axis=0, concat_axis=0, tiled...  4.79 us
    ppermute x1, starting transfers between devices, per_device(): low = lax.ppermute(rim, 'grp', inner_pairs(groups))  4.27 us
    ppermute x1, starting transfers between devices, per_device(): outer = lax.ppermute(outer, 'tile', outer_pairs(tiles, True))  2.53 us
    unnamed x12, local copies, waits for them, and re-layouts  0.97 us
  transfers between devices with their start and end apart: 14, of which 7 were waited for; matrix products, arithmetic and copies ran while one was open for 0% of the time, Pallas kernels for 9%

profile of v9, /device:TPU:0, one launch (start us, length us, event | category | flops | bytes accessed | tf_op | source)
XLA Modules:
  0.0 45.1 jit_solution(14046894899855420432)
XLA Ops:
  0.6 0.0 copy-start
  0.6 0.9 %copy-done = f32[70,8,128]{2,1,0:T(8,128)S(1)} copy-done((f32[70,8,128]{2,1,0:T(8,128)S(1)}, f32[70,8,128]{2,1,0:T(8,128)}, u32[]{:S(2)}) %copy-start) | copy-done | bytes 286744
  1.6 0.0 copy-start.3
  1.6 0.0 copy-start.4
  1.6 0.0 copy-start.5
  1.6 0.0 copy-start.2
  1.6 0.3 shard_map.77
  1.9 0.0 copy-start.1
  1.9 0.5 %collective-permute-start = (f32[4,72,128]{2,1,0:T(8,128)S(1)}, f32[4,72,128]{2,1,0:T(8,128)S(1)}, u32[]{:S(2)}, u32[]{:S(2)}) collective-permute-start(f32[4,72,128]{2,1,0:T(8,128)S(1)} %get-tuple-element.39), channel_id=1, source_target_pairs={{0,4},{4,0},{8,12},{12,8},{16,20},{20,16},{24,28},{28,24},{1,5},{5... | collective-permute-start | bytes 442376 | tf_op jit(solution)/shard_map/ppermute | solution.py:802
  2.4 0.0 copy-done.3
  2.4 0.0 copy-done.4
  2.4 0.0 copy-done.5
  2.4 0.4 shard_map.79
  2.8 0.6 %collective-permute-done.near_ref.refs_1_ = f32[4,72,128]{2,1,0:T(8,128)S(1)} collective-permute-done((f32[4,72,128]{2,1,0:T(8,128)S(1)}, f32[4,72,128]{2,1,0:T(8,128)S(1)}, u32[]{:S(2)}, u32[]{:S(2)}) %collective-permute-start) | collective-permute-done | bytes 147488 | tf_op jit(solution)/shard_map/ppermute | solution.py:802
  3.4 3.9 %collective-permute-start.1 = (f32[2,72,128]{2,1,0:T(8,128)S(1)}, f32[2,72,128]{2,1,0:T(8,128)S(1)}, u32[]{:S(2)}, u32[]{:S(2)}) collective-permute-start(f32[2,72,128]{2,1,0:T(8,128)S(1)} %get-tuple-element.40), channel_id=1, source_target_pairs={{0,24},{4,28},{8,16},{12,20},{16,8},{20,12},{24,0},{28,4},{1,25},{... | collective-permute-start | bytes 221192 | tf_op jit(solution)/shard_map/ppermute | solution.py:805
  7.3 0.5 %collective-permute-start.2 = (f32[2,72,128]{2,1,0:T(8,128)S(1)}, f32[2,72,128]{2,1,0:T(8,128)S(1)}, u32[]{:S(2)}, u32[]{:S(2)}) collective-permute-start(f32[2,72,128]{2,1,0:T(8,128)S(1)} %get-tuple-element.41), channel_id=1, source_target_pairs={{0,16},{4,20},{8,24},{12,28},{16,0},{20,4},{24,8},{28,12},{1,17},{... | collective-permute-start | bytes 221192 | tf_op jit(solution)/shard_map/ppermute | solution.py:805
  7.8 0.1 collective-permute-start.3
  8.0 0.0 copy-done.2
  8.0 0.0 copy-done.1
  8.0 0.5 %shard_map.80 = (f32[8,72,128]{2,1,0:T(8,128)S(1)}, f32[8,72,128]{2,1,0:T(8,128)S(1)}, f32[8,72,128]{2,1,0:T(8,128)S(1)}, f32[152,128]{1,0:T(8,128)S(1)}, f32[24,128]{1,0:T(8,128)S(1)}, /*index=5*/f32[72,128]{1,0:T(8,128)S(1)}) custom-call(f32[560,128]{1,0:T(8,128)S(1)} %bitcast.9, f32[560,128]{1,0:T(8,128)S(1)} %bitcast.10, ...), custom_call_target="tpu_custom_call" | custom-call | tf_op jit(solution)/shard_map/pallas_call | solution.py:32
  8.5 1.4 %collective-permute-done.1.refs_2_ = f32[2,72,128]{2,1,0:T(8,128)S(1)} collective-permute-done((f32[2,72,128]{2,1,0:T(8,128)S(1)}, f32[2,72,128]{2,1,0:T(8,128)S(1)}, u32[]{:S(2)}, u32[]{:S(2)}) %collective-permute-start.1) | collective-permute-done | bytes 73760 | tf_op jit(solution)/shard_map/ppermute | solution.py:805
  10.0 1.7 %collective-permute-done.2.refs_3_ = f32[2,72,128]{2,1,0:T(8,128)S(1)} collective-permute-done((f32[2,72,128]{2,1,0:T(8,128)S(1)}, f32[2,72,128]{2,1,0:T(8,128)S(1)}, u32[]{:S(2)}, u32[]{:S(2)}) %collective-permute-start.2) | collective-permute-done | bytes 73760 | tf_op jit(solution)/shard_map/ppermute | solution.py:805
  11.7 0.5 %collective-permute-done.3.refs_4_ = f32[2,72,128]{2,1,0:T(8,128)S(1)} collective-permute-done((f32[2,72,128]{2,1,0:T(8,128)S(1)}, f32[2,72,128]{2,1,0:T(8,128)S(1)}, u32[]{:S(2)}, u32[]{:S(2)}) %collective-permute-start.3) | collective-permute-done | bytes 73760 | tf_op jit(solution)/shard_map/ppermute | solution.py:805
  12.2 1.6 %shard_map.81 = (f32[32,4,128]{2,1,0:T(4,128)}, f32[8,72,128]{2,1,0:T(8,128)S(1)}, f32[8,72,128]{2,1,0:T(8,128)S(1)}, f32[72,128]{1,0:T(8,128)S(1)}, f32[3,72,12...) custom-call(f32[8,72,128]{2,1,0:T(8,128)S(1)} %get-tuple-element.38.packed_ref.refs_0_, ...), custom_call_target="tpu_custom_call" | custom-call | tf_op jit(solution)/shard_map/pallas_call | solution.py:32
  13.8 4.9 %all-to-all-start = ((f32[32,4,128]{2,1,0:T(4,128)}), f32[32,4,128]{2,1,0:T(4,128)S(1)}, u32[]{:S(2)}, u32[]{:S(2)}) async-start(f32[32,4,128]{2,1,0:T(4,128)} %get-tuple-element.54), calls=%async_computation | async-start | bytes 131072 | tf_op jit(solution)/shard_map/all_to_all | solution.py:793
  18.7 0.3 collective-permute-start.6
  19.0 2.5 %collective-permute-start.7 = (f32[3,72,128]{2,1,0:T(8,128)S(1)}, f32[3,72,128]{2,1,0:T(8,128)S(1)}, u32[]{:S(2)}, u32[]{:S(2)}) collective-permute-start(f32[3,72,128]{2,1,0:T(8,128)S(1)} %get-tuple-element.57), channel_id=1, source_target_pairs={{4,8},{12,16},{20,24},{28,0},{8,4},{16,12},{24,20},{0,28},{5,9},{1... | collective-permute-start | bytes 331784 | tf_op jit(solution)/shard_map/ppermute | solution.py:858
  21.6 0.7 %collective-permute-start.5 = (f32[72,128]{1,0:T(8,128)S(1)}, f32[72,128]{1,0:T(8,128)S(1)}, u32[]{:S(2)}, u32[]{:S(2)}) collective-permute-start(f32[72,128]{1,0:T(8,128)S(1)} %get-tuple-element.52.refs_2_), channel_id=1, source_target_pairs={{1,2},{2,1},{5,6},{6,5},{9,10},{10,9},{13,14},{14,13},{17,18},{18,... | collective-permute-start | bytes 110600 | tf_op jit(solution)/shard_map/ppermute | solution.py:860
  22.2 4.3 %collective-permute-start.4 = (f32[72,128]{1,0:T(8,128)S(1)}, f32[72,128]{1,0:T(8,128)S(1)}, u32[]{:S(2)}, u32[]{:S(2)}) collective-permute-start(f32[72,128]{1,0:T(8,128)S(1)} %get-tuple-element.52.refs_2_), channel_id=1, source_target_pairs={{0,1},{1,0},{2,3},{3,2},{4,5},{5,4},{6,7},{7,6},{8,9},{9,8},{10,11... | collective-permute-start | bytes 110600 | tf_op jit(solution)/shard_map/ppermute | solution.py:859
  26.5 0.0 all-to-all-done.refs_0_
  26.5 0.9 %shard_map.82 = (f32[112,128]{1,0:T(8,128)S(1)}, f32[1,128]{1,0:T(1,128)S(1)}) custom-call(f32[32,4,128]{2,1,0:T(4,128)S(1)} %all-to-all-done.refs_0_), custom_call_target="tpu_custom_call" | custom-call | tf_op jit(solution)/shard_map/pallas_call | solution.py:32
  27.4 0.0 collective-permute-done.6.refs_2_
  27.4 0.0 collective-permute-done.7.refs_3_
  27.4 0.7 %shard_map.83 = (f32[10,72,128]{2,1,0:T(8,128)S(1)}, f32[10,72,128]{2,1,0:T(8,128)S(1)}, f32[16,128]{1,0:T(8,128)S(1)}, f32[4,72,128]{2,1,0:T(8,128)S(1)}) custom-call(f32[32,4,128]{2,1,0:T(4,128)S(1)} %all-to-all-done.refs_0_, f32[1,128]{1,0:T(1,128)S(1)} %get-tuple-element.55.refs_1_.refs_2_, f32[3,72,128]{2,1,0:T(8,128)S(1)} %collective-permute-done.6.refs_2_, ...), custom_call_target="tpu_custom_call" | custom-call | tf_op jit(solution)/shard_map/pallas_call | solution.py:32
  28.1 0.0 collective-permute-done.5.refs_1_
  28.1 0.3 collective-permute-done.4.refs_0_
  28.4 1.7 %shard_map.84 = (f32[32,8,128]{2,1,0:T(8,128)}, f32[8,72,128]{2,1,0:T(8,128)S(1)}, f32[8,72,128]{2,1,0:T(8,128)S(1)}, f32[4,2,72,128]{3,2,1,0:T(8,128)S(1)}) custom-call(f32[72,128]{1,0:T(8,128)S(1)} %collective-permute-done.4.refs_0_, f32[72,128]{1,0:T(8,128)S(1)} %collective-permute-done.5.refs_1_, f32[72,128]{1,0:T(8,128)S(1)} %get-tuple-element.52.refs_2_, ...), custom_call_target="tpu_custom_call" | custom-call | tf_op jit(solution)/shard_map/pallas_call | solution.py:32
  30.1 0.1 collective-permute-start.8
  30.2 2.6 %all-to-all-start.1 = ((f32[32,8,128]{2,1,0:T(8,128)}), f32[32,8,128]{2,1,0:T(8,128)S(1)}, u32[]{:S(2)}, u32[]{:S(2)}) async-start(f32[32,8,128]{2,1,0:T(8,128)} %get-tuple-element.64), calls=%async_computation.1 | async-start | bytes 262144 | tf_op jit(solution)/shard_map/all_to_all | solution.py:793
  32.8 0.0 collective-permute-done.8.near_ref.refs_3_
  32.9 2.7 %collective-permute-start.9 = (f32[4,72,128]{2,1,0:T(8,128)S(1)}, f32[4,72,128]{2,1,0:T(8,128)S(1)}, u32[]{:S(2)}, u32[]{:S(2)}) collective-permute-start(f32[4,72,128]{2,1,0:T(8,128)S(1)} %get-tuple-element.71), channel_id=1, source_target_pairs={{0,24},{4,28},{8,16},{12,20},{16,8},{20,12},{24,0},{28,4},{1,25},{... | collective-permute-start | bytes 442376 | tf_op jit(solution)/shard_map/ppermute | solution.py:902
  35.5 0.6 %collective-permute-start.10 = (f32[4,72,128]{2,1,0:T(8,128)S(1)}, f32[4,72,128]{2,1,0:T(8,128)S(1)}, u32[]{:S(2)}, u32[]{:S(2)}) collective-permute-start(f32[4,72,128]{2,1,0:T(8,128)S(1)} %get-tuple-element.72), channel_id=1, source_target_pairs={{0,16},{4,20},{8,24},{12,28},{16,0},{20,4},{24,8},{28,12},{1,17},{... | collective-permute-start | bytes 442376 | tf_op jit(solution)/shard_map/ppermute | solution.py:902
  36.1 0.3 collective-permute-start.11
  36.4 4.8 %all-to-all-done.1.refs_0_ = f32[32,8,128]{2,1,0:T(8,128)S(1)} async-done(((f32[32,8,128]{2,1,0:T(8,128)}), f32[32,8,128]{2,1,0:T(8,128)S(1)}, u32[]{:S(2)}, u32[]{:S(2)}) %all-to-all-start.1) | async-done | bytes 131104 | tf_op jit(solution)/shard_map/all_to_all | solution.py:793
  41.2 1.6 %shard_map.85 = (f32[560,128]{1,0:T(8,128)}, f32[16,128]{1,0:T(8,128)S(1)}) custom-call(f32[32,8,128]{2,1,0:T(8,128)S(1)} %all-to-all-done.1.refs_0_, f32[112,128]{1,0:T(8,128)S(1)} %get-tuple-element.65.refs_1_, f32[1,128]{1,0:T(1,128)S(1)} %get-tuple-element.55.refs_1_.refs_2_, f32[8,72,128]{2,1,0:T(8,128)S(1)} %get-tuple-element.58.refs_4_.refs_3_, ...), custom_call_target="tpu_custom_call" | custom-call | tf_op jit(solution)/shard_map/pallas_call | solution.py:32
  42.8 0.0 collective-permute-done.9.refs_4_
  42.8 1.3 %collective-permute-done.10.refs_5_ = f32[4,72,128]{2,1,0:T(8,128)S(1)} collective-permute-done((f32[4,72,128]{2,1,0:T(8,128)S(1)}, f32[4,72,128]{2,1,0:T(8,128)S(1)}, u32[]{:S(2)}, u32[]{:S(2)}) %collective-permute-start.10) | collective-permute-done | bytes 147488 | tf_op jit(solution)/shard_map/ppermute | solution.py:902
  44.1 0.0 collective-permute-done.11.refs_6_
  44.1 1.0 %shard_map.87 = f32[560,128]{1,0:T(8,128)} custom-call(f32[16,128]{1,0:T(8,128)S(1)} %get-tuple-element.68.refs_0_, f32[8,72,128]{2,1,0:T(8,128)S(1)} %get-tuple-element.63.refs_10_.smooth_ref.refs_1_, f32[8,72,128]{2,1,0:T(8,128)S(1)} %get-tuple-element.69.second_ref.refs_2_, f32[4,2,72,128]{3,2,1,0:T(8,128)S(1)} %collective-permute-done.8.near_ref.refs_3_, ...), custom_call_target="tpu_custom_call" | custom-call | tf_op jit(solution)/shard_map/pallas_call | solution.py:32
  (3 shorter events, 0.1 us)
Async XLA Ops:
  0.6 1.0 %copy-start = (f32[70,8,128]{2,1,0:T(8,128)S(1)}, f32[70,8,128]{2,1,0:T(8,128)}, u32[]{:S(2)}) copy-start(f32[70,8,128]{2,1,0:T(8,128)} %param.9) | copy-start | bytes 860164
  1.6 0.8 %copy-start.3 = (f32[69]{0:T(128)S(1)}, f32[69]{0:T(128)}, u32[]{:S(2)}) copy-start(f32[69]{0:T(128)} %param.8) | copy-start | bytes 832
  1.6 0.8 %copy-start.4 = (f32[70]{0:T(128)S(1)}, f32[70]{0:T(128)}, u32[]{:S(2)}) copy-start(f32[70]{0:T(128)} %param.10) | copy-start | bytes 844
  1.6 0.8 %copy-start.5 = (f32[70]{0:T(128)S(1)}, f32[70]{0:T(128)}, u32[]{:S(2)}) copy-start(f32[70]{0:T(128)} %param.11) | copy-start | bytes 844
  1.6 6.4 %copy-start.2 = (f32[70,8,128]{2,1,0:T(8,128)S(1)}, f32[70,8,128]{2,1,0:T(8,128)}, u32[]{:S(2)}) copy-start(f32[70,8,128]{2,1,0:T(8,128)} %param.7) | copy-start | bytes 860164
  1.9 6.1 %copy-start.1 = (f32[70,8,128]{2,1,0:T(8,128)S(1)}, f32[70,8,128]{2,1,0:T(8,128)}, u32[]{:S(2)}) copy-start(f32[70,8,128]{2,1,0:T(8,128)} %param.6) | copy-start | bytes 860164
  1.9 1.5 %collective-permute-start = (f32[4,72,128]{2,1,0:T(8,128)S(1)}, f32[4,72,128]{2,1,0:T(8,128)S(1)}, u32[]{:S(2)}, u32[]{:S(2)}) collective-permute-start(f32[4,72,128]{2,1,0:T(8,128)S(1)} %get-tuple-element.39), channel_id=1, source_target_pairs={{0,4},{4,0},{8,12},{12,8},{16,20},{20,16},{24,28},{28,24},{1,5},{5... | collective-permute-start | bytes 442376 | tf_op jit(solution)/shard_map/ppermute | solution.py:802
  3.4 6.5 %collective-permute-start.1 = (f32[2,72,128]{2,1,0:T(8,128)S(1)}, f32[2,72,128]{2,1,0:T(8,128)S(1)}, u32[]{:S(2)}, u32[]{:S(2)}) collective-permute-start(f32[2,72,128]{2,1,0:T(8,128)S(1)} %get-tuple-element.40), channel_id=1, source_target_pairs={{0,24},{4,28},{8,16},{12,20},{16,8},{20,12},{24,0},{28,4},{1,25},{... | collective-permute-start | bytes 221192 | tf_op jit(solution)/shard_map/ppermute | solution.py:805
  7.3 4.4 %collective-permute-start.2 = (f32[2,72,128]{2,1,0:T(8,128)S(1)}, f32[2,72,128]{2,1,0:T(8,128)S(1)}, u32[]{:S(2)}, u32[]{:S(2)}) collective-permute-start(f32[2,72,128]{2,1,0:T(8,128)S(1)} %get-tuple-element.41), channel_id=1, source_target_pairs={{0,16},{4,20},{8,24},{12,28},{16,0},{20,4},{24,8},{28,12},{1,17},{... | collective-permute-start | bytes 221192 | tf_op jit(solution)/shard_map/ppermute | solution.py:805
  7.8 4.4 %collective-permute-start.3 = (f32[2,72,128]{2,1,0:T(8,128)S(1)}, f32[2,72,128]{2,1,0:T(8,128)S(1)}, u32[]{:S(2)}, u32[]{:S(2)}) collective-permute-start(f32[2,72,128]{2,1,0:T(8,128)S(1)} %get-tuple-element.42), channel_id=1, source_target_pairs={{0,8},{4,12},{8,0},{12,4},{16,24},{20,28},{24,16},{28,20},{1,9},{5... | collective-permute-start | bytes 221192 | tf_op jit(solution)/shard_map/ppermute | solution.py:805
  13.8 12.7 %all-to-all-start = ((f32[32,4,128]{2,1,0:T(4,128)}), f32[32,4,128]{2,1,0:T(4,128)S(1)}, u32[]{:S(2)}, u32[]{:S(2)}) async-start(f32[32,4,128]{2,1,0:T(4,128)} %get-tuple-element.54), calls=%async_computation | async-start | bytes 131072 | tf_op jit(solution)/shard_map/all_to_all | solution.py:793
  18.7 8.6 %collective-permute-start.6 = (f32[3,72,128]{2,1,0:T(8,128)S(1)}, f32[3,72,128]{2,1,0:T(8,128)S(1)}, u32[]{:S(2)}, u32[]{:S(2)}) collective-permute-start(f32[3,72,128]{2,1,0:T(8,128)S(1)} %get-tuple-element.56), channel_id=1, source_target_pairs={{0,4},{4,0},{8,12},{12,8},{16,20},{20,16},{24,28},{28,24},{1,5},{5... | collective-permute-start | bytes 331784 | tf_op jit(solution)/shard_map/ppermute | solution.py:857
  19.0 8.3 %collective-permute-start.7 = (f32[3,72,128]{2,1,0:T(8,128)S(1)}, f32[3,72,128]{2,1,0:T(8,128)S(1)}, u32[]{:S(2)}, u32[]{:S(2)}) collective-permute-start(f32[3,72,128]{2,1,0:T(8,128)S(1)} %get-tuple-element.57), channel_id=1, source_target_pairs={{4,8},{12,16},{20,24},{28,0},{8,4},{16,12},{24,20},{0,28},{5,9},{1... | collective-permute-start | bytes 331784 | tf_op jit(solution)/shard_map/ppermute | solution.py:858
  21.6 6.5 %collective-permute-start.5 = (f32[72,128]{1,0:T(8,128)S(1)}, f32[72,128]{1,0:T(8,128)S(1)}, u32[]{:S(2)}, u32[]{:S(2)}) collective-permute-start(f32[72,128]{1,0:T(8,128)S(1)} %get-tuple-element.52.refs_2_), channel_id=1, source_target_pairs={{1,2},{2,1},{5,6},{6,5},{9,10},{10,9},{13,14},{14,13},{17,18},{18,... | collective-permute-start | bytes 110600 | tf_op jit(solution)/shard_map/ppermute | solution.py:860
  22.2 6.2 %collective-permute-start.4 = (f32[72,128]{1,0:T(8,128)S(1)}, f32[72,128]{1,0:T(8,128)S(1)}, u32[]{:S(2)}, u32[]{:S(2)}) collective-permute-start(f32[72,128]{1,0:T(8,128)S(1)} %get-tuple-element.52.refs_2_), channel_id=1, source_target_pairs={{0,1},{1,0},{2,3},{3,2},{4,5},{5,4},{6,7},{7,6},{8,9},{9,8},{10,11... | collective-permute-start | bytes 110600 | tf_op jit(solution)/shard_map/ppermute | solution.py:859
  30.1 2.7 %collective-permute-start.8 = (f32[4,2,72,128]{3,2,1,0:T(8,128)S(1)}, f32[4,2,72,128]{3,2,1,0:T(8,128)S(1)}, u32[]{:S(2)}, u32[]{:S(2)}) collective-permute-start(f32[4,2,72,128]{3,2,1,0:T(8,128)S(1)} %get-tuple-element.70), channel_id=1, source_target_pairs={{0,4},{4,0},{8,12},{12,8},{16,20},{20,16},{24,28},{28,24},{1,5},{5... | collective-permute-start | bytes 884744 | tf_op jit(solution)/shard_map/ppermute | solution.py:898
  30.2 11.0 %all-to-all-start.1 = ((f32[32,8,128]{2,1,0:T(8,128)}), f32[32,8,128]{2,1,0:T(8,128)S(1)}, u32[]{:S(2)}, u32[]{:S(2)}) async-start(f32[32,8,128]{2,1,0:T(8,128)} %get-tuple-element.64), calls=%async_computation.1 | async-start | bytes 262144 | tf_op jit(solution)/shard_map/all_to_all | solution.py:793
  32.9 10.0 %collective-permute-start.9 = (f32[4,72,128]{2,1,0:T(8,128)S(1)}, f32[4,72,128]{2,1,0:T(8,128)S(1)}, u32[]{:S(2)}, u32[]{:S(2)}) collective-permute-start(f32[4,72,128]{2,1,0:T(8,128)S(1)} %get-tuple-element.71), channel_id=1, source_target_pairs={{0,24},{4,28},{8,16},{12,20},{16,8},{20,12},{24,0},{28,4},{1,25},{... | collective-permute-start | bytes 442376 | tf_op jit(solution)/shard_map/ppermute | solution.py:902
  35.5 8.6 %collective-permute-start.10 = (f32[4,72,128]{2,1,0:T(8,128)S(1)}, f32[4,72,128]{2,1,0:T(8,128)S(1)}, u32[]{:S(2)}, u32[]{:S(2)}) collective-permute-start(f32[4,72,128]{2,1,0:T(8,128)S(1)} %get-tuple-element.72), channel_id=1, source_target_pairs={{0,16},{4,20},{8,24},{12,28},{16,0},{20,4},{24,8},{28,12},{1,17},{... | collective-permute-start | bytes 442376 | tf_op jit(solution)/shard_map/ppermute | solution.py:902
  36.1 8.0 %collective-permute-start.11 = (f32[4,72,128]{2,1,0:T(8,128)S(1)}, f32[4,72,128]{2,1,0:T(8,128)S(1)}, u32[]{:S(2)}, u32[]{:S(2)}) collective-permute-start(f32[4,72,128]{2,1,0:T(8,128)S(1)} %get-tuple-element.73), channel_id=1, source_target_pairs={{0,8},{4,12},{8,0},{12,4},{16,24},{20,28},{24,16},{28,20},{1,9},{5... | collective-permute-start | bytes 442376 | tf_op jit(solution)/shard_map/ppermute | solution.py:902
